TPU v7x, 256 devices: a whole 4x4x8 slice. The times are simulated.
256 devices in a mesh: lat: 8 (over y, x_hi), lon: 32 (over x_lo, z, core).
Axes of the slice: x: 4 (x_hi: 2, x_lo: 2; x = x_hi * 2 + x_lo), y: 4, z: 8, core: 2. Of those that a mesh axis runs over, the one named last changes fastest.
Arguments:
- inputs: bfloat16 [4, 48, 384, 384], P(None, 'lat', 'lon'), may hold values from -60 to 60
- cotangent: bfloat16 [4, 48, 384, 384], P(None, 'lat', 'lon'), may hold values from -6 to 6
- land_sea: int32 [48, 384], P('lat', 'lon'), may hold values from 0 to 3
- rel_index: int32 [144, 144], replicated, may hold values from 0 to 758, as said below
- norm_gain: float32 [384], replicated, may hold values from 0.1 to 1.9
- norm_shift: float32 [384], replicated, may hold values from -3 to 3
- w_qkv: bfloat16 [384, 1152], replicated, may hold values from -0.3125 to 0.3125
- b_qkv: float32 [1152], replicated, may hold values from -3 to 3
- w_proj: bfloat16 [384, 384], replicated, may hold values from -0.3125 to 0.3125
- pos_bias: float32 [16, 12, 759], replicated, may hold values from -6 to 330
- surf_bias: float32 [12, 4, 4], replicated, may hold values from -4 to 4
Outputs:
- grad_inputs: bfloat16 [4, 48, 384, 384], P(None, 'lat', 'lon')
- grad_wqkv: float32 [384, 1152], replicated
- grad_bqkv: float32 [1152], replicated
- grad_wproj: float32 [384, 384], replicated
- grad_bproj: float32 [384], replicated
- grad_gain: float32 [384], replicated
- grad_shift: float32 [384], replicated
- grad_pos_bias: float32 [16, 12, 759], replicated
- grad_surf_bias: float32 [12, 4, 4], replicated
Inputs may be any that keep to these rules, and one draw needn't show every extreme that they name: rel_index gives every pair of tokens of a window its relative offset in levels, rows and columns as a slot: pairs with the same offset share a slot and pairs with different offsets have different slots.
All inputs are finite; a program needn't handle non-finite values.
Results may differ from a plain program's by a relative error of at most 0.015.
Values may be sent and summed in bfloat16 or wider, within the bound.
A program may use at most 64 MiB of HBM per device.

v0:
```python
import jax
import jax.numpy as jnp
from jax import lax
from jax.sharding import PartitionSpec as P

WLEV = 2
WLAT = 6
WLON = 12
WT = 144


EPS = 1e-05
NEG_FILL = -1000000000.0


def passed_along(block, axis, distance):
    devices = range(lax.axis_size(axis))
    route = [((i - distance) % len(devices), i) for i in devices]
    return lax.ppermute(block, axis, route)


def as_sent(array):
    return jax.tree.map(lambda a: a.astype(jnp.bfloat16) if a.dtype == jnp.float32 else a, array)


def layer_stats(block_data):
    as_float = block_data.astype(jnp.float32)
    centred = as_float - jnp.mean(as_float, -1, keepdims=True)
    inv_std = lax.rsqrt(jnp.mean(centred * centred, -1, keepdims=True) + EPS)
    return (centred * inv_std, inv_std)


def to_windows(block_data):
    shape_in = block_data.shape
    tile_view = block_data.reshape(
        shape_in[0] // WLEV, WLEV, shape_in[1] // WLAT, WLAT, shape_in[2] // WLON, WLON, shape_in[3]
    )
    tile_view = tile_view.transpose(0, 2, 4, 1, 3, 5, 6)
    return tile_view.reshape(-1, WT, shape_in[3])


def from_windows(windows, levels, lat_rows, lon_cols):
    channels = windows.shape[-1]
    tile_view = windows.reshape(
        levels // WLEV, lat_rows // WLAT, lon_cols // WLON, WLEV, WLAT, WLON, channels
    )
    return tile_view.transpose(0, 3, 1, 4, 2, 5, 6).reshape(levels, lat_rows, lon_cols, channels)


def token_labels(lev_label, lat_label):
    label_rows = lat_label.shape[0]
    joined = (
        lev_label[None, :, None, None] * 2
        + lat_label[:, None, :, None]
        + jnp.zeros((1, 1, 1, WLON), jnp.int32)
    )
    return joined.reshape(label_rows, WT)


def surf_terms(onehot, surf_bias):
    side_terms = jnp.einsum("bqa,hac->bhqc", onehot, surf_bias, precision=lax.Precision.HIGHEST)
    return jnp.einsum("bhqc,bkc->bhqk", side_terms, onehot, precision=lax.Precision.HIGHEST)


def surf_grad(grad_scores, onehot):
    side_terms = jnp.einsum("bhqk,bkc->bhqc", grad_scores, onehot, precision=lax.Precision.HIGHEST)
    return jnp.einsum("bhqc,bqa->hac", side_terms, onehot, precision=lax.Precision.HIGHEST)


def table_grad(grad_sum, rel_index, slot_count):
    group_rows = grad_sum.shape[0]
    head_count = grad_sum.shape[1]
    flat_terms = grad_sum.reshape(group_rows * head_count, WT * WT).T
    summed = jax.ops.segment_sum(flat_terms, rel_index.reshape(-1), num_segments=slot_count)
    return summed.T.reshape(group_rows, head_count, slot_count)


def window_core(normed_win, grad_win, score_bias, allowed, w_qkv, b_qkv, w_proj):
    win_count, token_count, model_width = normed_win.shape
    head_count = score_bias.shape[-3]
    head_size = model_width // head_count
    score_scale = head_size ** (-0.5)
    flat_rows = normed_win.reshape(win_count * token_count, model_width)
    qkv_rows = (jnp.dot(flat_rows, w_qkv, preferred_element_type=jnp.float32) + b_qkv).astype(
        jnp.bfloat16
    )
    qkv_rows = qkv_rows.reshape(win_count, token_count, 3, head_count, head_size)
    queries = qkv_rows[:, :, 0]
    key_vecs = qkv_rows[:, :, 1]
    value_vecs = qkv_rows[:, :, 2]
    scores = (
        jnp.einsum("bqhd,bkhd->bhqk", queries, key_vecs, preferred_element_type=jnp.float32)
        * score_scale
        + score_bias
    )
    scores = jnp.where(allowed, scores, NEG_FILL)
    top_score = jnp.max(scores, -1, keepdims=True)
    exponent = jnp.exp(scores - top_score)
    attn_probs = exponent / jnp.sum(exponent, -1, keepdims=True)
    probs_low = attn_probs.astype(jnp.bfloat16)
    context = jnp.einsum(
        "bhqk,bkhd->bqhd", probs_low, value_vecs, preferred_element_type=jnp.float32
    ).astype(jnp.bfloat16)
    context = context.reshape(win_count * token_count, model_width)
    grad_rows = grad_win.reshape(win_count * token_count, model_width)
    grad_context = jnp.dot(grad_rows, w_proj.T, preferred_element_type=jnp.float32).astype(
        jnp.bfloat16
    )
    grad_context = grad_context.reshape(win_count, token_count, head_count, head_size)
    grad_wproj = jnp.dot(context.T, grad_rows, preferred_element_type=jnp.float32)
    grad_bproj = jnp.sum(grad_rows.astype(jnp.float32), 0)
    grad_probs = jnp.einsum(
        "bqhd,bkhd->bhqk", grad_context, value_vecs, preferred_element_type=jnp.float32
    )
    grad_values = jnp.einsum(
        "bhqk,bqhd->bkhd", probs_low, grad_context, preferred_element_type=jnp.float32
    )
    grad_scores = attn_probs * (grad_probs - jnp.sum(grad_probs * attn_probs, -1, keepdims=True))
    scores_low = grad_scores.astype(jnp.bfloat16)
    grad_queries = (
        jnp.einsum("bhqk,bkhd->bqhd", scores_low, key_vecs, preferred_element_type=jnp.float32)
        * score_scale
    )
    grad_keys = (
        jnp.einsum("bhqk,bqhd->bkhd", scores_low, queries, preferred_element_type=jnp.float32)
        * score_scale
    )
    grad_qkv = jnp.stack([grad_queries, grad_keys, grad_values], 2).reshape(
        win_count * token_count, 3 * model_width
    )
    grad_bqkv = jnp.sum(grad_qkv, 0)
    qkv_low = grad_qkv.astype(jnp.bfloat16)
    grad_wqkv = jnp.dot(flat_rows.T, qkv_low, preferred_element_type=jnp.float32)
    grad_normed = jnp.dot(qkv_low, w_qkv.T, preferred_element_type=jnp.float32).astype(jnp.bfloat16)
    grad_normed = grad_normed.reshape(win_count, token_count, model_width)
    return (grad_normed, grad_scores, grad_wqkv, grad_bqkv, grad_wproj, grad_bproj)


def lon_forward(normed_part, grad_part, surf_part):
    half_cols = WLON // 2
    received = passed_along(
        (normed_part[:, :, :half_cols], grad_part[:, :, :half_cols], surf_part[:, :half_cols]),
        "lon",
        -1,
    )
    return (
        jnp.concatenate([normed_part[:, :, half_cols:], received[0]], 2),
        jnp.concatenate([grad_part[:, :, half_cols:], received[1]], 2),
        jnp.concatenate([surf_part[:, half_cols:], received[2]], 1),
    )


def lat_forward(normed_part, grad_part, surf_part):
    half_rows = WLAT // 2
    received = passed_along(
        (normed_part[:, :half_rows], grad_part[:, :half_rows], as_sent(surf_part[:half_rows])),
        "lat",
        -1,
    )
    return (
        jnp.concatenate([normed_part[:, half_rows:], received[0]], 1),
        jnp.concatenate([grad_part[:, half_rows:], received[1]], 1),
        jnp.concatenate([surf_part[half_rows:], received[2]], 0),
    )


def lat_reverse(grad_part):
    lat_rows = grad_part.shape[1]
    half_rows = WLAT // 2
    received = passed_along(grad_part[:, lat_rows - half_rows :], "lat", 1)
    return jnp.concatenate([received, grad_part[:, : lat_rows - half_rows]], 1)


def lon_reverse(grad_part):
    lon_cols = grad_part.shape[2]
    half_cols = WLON // 2
    received = passed_along(grad_part[:, :, lon_cols - half_cols :], "lon", 1)
    return jnp.concatenate([received, grad_part[:, :, : lon_cols - half_cols]], 2)


def on_device(
    inputs,
    cotangent,
    land_sea,
    rel_index,
    norm_gain,
    norm_shift,
    w_qkv,
    b_qkv,
    w_proj,
    pos_bias,
    surf_bias,
):
    levels, lat_rows, lon_cols, model_width = inputs.shape
    lat_count = lax.axis_size("lat")
    lon_count = lax.axis_size("lon")
    lat_index = lax.axis_index("lat")
    head_count = surf_bias.shape[0]
    surf_kinds = surf_bias.shape[1]
    slot_count = pos_bias.shape[-1]
    lat_windows = lat_rows // WLAT
    lon_windows = lon_cols // WLON
    lev_windows = levels // WLEV
    all_lat_windows = lat_windows * lat_count
    batch_windows = lat_windows * lon_windows
    whitened, inv_std = layer_stats(inputs)
    normed = (whitened * norm_gain + norm_shift).astype(jnp.bfloat16)
    normed_rolled = jnp.roll(normed, -(WLEV // 2), 0)
    grad_rolled = jnp.roll(cotangent, -(WLEV // 2), 0)
    block_normed, block_grad, block_surf = lat_forward(
        *lon_forward(normed_rolled, grad_rolled, land_sea)
    )
    surf_windows = to_windows(
        jnp.broadcast_to(block_surf[None, :, :, None], (WLEV, lat_rows, lon_cols, 1))
    )[..., 0]
    onehot = (surf_windows[..., None] == jnp.arange(surf_kinds, dtype=jnp.int32)).astype(
        jnp.float32
    )
    surf_part = surf_terms(onehot, surf_bias).reshape(lat_windows, lon_windows, head_count, WT, WT)
    lat_orig = (lat_index * lat_rows + jnp.arange(lat_rows, dtype=jnp.int32) + WLAT // 2) % (
        lat_rows * lat_count
    )
    lat_label = (lat_orig < WLAT // 2).astype(jnp.int32).reshape(lat_windows, WLAT)
    table_view = pos_bias.reshape(all_lat_windows, lev_windows, head_count, slot_count)
    sum_wqkv = jnp.zeros((model_width, 3 * model_width), jnp.float32)
    sum_bqkv = jnp.zeros((3 * model_width,), jnp.float32)
    sum_wproj = jnp.zeros((model_width, model_width), jnp.float32)
    sum_bproj = jnp.zeros((model_width,), jnp.float32)
    sum_surf = jnp.zeros((head_count, surf_kinds, surf_kinds), jnp.float32)
    grad_pieces = []
    table_pieces = []
    for lev_index in range(lev_windows):
        lev_label = (lev_index * WLEV + jnp.arange(WLEV, dtype=jnp.int32) == levels - 1).astype(
            jnp.int32
        )
        labels = token_labels(lev_label, lat_label)
        allowed = (labels[:, :, None] == labels[:, None, :])[:, None, None]
        allowed = allowed.reshape(batch_windows, 1, WT, WT)
        pos_rows = lax.dynamic_slice_in_dim(
            table_view[:, lev_index], lat_index * lat_windows, lat_windows, 0
        )
        pos_terms = jnp.take(pos_rows, rel_index, axis=2)
        score_bias = (pos_terms[:, None] + surf_part).reshape(batch_windows, head_count, WT, WT)
        lev_lo = lev_index * WLEV
        normed_win = to_windows(block_normed[lev_lo : lev_lo + WLEV])
        grad_win = to_windows(block_grad[lev_lo : lev_lo + WLEV])
        grad_norm_w, grad_scores, g_wqkv, g_bqkv, g_wproj, g_bproj = window_core(
            normed_win, grad_win, score_bias, allowed, w_qkv, b_qkv, w_proj
        )
        sum_wqkv = sum_wqkv + g_wqkv
        sum_bqkv = sum_bqkv + g_bqkv
        sum_wproj = sum_wproj + g_wproj
        sum_bproj = sum_bproj + g_bproj
        sum_surf = sum_surf + surf_grad(grad_scores, onehot)
        grad_sum = jnp.sum(grad_scores.reshape(lat_windows, lon_windows, head_count, WT, WT), 1)
        table_pieces.append(table_grad(grad_sum, rel_index, slot_count))
        grad_pieces.append(from_windows(grad_norm_w, WLEV, lat_rows, lon_cols))
    grad_block = jnp.concatenate(grad_pieces, 0)
    grad_orig = lon_reverse(lat_reverse(grad_block))
    grad_normed = jnp.roll(grad_orig, WLEV // 2, 0).astype(jnp.float32)
    gain_scaled = grad_normed * norm_gain
    first_mean = jnp.mean(gain_scaled, -1, keepdims=True)
    second_mean = jnp.mean(gain_scaled * whitened, -1, keepdims=True)
    grad_inputs = (
        cotangent.astype(jnp.float32)
        + inv_std * (gain_scaled - first_mean - whitened * second_mean)
    ).astype(jnp.bfloat16)
    sum_gain = jnp.sum(grad_normed * whitened, (0, 1, 2))
    sum_shift = jnp.sum(grad_normed, (0, 1, 2))
    local_table = jnp.stack(table_pieces, 1)
    full_table = lax.dynamic_update_slice(
        jnp.zeros((all_lat_windows, lev_windows, head_count, slot_count), jnp.float32),
        local_table,
        (lat_index * lat_windows, 0, 0, 0),
    )
    summed = lax.psum(
        (sum_wqkv, sum_bqkv, sum_wproj, sum_bproj, sum_gain, sum_shift, sum_surf, full_table),
        ("lat", "lon"),
    )
    table_total = summed[7]
    grad_scale = float(levels * lat_rows * lon_cols * lat_count * lon_count) ** (-0.5)
    table_total = table_total.reshape(all_lat_windows * lev_windows, head_count, slot_count)
    return (
        grad_inputs,
        summed[0] * grad_scale,
        summed[1] * grad_scale,
        summed[2] * grad_scale,
        summed[3] * grad_scale,
        summed[4] * grad_scale,
        summed[5] * grad_scale,
        table_total * grad_scale,
        summed[6] * grad_scale,
    )


def solution(mesh):
    in_specs = (
        P(None, "lat", "lon", None),
        P(None, "lat", "lon", None),
        P("lat", "lon"),
        P(),
        P(),
        P(),
        P(),
        P(),
        P(),
        P(),
        P(),
    )
    out_specs = (P(None, "lat", "lon", None), P(), P(), P(), P(), P(), P(), P(), P())
    return jax.shard_map(
        on_device, mesh=mesh, in_specs=in_specs, out_specs=out_specs, check_vma=False
    )
```

profile of v0, /device:TPU:1, one launch (start us, length us, event | category | flops | bytes accessed | tf_op | source)
XLA Modules:
  0.0 756.4 jit_solution(3536061815891273842)
XLA Ops:
  8.1 3.2 collective-permute-start.2
  14.3 4.5 collective-permute-start.4
  26.9 4.0 copy.252
  30.9 5.9 fusion.78
  38.0 38.7 %gather_fusion.1 = f32[20736,12]{1,0:T(8,128)} fusion(f32[12,759]{0,1:T(8,128)S(1)} %get-tuple-element.111, s32[21504]{0:T(1024)S(1)} %pad_clamp_fusion), kind=kCustom, calls=%fused_computation.1.clone | custom fusion | bytes 2073600 | tf_op jit(solution)/shard_map/jit(_take)/gather | solution.py:242
  76.6 12.1 %copy.217 = f32[144,144,12]{0,1,2:T(8,128)} copy(f32[144,144,12]{2,1,0:T(8,128)} %bitcast.193) | data formatting | bytes 1990656 | tf_op jit(solution)/shard_map/jit(_take)/gather | solution.py:242
  88.8 38.7 %gather_fusion = f32[20736,12]{1,0:T(8,128)} fusion(f32[12,759]{0,1:T(8,128)S(1)} %get-tuple-element.112, s32[21504]{0:T(1024)S(1)} %pad_clamp_fusion), kind=kCustom, calls=%fused_computation.clone | custom fusion | bytes 2073600 | tf_op jit(solution)/shard_map/jit(_take)/gather | solution.py:242
  127.5 4.9 collective-permute-start.3
  132.4 12.1 %copy.205 = f32[144,144,12]{0,1,2:T(8,128)} copy(f32[144,144,12]{2,1,0:T(8,128)} %bitcast.192) | data formatting | bytes 1990656 | tf_op jit(solution)/shard_map/jit(_take)/gather | solution.py:242
  149.5 2.6 collective-permute-start.1
  160.4 2.3 fusion.7
  164.5 3.9 convolution_convert_fusion
  168.3 3.4 convolution_bitcast_fusion
  186.3 2.0 copy.201
  188.4 2.8 fusion.11
  192.9 3.3 convolution_convert_fusion.1
  196.2 3.3 convolution_bitcast_fusion.1
  199.6 2.3 multiply_reduce_fusion.1
  217.4 3.5 collective-permute-start.6
  220.9 2.2 convolution_add_fusion.3
  226.0 2.1 copy.225
  228.0 3.7 reshape.683
  231.7 6.8 copy.229
  238.5 113.1 %scatter_custom_fusion.1 = f32[759,12]{1,0:T(8,128)} fusion(s32[20736]{0:T(1024)} %reshape.706, f32[20736,12]{1,0:T(8,128)} %copy.229, f32[]{:T(128)} %constant.23.clone.1), kind=kCustom, calls=%fused_computation.117 | custom fusion | flops 248832 | bytes 36944 | tf_op jit(solution)/shard_map/scatter-add | solution.py:74
  352.9 2.2 reshape.682
  358.1 5.7 copy.226
  363.8 112.5 %scatter_custom_fusion = f32[759,12]{1,0:T(8,128)S(1)} fusion(s32[20736]{0:T(1024)} %reshape.706, f32[20736,12]{1,0:T(8,128)} %copy.226, f32[]{:T(128)} %constant.23.clone.1), kind=kCustom, calls=%fused_computation.119 | custom fusion | flops 248832 | bytes 36944 | tf_op jit(solution)/shard_map/scatter-add | solution.py:74
  477.6 2.8 collective-permute-start.7
  480.5 2.7 dynamic_update_slice.3
  485.6 76.4 %all-reduce = (f32[1152]{0:T(1024)S(1)}, f32[384]{0:T(512)S(1)}, f32[384]{0:T(512)S(1)}, f32[384]{0:T(512)S(1)}, f32[12,4,4]{0,1,2:T(4,128)S(1)}) all-reduce(f32[1152]{0:T(1024)S(1)} %add.209, f32[384]{0:T(512)S(1)} %add.211, f32[384]{0:T(512)S(1)} %get-tuple-element.64, ...), channel_id=1, replica_groups=mesh['lat'=8,'lon'=32] {'lat','lon'}, use_global_device_ids=true, to_apply=%region_13.15 | all-reduce | flops 2496 | bytes 19968 | tf_op jit(solution)/shard_map/psum | solution.py:276
  566.0 177.6 %all-reduce.4.cloned.1.call-done = (f32[384,1152]{1,0:T(8,128)}, f32[384,384]{1,0:T(8,128)}, f32[8,2,12,759]{3,0,2,1:T(8,128)}) async-done(((f32[384,1152]{1,0:T(8,128)}, f32[384,384]{1,0:T(8,128)}, f32[8,2,12,759]{3,0,2,1:T(8,128)}), (f32[384,1152]{1,0:T(8,128)}, f32[384,384]{1,0:T(8,128)}, f32[8,2,12,759]{3,0,2,1:T(8,128)})) %all-reduce.4.cloned.1.call-update) | async-done | bytes 2942224 | tf_op jit(solution)/shard_map/psum | solution.py:276
  743.6 2.9 broadcast_multiply_fusion
  (195 shorter events, 77.0 us)
Async XLA Ops:
  7.2 150.9 %copy-start = (bf16[384,1152]{1,0:T(8,128)(2,1)S(1)}, bf16[384,1152]{1,0:T(8,128)(2,1)}, u32[]{:S(2)}) copy-start(bf16[384,1152]{1,0:T(8,128)(2,1)} %param.19) | copy-start | bytes 2654212
  7.2 14.5 %copy-start.8 = (bf16[4,6,12,384]{3,0,2,1:T(4,128)(2,1)S(1)}, bf16[4,6,12,384]{3,0,2,1:T(4,128)(2,1)}, u32[]{:S(2)}) copy-start(bf16[4,6,12,384]{3,0,2,1:T(4,128)(2,1)} %param.13) | copy-start | bytes 663556
  7.2 14.5 %copy-start.33 = (f32[384]{0:T(512)S(1)}, f32[384]{0:T(512)}, u32[]{:S(2)}) copy-start(f32[384]{0:T(512)} %param.17) | copy-start | bytes 4612
  7.2 14.5 %copy-start.38 = (f32[384]{0:T(512)S(1)}, f32[384]{0:T(512)}, u32[]{:S(2)}) copy-start(f32[384]{0:T(512)} %param.18) | copy-start | bytes 4612
  7.2 16.1 %copy-start.17 = (s32[144,144]{1,0:T(8,128)S(1)}, s32[144,144]{1,0:T(8,128)}, u32[]{:S(2)}) copy-start(s32[144,144]{1,0:T(8,128)} %param.16) | copy-start | bytes 248836
  7.2 736.4 %all-reduce.4.cloned.1.call-start = ((), (), s32[]{:S(2)}) async-start(), calls=%async_computation | async-start | bytes 5898240 | tf_op jit(solution)/shard_map/psum | solution.py:276
  8.1 119.3 %collective-permute-start.2 = (s32[6,6]{1,0:T(8,128)S(1)}, s32[6,6]{1,0:T(8,128)S(1)}, u32[]{:S(2)}, u32[]{:S(2)}) collective-permute-start(s32[6,6]{1,0:T(8,128)S(1)} %get-tuple-element.100), channel_id=1, source_target_pairs={{1,0},{2,1},{3,2},{4,3},{5,4},{6,5},{7,6},{8,7},{9,8},{10,9},{11,1... | collective-permute-start | bytes 440 | tf_op jit(solution)/shard_map/ppermute | solution.py:19
  14.3 12.5 %copy-start.25 = (f32[16,12,759]{2,0,1:T(8,128)S(1)}, f32[16,12,759]{2,0,1:T(8,128)}, u32[]{:S(2)}) copy-start(f32[16,12,759]{2,0,1:T(8,128)} %param.22) | copy-start | bytes 1748740
  14.3 131.4 %collective-permute-start.4 = (bf16[4,6,6,384]{3,0,2,1:T(4,128)(2,1)}, bf16[4,6,6,384]{3,0,2,1:T(4,128)(2,1)}, u32[]{:S(2)}, u32[]{:S(2)}) collective-permute-start(bf16[4,6,6,384]{3,0,2,1:T(4,128)(2,1)} %get-tuple-element.84), channel_id=1, source_target_pairs={{1,0},{2,1},{3,2},{4,3},{5,4},{6,5},{7,6},{8,7},{9,8},{10,9},{11,1... | collective-permute-start | bytes 331784 | tf_op jit(solution)/shard_map/ppermute | solution.py:19
  22.7 125.1 %collective-permute-start = (bf16[4,6,6,384]{3,2,1,0:T(8,128)(2,1)}, bf16[4,6,6,384]{3,2,1,0:T(8,128)(2,1)}, u32[]{:S(2)}, u32[]{:S(2)}) collective-permute-start(bf16[4,6,6,384]{3,2,1,0:T(8,128)(2,1)} %get-tuple-element.91), channel_id=1, source_target_pairs={{1,0},{2,1},{3,2},{4,3},{5,4},{6,5},{7,6},{8,7},{9,8},{10,9},{11,1... | collective-permute-start | bytes 331784 | tf_op jit(solution)/shard_map/ppermute | solution.py:19
  127.5 17.0 %collective-permute-start.3 = (s32[3,12]{1,0:T(4,128)S(1)}, s32[3,12]{1,0:T(4,128)S(1)}, u32[]{:S(2)}, u32[]{:S(2)}) collective-permute-start(s32[3,12]{1,0:T(4,128)S(1)} %get-tuple-element.98), channel_id=1, source_target_pairs={{32,0},{64,32},{96,64},{128,96},{160,128},{192,160},{224,192},{0,2... | collective-permute-start | bytes 440 | tf_op jit(solution)/shard_map/ppermute | solution.py:19
  132.4 12.2 %copy-start.37 = (f32[12,4,4]{0,2,1:T(4,128)S(1)}, f32[12,4,4]{0,2,1:T(4,128)}, u32[]{:S(2)}) copy-start(f32[12,4,4]{0,2,1:T(4,128)} %param.23) | copy-start | bytes 2308
  144.9 9.1 %copy-start.18 = (bf16[384,384]{1,0:T(8,128)(2,1)S(1)}, bf16[384,384]{1,0:T(8,128)(2,1)}, u32[]{:S(2)}) copy-start(bf16[384,384]{1,0:T(8,128)(2,1)} %param.21) | copy-start | bytes 884740
  145.8 14.6 %copy-start.2 = (f32[12,144,144]{1,2,0:T(8,128)}, f32[12,144,144]{1,2,0:T(8,128)S(1)}, u32[]{:S(2)}) copy-start(f32[12,144,144]{1,2,0:T(8,128)S(1)} %fusion.62) | copy-start | bytes 2985988
  145.8 12.3 %copy-start.31 = (f32[1152]{0:T(1024)S(1)}, f32[1152]{0:T(1024)}, u32[]{:S(2)}) copy-start(f32[1152]{0:T(1024)} %param.20) | copy-start | bytes 13828
  147.0 5.4 collective-permute-start.5
  149.5 6.2 collective-permute-start.1
  153.9 3.5 copy-start.19
  154.2 6.2 copy-start.27
  160.4 11.3 %copy-start.12 = (bf16[144,1152]{0,1:T(8,128)(2,1)}, bf16[144,1152]{0,1:T(8,128)(2,1)S(1)}, u32[]{:S(2)}) copy-start(bf16[144,1152]{0,1:T(8,128)(2,1)S(1)} %copy.213) | copy-start | bytes 995332
  164.4 7.2 copy-start.6
  209.4 3.6 copy-start.3
  213.1 7.9 %copy-start.20 = (bf16[144,384]{1,0:T(8,128)(2,1)S(1)}, bf16[144,384]{1,0:T(8,128)(2,1)}, u32[]{:S(2)}) copy-start(bf16[144,384]{1,0:T(8,128)(2,1)} %copy-done.19) | copy-start | bytes 331780
  215.7 7.5 copy-start.28
  217.4 259.2 %collective-permute-start.6 = (bf16[4,3,12,384]{3,2,1,0:T(8,128)(2,1)}, bf16[4,3,12,384]{3,2,1,0:T(8,128)(2,1)}, u32[]{:S(2)}, u32[]{:S(2)}) collective-permute-start(bf16[4,3,12,384]{3,2,1,0:T(8,128)(2,1)} %get-tuple-element.85), channel_id=1, source_target_pairs={{224,0},{0,32},{32,64},{64,96},{96,128},{128,160},{160,192},{192,2... | collective-permute-start | bytes 331784 | tf_op jit(solution)/shard_map/ppermute | solution.py:19
  358.1 118.4 %copy-start.35 = (f32[384]{0:T(512)S(1)}, f32[384]{0:T(512)}, u32[]{:S(2)}) copy-start(f32[384]{0:T(512)} %get-tuple-element.76) | copy-start | bytes 4612
  358.1 118.4 %copy-start.36 = (f32[384]{0:T(512)S(1)}, f32[384]{0:T(512)}, u32[]{:S(2)}) copy-start(f32[384]{0:T(512)} %get-tuple-element.93) | copy-start | bytes 4612
  477.6 6.5 collective-permute-start.7
  480.4 3.7 copy-start.30
  480.4 3.7 copy-start.34
  483.2 79.4 %copy-start.16 = (bf16[4,6,12,384]{3,0,2,1:T(4,128)(2,1)S(1)}, bf16[4,6,12,384]{3,0,2,1:T(4,128)(2,1)}, u32[]{:S(2)}) copy-start(bf16[4,6,12,384]{3,0,2,1:T(4,128)(2,1)} %param.14) | copy-start | bytes 663556
  743.6 3.8 copy-start.23
  (16 other events, 29.7 us)
Sparse Core Ops, SparseCore 0:
  484.2 259.3 all-reduce.3
where the time goes:
time: 767 us; the launch traced here: 756 us
  other arithmetic  256 us (33%)
  waiting for transfers between devices  178 us (23%)
  local copies, waits for them, and re-layouts  162 us (21%)
  blocking collectives  76.4 us (10%)
  matrix products  44.7 us (6%)
  starting transfers between devices  23.1 us (3%)
  between operations  15.2 us (2%)
    scatter-add x2, other arithmetic, table_grad(): jax.ops.segment_sum(flat_terms, rel_index.reshape(-1), num_segments=slot_...  226 us
    psum x1, waiting for transfers between devices, on_device(): lax.psum((sum_wqkv, sum_bqkv, sum_wproj, sum_bproj, sum_gain, sum_shift,...  178 us
    gather x4, local copies, waits for them, and re-layouts, on_device(): pos_terms = jnp.take(pos_rows, rel_index, axis=2)  102 us
    psum x1, blocking collectives, on_device(): lax.psum((sum_wqkv, sum_bqkv, sum_wproj, sum_bproj, sum_gain, sum_shift,...  76.4 us
    ppermute x8, starting transfers between devices, passed_along(): return lax.ppermute(block, axis, route)  23 us
  transfers between devices with their start and end apart: 9, of which 3 were waited for; matrix products, arithmetic and copies ran while one was open for 52% of the time, Pallas kernels for 0%

commit v1 on v0

v1 whole, which is shorter than its diff:
```python
import functools

import jax
import jax.numpy as jnp
import ml_dtypes
import numpy as np
from jax import lax
from jax.experimental import pallas as pl
from jax.experimental.pallas import tpu as pltpu
from jax.sharding import PartitionSpec as P

F32 = jnp.float32
BF16 = jnp.bfloat16
MESH = pl.DeviceIdType.MESH
EPS = 1e-05
LOG2E = 1.4426950408889634
BIG = 2.0**33
HEADS = 12
SLOTS = 759
WIDTH = 384
WT = 144
PITCH = 23
KEYS = 256
SCALE = 32.0**-0.5
NT = (((1,), (1,)), ((), ()))
TN = (((0,), (0,)), ((), ()))
NN = (((1,), (0,)), ((), ()))
PX, PY, PZ = 4, 4, 8
PLANE = PX * PY
VMEM = pl.BlockSpec(memory_space=pltpu.VMEM)


def dot(a, b, dims=NN):
    return lax.dot_general(a, b, dims, preferred_element_type=F32)


def quad_order():
    return [(li, q, r, c) for li in range(2) for q in range(4) for r in range(3) for c in range(6)]


def constants():
    order = quad_order()
    gather = np.zeros((576, 576), np.float32)
    back = np.zeros((320, 288), np.float32)
    for part in range(2):
        for w in range(2):
            for k, (li, q, r, c) in enumerate(order):
                row = part * 288 + w * 144 + k
                in_quad = (2 * w + li) * 18 + r * 6 + c
                gather[row, q * 144 + part * 72 + in_quad] = 1
                if part == 0:
                    back[q * 80 + in_quad, row] = 1
    spread = np.zeros((KEYS, WT), np.float32)
    cells = np.zeros((WT, 128), np.float32)
    for k, (li, q, r, c) in enumerate(order):
        spread[li * 128 + PITCH * (3 * (q // 2) + r) + 6 * (q % 2) + c, k] = 1
        cells[k, q * 32 + r * 6 + c] = 1
    spread_plain = np.zeros((KEYS, WT), np.float32)
    for k in range(WT):
        li, ri, ci = k // 72, k // 12 % 6, k % 12
        spread_plain[li * 128 + PITCH * ri + ci, k] = 1
    rows = np.array([[PITCH * (3 * (q // 2) + r) + 6 * (q % 2) + c] for li, q, r, c in order[:72]], np.int32)
    place = np.zeros((384, 320), np.float32)
    for l in range(4):
        for r in range(6):
            for c in range(12):
                q = (r // 3) * 2 + c // 6
                place[(l * 6 + r) * 16 + c, q * 80 + ((l - 1) % 4) * 18 + (r % 3) * 6 + c % 6] = 1
    low = lambda a: a.astype(ml_dtypes.bfloat16)
    return (low(gather), low(back), low(spread), low(spread_plain), low(cells), rows), low(place)


def halo_kernel(buf, cls, out, out_cls, send, recv, local):
    lat, lon = lax.axis_index("lat"), lax.axis_index("lon")
    n_lat, n_lon = lax.axis_size("lat"), lax.axis_size("lon")
    up, down = lax.rem(lat + 1, n_lat), lax.rem(lat + n_lat - 1, n_lat)
    east, west = lax.rem(lon + 1, n_lon), lax.rem(lon + n_lon - 1, n_lon)
    barrier = pltpu.get_barrier_semaphore()
    for device in ((lat, east), (up, lon), (up, east)):
        pl.semaphore_signal(barrier, inc=1, device_id=device, device_id_type=MESH)
    pl.semaphore_wait(barrier, 3)
    copies = []
    for k, (src, dst, device) in enumerate(((2, 1, (lat, west)), (1, 2, (down, lon)), (0, 3, (down, west)))):
        for m, (a, b) in enumerate(((buf, out), (cls, out_cls))):
            copies.append(
                pltpu.make_async_remote_copy(
                    src_ref=a.at[src],
                    dst_ref=b.at[dst],
                    send_sem=send.at[2 * k + m],
                    recv_sem=recv.at[2 * k + m],
                    device_id=device,
                    device_id_type=MESH,
                )
            )
    for copy in copies:
        copy.start()
    own = [
        pltpu.make_async_copy(buf.at[3], out.at[0], local.at[0]),
        pltpu.make_async_copy(cls.at[3], out_cls.at[0], local.at[1]),
    ]
    for copy in own:
        copy.start()
    for copy in own + copies:
        copy.wait()


def halo_forward(buf, cls):
    return pl.pallas_call(
        halo_kernel,
        out_shape=(jax.ShapeDtypeStruct(buf.shape, buf.dtype), jax.ShapeDtypeStruct(cls.shape, cls.dtype)),
        in_specs=[VMEM] * 2,
        out_specs=(VMEM, VMEM),
        scratch_shapes=[
            pltpu.SemaphoreType.DMA((6,)),
            pltpu.SemaphoreType.DMA((6,)),
            pltpu.SemaphoreType.DMA((2,)),
        ],
        compiler_params=pltpu.CompilerParams(collective_id=0, has_side_effects=True),
        name="halo",
    )(buf, cls)


def skew_parts(rows):
    lane = lax.broadcasted_iota(jnp.int32, (72, 128), 1)
    first = lane + rows >= PITCH * 5 + 11
    there = jnp.bitwise_and(lane - rows - 2, 127)
    back = jnp.bitwise_and(lane + rows + 2, 127)
    return first, there, back


def skew(table, first, there):
    mixed = jnp.where(first, table[:, :128], table[:, 128:])
    return jnp.take_along_axis(mixed, there, axis=1)


def split(values, count):
    pieces = []
    for _ in range(count):
        piece = values.astype(BF16)
        pieces.append(piece)
        values = values - piece.astype(F32)
    return pieces


def window_kernel(
    tok_in, cls_in, rel, gain, shift, w_qkv, b_qkv, w_proj, pos, surf,
    c_gather, c_back, c_spread, c_plain, c_cells, c_rows,
    out_w, out_t, out_gx,
    white, inv_std, normed, dy_low, qkv, dctx, turned, kv_pad, q_feat, k_feat,
    onehot, tables, d_tables, ctx_acc, dq_acc, f_acc, dkv_t, low, table_in,
):
    lat = lax.axis_index("lat")
    last_band = lat == lax.axis_size("lat") - 1

    tokens = dot(c_gather[...], tok_in[...])
    x = tokens[:288]
    dy = tokens[288:]
    dy_low[...] = dy.astype(BF16)
    centred = x - jnp.mean(x, -1, keepdims=True)
    inv = lax.rsqrt(jnp.mean(centred * centred, -1, keepdims=True) + EPS)
    inv_std[...] = inv
    whitened = centred * inv
    white[...] = whitened
    normed[...] = (whitened * gain[...] + shift[...]).astype(BF16)
    qkv[...] = (dot(normed[...], w_qkv[...]) + b_qkv[...]).astype(BF16)
    dctx[...] = dot(dy_low[...], w_proj[...], NT).astype(BF16)
    eye = (
        lax.broadcasted_iota(jnp.int32, (WIDTH, WIDTH), 0) == lax.broadcasted_iota(jnp.int32, (WIDTH, WIDTH), 1)
    ).astype(F32).astype(BF16)
    for w in range(2):
        rows = slice(w * WT, (w + 1) * WT)
        turned[w, 0] = dot(eye, qkv[rows, :WIDTH], NT).astype(BF16)
        turned[w, 1] = dot(eye, dctx[rows, :], NT).astype(BF16)
        kv_pad[w] = dot(c_spread[...], qkv[rows, WIDTH:]).astype(BF16)

    lane = lax.broadcasted_iota(jnp.int32, (WT, 128), 1)
    token = lax.broadcasted_iota(jnp.int32, (WT, 128), 0)
    kind = dot(c_cells[...], cls_in[...]).astype(jnp.int32)
    turned_over = jnp.logical_and(lax.rem(token, 72) >= 36, last_band).astype(F32)
    of_key = jnp.where(kind == jnp.bitwise_and(lane, 3), 1.0, 0.0)
    of_query = jnp.where(lane < 4, of_key, 0.0).astype(BF16)
    surf_over = surf[...] * (1.0 / SCALE)
    surf_lane = lax.broadcasted_iota(jnp.int32, (128, 128), 1)
    surf_hi, surf_lo = split(surf_over, 2)
    side = dot(of_query, jnp.where(surf_lane < 48, surf_hi.astype(F32), surf_lo.astype(F32)).astype(BF16))
    q_feat[...] = jnp.where(
        lane < 96, side, jnp.where(lane == 96, turned_over, jnp.where(lane == 97, 1.0 - turned_over, 0.0))
    ).astype(BF16)
    key_side = jnp.where(
        lane < 96,
        of_key,
        jnp.where(lane == 96, -BIG * (1.0 - turned_over), jnp.where(lane == 97, -BIG * turned_over, 0.0)),
    ).astype(BF16)
    key_lane = lax.broadcasted_iota(jnp.int32, (KEYS, 128), 1)
    key_row = jnp.bitwise_and(lax.broadcasted_iota(jnp.int32, (KEYS, 128), 0), 127)
    hidden = jnp.logical_and(lax.rem(key_row, PITCH) >= 12, jnp.logical_and(key_lane >= 96, key_lane < 98))
    k_feat[...] = jnp.where(hidden, -BIG, dot(c_spread[...], key_side)).astype(BF16)

    rel_now = rel[...]
    rel_low = jnp.bitwise_and(rel_now, 15)
    rel_wide = dot((rel_now - rel_low).astype(F32).astype(BF16), c_plain[...], NT) + dot(
        rel_low.astype(F32).astype(BF16), c_plain[...], NT
    )
    rel_lane = jnp.bitwise_and(lax.broadcasted_iota(jnp.int32, (WT, KEYS), 1), 127)
    rel_wide = jnp.where(lax.rem(rel_lane, PITCH) < 12, rel_wide, -1.0)
    plain = lax.broadcasted_iota(jnp.int32, (72, 128), 0)
    plain = plain + 11 * (plain // 12)
    first, _, back = skew_parts(plain)
    slot = lax.broadcasted_iota(jnp.int32, (768, 128), 0).astype(F32)
    for b, block in enumerate((rel_wide[:72, :128], rel_wide[:72, 128:], rel_wide[72:, :128])):
        turned_back = jnp.take_along_axis(block, back, axis=1)
        for half in range(2):
            kept = jnp.where(first, turned_back, -1.0) if half == 0 else jnp.where(first, -1.0, turned_back)
            slots = jnp.max(kept, 0, keepdims=True)
            lanes = slice(b * 256 + half * 128, b * 256 + half * 128 + 128)
            onehot[:, lanes] = jnp.where(slot == slots, 1.0, 0.0).astype(BF16)
    table_in[...] = jnp.zeros_like(table_in)
    for w in range(2):
        table_in[w, :HEADS, :SLOTS] = pos[2 * lat + w] * LOG2E
        tables[w] = functools.reduce(jnp.add, [dot(part, onehot[...]) for part in split(table_in[w], 3)])

    d_tables[...] = jnp.zeros_like(d_tables)
    f_acc[...] = jnp.zeros_like(f_acc)
    zero = jnp.zeros((72, 128), F32)

    def group_step(g, carry):
        first, there, back = skew_parts(jnp.broadcast_to(c_rows[...], (72, 128)))
        lanes = pl.ds(pl.multiple_of(g * 128, 128), 128)
        v_lanes = pl.ds(pl.multiple_of(WIDTH + g * 128, 128), 128)
        cat_lane = lax.broadcasted_iota(jnp.int32, (1, 256), 1)
        feat_lane = cat_lane - 128
        for w in range(2):
            rows = slice(w * WT, (w + 1) * WT)
            q_cat = jnp.concatenate([qkv[rows, lanes], q_feat[...]], 1)
            k_cat = jnp.concatenate([kv_pad[w, :, lanes], k_feat[...]], 1)
            v_now = kv_pad[w, :, v_lanes]
            dctx_now = dctx[rows, lanes]
            ctx_sum = jnp.zeros((WT, 128), F32)
            dq_sum = jnp.zeros((WT, 128), F32)
            feat_sum = jnp.zeros((WT, 128), F32)
            for hh in range(4):
                head = g * 4 + hh
                mine = cat_lane // 32 == hh
                feat_mine = jnp.logical_and(
                    cat_lane >= 128,
                    jnp.logical_or(feat_lane >= 96, lax.rem(feat_lane // 4 + 12, 12) == head),
                )
                keep = jnp.logical_or(mine, feat_mine).astype(F32).astype(BF16)
                k_head = k_cat * keep
                v_head = v_now * keep[:, :128]
                raw = dot(q_cat, k_head, NT)
                d_raw = dot(dctx_now, v_head, NT)
                table = tables[w, pl.ds(head, 1), :]
                same = skew(table[:, :256], first, there)
                if w == 0:
                    upper = jnp.concatenate([same, skew(table[:, 256:512], first, there)], 1)
                    lower = jnp.concatenate([skew(table[:, 512:], first, there), same], 1)
                    bias = jnp.concatenate([upper, lower], 0)
                else:
                    raw = jnp.concatenate([raw[:72, :128], raw[72:, 128:]], 0)
                    d_raw = jnp.concatenate([d_raw[:72, :128], d_raw[72:, 128:]], 0)
                    bias = jnp.concatenate([same, same], 0)
                score = raw * (SCALE * LOG2E) + bias
                power = jnp.exp2(score - jnp.max(score, -1, keepdims=True))
                probs = power * (1.0 / jnp.sum(power, -1, keepdims=True))
                dot_sum = jnp.sum(d_raw * probs, -1, keepdims=True)
                d_score = probs * (d_raw - dot_sum)
                if w == 0:
                    probs_low = probs.astype(BF16)
                    score_low = d_score.astype(BF16)
                    blocks = (d_score[:72, :128] + d_score[72:, 128:], d_score[:72, 128:], d_score[72:, :128])
                else:
                    def wide(a):
                        top = jnp.concatenate([a[:72], zero], 1)
                        return jnp.concatenate([top, jnp.concatenate([zero, a[72:]], 1)], 0).astype(BF16)

                    probs_low = wide(probs)
                    score_low = wide(d_score)
                    blocks = (d_score[:72] + d_score[72:],)
                for b, block in enumerate(blocks):
                    turned_back = jnp.take_along_axis(block, back, axis=1)
                    early = jnp.where(first, turned_back, 0.0)
                    late = turned_back - early
                    d_tables[w, head, :, b * 256 : b * 256 + 128] = jnp.sum(early.reshape(9, 8, 128), 0)
                    d_tables[w, head, :, b * 256 + 128 : b * 256 + 256] = jnp.sum(late.reshape(9, 8, 128), 0)
                ctx_sum += dot(probs_low, v_head)
                both = dot(score_low, k_head)
                dq_sum += both[:, :128]
                feat_sum += both[:, 128:]
                head_rows = pl.ds(pl.multiple_of(g * 128 + hh * 32, 32), 32)
                dkv_t[w, 0, head_rows, :] = dot(turned[w, 0, head_rows, :], score_low) * SCALE
                dkv_t[w, 1, head_rows, :] = dot(turned[w, 1, head_rows, :], probs_low)
            ctx_acc[rows, lanes] = ctx_sum.astype(BF16)
            dq_acc[rows, lanes] = dq_sum * SCALE
            f_acc[w] += feat_sum
        return carry

    lax.fori_loop(0, 3, group_step, 0)

    for w in range(2):
        table = functools.reduce(jnp.add, [dot(part, onehot[...], NT) for part in split(jnp.sum(d_tables[w], 1), 2)])
        for half in range(2):
            for k in range(3):
                at = 128 * (3 * half + k)
                out_t[w, half, 16 * k : 16 * k + 16, :] = table[:, at : at + 128].astype(BF16)

    low[:, :WIDTH] = dq_acc[...].astype(BF16)
    sums = [jnp.sum(dq_acc[...], 0, keepdims=True)]
    for part in range(2):
        total = jnp.zeros((1, WIDTH), F32)
        for w in range(2):
            plain_rows = dot(c_spread[...], dkv_t[w, part].astype(BF16), (((0,), (1,)), ((), ())))
            total += jnp.sum(plain_rows, 0, keepdims=True)
            low[w * WT : (w + 1) * WT, WIDTH * (part + 1) : WIDTH * (part + 2)] = plain_rows.astype(BF16)
        sums.append(total)
    d_normed = dot(low[...], w_qkv[...], NT).astype(BF16).astype(F32)
    scaled = d_normed * gain[...]
    first_mean = jnp.mean(scaled, -1, keepdims=True)
    second_mean = jnp.mean(scaled * white[...], -1, keepdims=True)
    d_inputs = dy_low[...].astype(F32) + inv_std[...] * (scaled - first_mean - white[...] * second_mean)
    moved = dot(c_back[...], d_inputs.astype(BF16)).astype(BF16)
    for q in range(4):
        out_gx[q] = moved[q * 80 : q * 80 + 80]
    sums.append(jnp.sum(dy_low[...].astype(F32), 0, keepdims=True))
    sums.append(jnp.sum(d_normed * white[...], 0, keepdims=True))
    sums.append(jnp.sum(d_normed, 0, keepdims=True))
    of_row = jnp.where(lane < 4, of_key, 0.0).astype(BF16)
    d_surf = functools.reduce(jnp.add, [dot(of_row, part, TN) for part in split(f_acc[0] + f_acc[1], 2)])

    for j in range(4):
        if j < 3:
            grad = dot(normed[...], low[:, j * WIDTH : (j + 1) * WIDTH], TN)
        else:
            grad = dot(ctx_acc[...], dy_low[...], TN)
        for i in range(8):
            n = i * 4 + j
            for m in range(3):
                out_w[n // PLANE, n % PLANE, 48 * m : 48 * m + 48, :] = grad[
                    48 * i : 48 * i + 48, 128 * m : 128 * m + 128
                ].astype(BF16)
    extra_row = lax.broadcasted_iota(jnp.int32, (16, 128), 0) == 12
    for n in range(2 * PLANE):
        if n < 18:
            row = sums[n // 3][:, 128 * (n % 3) : 128 * (n % 3) + 128]
        elif n < 22:
            row = d_surf[n - 18 : n - 17, :]
        else:
            row = jnp.zeros((1, 128), F32)
        out_w[n // PLANE, n % PLANE, 144:160, :] = jnp.where(extra_row, row, 0.0).astype(BF16)


def windows(tok, cls, rel, gain, shift, w_qkv, b_qkv, w_proj, pos, surf, consts):
    operands = (tok, cls, rel, gain, shift, w_qkv, b_qkv, w_proj, pos, surf, *consts)
    return pl.pallas_call(
        window_kernel,
        out_shape=(
            jax.ShapeDtypeStruct((2, PLANE, 160, 128), BF16),
            jax.ShapeDtypeStruct((2, 2, 48, 128), BF16),
            jax.ShapeDtypeStruct((4, 80, WIDTH), BF16),
        ),
        in_specs=[VMEM] * len(operands),
        out_specs=(VMEM,) * 3,
        scratch_shapes=[
            pltpu.VMEM((288, WIDTH), F32),
            pltpu.VMEM((288, 1), F32),
            pltpu.VMEM((288, WIDTH), BF16),
            pltpu.VMEM((288, WIDTH), BF16),
            pltpu.VMEM((288, 3 * WIDTH), BF16),
            pltpu.VMEM((288, WIDTH), BF16),
            pltpu.VMEM((2, 2, WIDTH, WT), BF16),
            pltpu.VMEM((2, KEYS, 2 * WIDTH), BF16),
            pltpu.VMEM((WT, 128), BF16),
            pltpu.VMEM((KEYS, 128), BF16),
            pltpu.VMEM((768, 768), BF16),
            pltpu.VMEM((2, 16, 768), F32),
            pltpu.VMEM((2, 16, 8, 768), F32),
            pltpu.VMEM((288, WIDTH), BF16),
            pltpu.VMEM((288, WIDTH), F32),
            pltpu.VMEM((2, WT, 128), F32),
            pltpu.VMEM((2, 2, WIDTH, KEYS), F32),
            pltpu.VMEM((288, 3 * WIDTH), BF16),
            pltpu.VMEM((2, 16, 768), F32),
        ],
        compiler_params=pltpu.CompilerParams(vmem_limit_bytes=56 * 1024 * 1024),
        name="windows",
    )(*operands)


def reduce_kernel(
    wp, tp, gx, full, gx_out,
    c_recv, tc_recv, t_send, t_recv, p_send, p_recv, z_own, z_send, z_recv, z_full,
    h_sems, c_sems, t_sems, p_sems, z_sems, a_sems, g_sems, k_sems, local,
):
    lat, lon = lax.axis_index("lat"), lax.axis_index("lon")
    n_lat, n_lon = lax.axis_size("lat"), lax.axis_size("lon")
    core = lax.rem(lon, 2)
    z = lax.rem(lon // 2, PZ)
    x = lax.rem(lat, 2) * 2 + lon // (2 * PZ)
    y = lat // 2
    here = y * PX + x

    def device(x_at, y_at, z_at, core_at):
        return (y_at * 2 + x_at // 2, (lax.rem(x_at, 2) * PZ + z_at) * 2 + core_at)

    def in_plane(step, sign):
        x_at = lax.rem(x + PX + sign * (step % PX), PX)
        y_at = lax.rem(y + PY + sign * (step // PX), PY)
        return x_at, y_at, y_at * PX + x_at

    up, down = lax.rem(lat + 1, n_lat), lax.rem(lat + n_lat - 1, n_lat)
    east, west = lax.rem(lon + 1, n_lon), lax.rem(lon + n_lon - 1, n_lon)
    sibling = (lat, lon + 1 - 2 * core)
    x_pair = device(x + 1 - 2 * lax.rem(x, 2), y, z, core)

    barrier = pltpu.get_barrier_semaphore()
    greeted = [(lat, west), (down, lon), (down, west), sibling]
    for step in range(1, PLANE):
        x_at, y_at, _ = in_plane(step, -1)
        greeted.append(device(x_at, y_at, z, core))
    for step in range(1, PZ):
        greeted.append(device(x, y, lax.rem(z + PZ - step, PZ), core))
    for other in greeted:
        pl.semaphore_signal(barrier, inc=1, device_id=other, device_id_type=MESH)
    pl.semaphore_wait(barrier, len(greeted))

    def send(src, dst, sems, k, to):
        copy = pltpu.make_async_remote_copy(
            src_ref=src,
            dst_ref=dst,
            send_sem=sems.at[0, k],
            recv_sem=sems.at[1, k],
            device_id=to,
            device_id_type=MESH,
        )
        copy.start()
        return copy

    order = list(range(1, PLANE)) + [0]
    core_copies = {}
    t_copy = send(tp.at[1 - core], tc_recv, t_sems, 0, sibling)
    for step in order:
        at = in_plane(step, 1)[2]
        core_copies[step] = send(wp.at[1 - core, at], c_recv.at[step], c_sems, step, sibling)

    halo = [
        send(gx.at[1], gx_out.at[2], h_sems, 0, (lat, east)),
        send(gx.at[2], gx_out.at[1], h_sems, 1, (up, lon)),
        send(gx.at[3], gx_out.at[0], h_sems, 2, (up, east)),
    ]
    own = pltpu.make_async_copy(gx.at[0], gx_out.at[3], local)
    own.start()

    t_copy.wait()
    t_mine = lax.rem(x, 2)
    t_send[...] = (tp[core, 1 - t_mine].astype(F32) + tc_recv[1 - t_mine].astype(F32)).astype(BF16)
    tx_copy = send(t_send, t_recv, t_sems, 1, x_pair)
    plane_copies = []
    for step in range(1, PLANE):
        x_at, y_at, at = in_plane(step, 1)
        core_copies[step].wait()
        p_send[step] = (wp[core, at].astype(F32) + c_recv[step].astype(F32)).astype(BF16)
        plane_copies.append(send(p_send.at[step], p_recv.at[step], p_sems, step, device(x_at, y_at, z, core)))
    core_copies[0].wait()
    total = wp[core, here].astype(F32) + c_recv[0].astype(F32)
    tx_copy.wait()
    t_total = tp[core, t_mine].astype(F32) + tc_recv[t_mine].astype(F32) + t_recv[...].astype(F32)
    for step in range(1, PLANE):
        plane_copies[step - 1].wait()
        total = total + p_recv[step].astype(F32)
    z_own[0:144, :] = total[:144]
    z_own[144:160, :] = total[144:] + t_total[:16]
    z_own[160:192, :] = t_total[16:]

    for k in range(PZ):
        z_send[k] = z_own[24 * k : 24 * k + 24, :].astype(BF16)
    z_copies = []
    for step in range(1, PZ):
        z_at = lax.rem(z + step, PZ)
        z_copies.append(send(z_send.at[z_at], z_recv.at[step], z_sems, step, device(x, y, z_at, core)))
    summed = z_own[pl.ds(pl.multiple_of(24 * z, 8), 24), :]
    for step in range(1, PZ):
        z_copies[step - 1].wait()
        summed = summed + z_recv[step].astype(F32)
    z_full[z] = summed.astype(BF16)
    a_copies = []
    for step in range(1, PZ):
        z_at = lax.rem(z + step, PZ)
        a_copies.append(send(z_full.at[z], z_full.at[z], a_sems, step, device(x, y, z_at, core)))
    for copy in a_copies:
        copy.wait()
    full[core, here] = jnp.concatenate([z_full[k].astype(F32) for k in range(PZ)], 0).astype(BF16)

    g_copies = []
    for step in range(1, PLANE):
        x_at, y_at, _ = in_plane(step, 1)
        g_copies.append(send(full.at[core, here], full.at[core, here], g_sems, step, device(x_at, y_at, z, core)))
    k_copies = [send(full.at[core, here], full.at[core, here], k_sems, 0, sibling)]
    for step in range(1, PLANE):
        at = in_plane(step, -1)[2]
        g_copies[step - 1].wait()
        k_copies.append(send(full.at[core, at], full.at[core, at], k_sems, step, sibling))
    for copy in k_copies + halo:
        copy.wait()
    own.wait()


def reduce_all(wp, tp, gx):
    sems = pltpu.SemaphoreType.DMA
    return pl.pallas_call(
        reduce_kernel,
        out_shape=(
            jax.ShapeDtypeStruct((2, PLANE, 192, 128), BF16),
            jax.ShapeDtypeStruct((4, 80, WIDTH), BF16),
        ),
        in_specs=[VMEM] * 3,
        out_specs=(VMEM, VMEM),
        scratch_shapes=[
            pltpu.VMEM((PLANE, 160, 128), BF16),
            pltpu.VMEM((2, 48, 128), BF16),
            pltpu.VMEM((48, 128), BF16),
            pltpu.VMEM((48, 128), BF16),
            pltpu.VMEM((PLANE, 160, 128), BF16),
            pltpu.VMEM((PLANE, 160, 128), BF16),
            pltpu.VMEM((192, 128), F32),
            pltpu.VMEM((PZ, 24, 128), BF16),
            pltpu.VMEM((PZ, 24, 128), BF16),
            pltpu.VMEM((PZ, 24, 128), BF16),
            sems((2, 3)),
            sems((2, PLANE)),
            sems((2, 2)),
            sems((2, PLANE)),
            sems((2, PZ)),
            sems((2, PZ)),
            sems((2, PLANE)),
            sems((2, PLANE)),
            sems(()),
        ],
        compiler_params=pltpu.CompilerParams(
            collective_id=1, has_side_effects=True, vmem_limit_bytes=32 * 1024 * 1024
        ),
        name="reduce",
    )(wp, tp, gx)


def finish_kernel(grad_scale, full, gx, place, o_gx, o_wqkv, o_bqkv, o_wproj, o_bproj, o_gain, o_shift, o_pos, o_surf):
    rows = jnp.concatenate([gx[q] for q in range(4)], 0)
    o_gx[...] = dot(place[...], rows).astype(BF16).reshape(4, 6, 16, WIDTH)[:, :, :12, :]
    for j in range(4):
        for i in range(8):
            n = i * 4 + j
            for m in range(3):
                part = full[n // PLANE, n % PLANE, 48 * m : 48 * m + 48, :].astype(F32) * grad_scale
                if j < 3:
                    o_wqkv[48 * i : 48 * i + 48, WIDTH * j + 128 * m : WIDTH * j + 128 * m + 128] = part
                else:
                    o_wproj[48 * i : 48 * i + 48, 128 * m : 128 * m + 128] = part
    for core in range(2):
        for at in range(PLANE):
            x, y = at % PX, at // PX
            kind = (y * 2 + x // 2) * 2 + core
            for k in range(3):
                part = full[core, at, 144 + 16 * k : 160 + 16 * k, :].astype(F32) * grad_scale
                lo = 128 * (3 * (x % 2) + k)
                width = min(128, SLOTS - lo)
                o_pos[kind, :, lo : lo + width] = part[:HEADS, :width]

    def extra(n):
        tile = full[n // PLANE, n % PLANE, 144:160, :].astype(F32) * grad_scale
        return tile[12:13, :]

    for n in range(9):
        o_bqkv[:, 128 * n : 128 * n + 128] = extra(n)
    for v, out in enumerate((o_bproj, o_gain, o_shift)):
        for m in range(3):
            out[:, 128 * m : 128 * m + 128] = extra(9 + 3 * v + m)
    sides = jnp.concatenate([extra(18 + a) for a in range(4)], 0)
    for h in range(HEADS):
        o_surf[h] = sides[:, 4 * h : 4 * h + 4]


def finish(full, gx, place, grad_scale):
    one = lambda *shape: jax.ShapeDtypeStruct(shape, F32)
    return pl.pallas_call(
        functools.partial(finish_kernel, grad_scale),
        out_shape=(
            jax.ShapeDtypeStruct((4, 6, 12, WIDTH), BF16),
            one(WIDTH, 3 * WIDTH),
            one(1, 3 * WIDTH),
            one(WIDTH, WIDTH),
            one(1, WIDTH),
            one(1, WIDTH),
            one(1, WIDTH),
            one(16, HEADS, SLOTS),
            one(HEADS, 4, 4),
        ),
        in_specs=[VMEM] * 3,
        out_specs=(VMEM,) * 9,
        compiler_params=pltpu.CompilerParams(vmem_limit_bytes=32 * 1024 * 1024),
        name="finish",
    )(full, gx, place)


def on_device(
    inputs, cotangent, land_sea, rel_index, norm_gain, norm_shift, w_qkv, b_qkv, w_proj, pos_bias, surf_bias
):
    levels, lat_rows, lon_cols, width = inputs.shape
    count = levels * lat_rows * lon_cols * lax.axis_size("lat") * lax.axis_size("lon")
    consts, place = constants()
    both = jnp.stack([inputs, cotangent])
    both = jnp.roll(both, -1, 1).reshape(2, 4, 2, 3, 2, 6, width)
    buf = both.transpose(2, 4, 0, 1, 3, 5, 6).reshape(4, 144, width)
    cells = land_sea.reshape(2, 3, 2, 6).transpose(0, 2, 1, 3).reshape(4, 18, 1).astype(BF16)
    cells = jnp.pad(jnp.broadcast_to(cells, (4, 18, 128)), ((0, 0), (0, 14), (0, 0)))
    side = surf_bias.transpose(1, 0, 2).reshape(4, 48)
    side = jnp.pad(jnp.concatenate([side, side], 1), ((0, 124), (0, 32)))
    tok, cls = halo_forward(buf, cells)
    wp, tp, gx = windows(
        tok.reshape(576, width),
        cls.reshape(128, 128),
        rel_index,
        norm_gain.reshape(1, width),
        norm_shift.reshape(1, width),
        w_qkv,
        b_qkv.reshape(1, 3 * width),
        w_proj,
        pos_bias,
        side,
        tuple(jnp.asarray(a) for a in consts),
    )
    full, gx = reduce_all(wp, tp, gx)
    outs = finish(full, gx, jnp.asarray(place), float(count) ** -0.5)
    g_x, g_wqkv, g_bqkv, g_wproj, g_bproj, g_gain, g_shift, g_pos, g_surf = outs
    return (
        g_x,
        g_wqkv,
        g_bqkv.reshape(-1),
        g_wproj,
        g_bproj.reshape(-1),
        g_gain.reshape(-1),
        g_shift.reshape(-1),
        g_pos,
        g_surf,
    )


def solution(mesh):
    in_specs = (P(None, "lat", "lon", None), P(None, "lat", "lon", None), P("lat", "lon")) + (P(),) * 8
    out_specs = (P(None, "lat", "lon", None),) + (P(),) * 8
    return jax.shard_map(on_device, mesh=mesh, in_specs=in_specs, out_specs=out_specs, check_vma=False)
```

time: 767 us -> 107 us (0.14); the launches traced: 756 us -> 106 us
  other arithmetic: 256 us -> 6.78 us
  waiting for transfers between devices: 178 us -> 0 us
  local copies, waits for them, and re-layouts: 162 us -> 13.9 us
  Pallas kernels: 0 us -> 85 us
  blocking collectives: 76.4 us -> 0 us
  matrix products: 44.7 us -> 0 us
  starting transfers between devices: 23.1 us -> 0 us
  between operations: 15.2 us -> 0.72 us
    scatter-add x2 -> x0, other arithmetic: 226 us -> none  [table_grad(): jax.ops.segment_sum(flat_terms, rel_index.reshape(-1), num_segments=slot_...]
    psum x1 -> x0, waiting for transfers between devices: 178 us -> none  [on_device(): lax.psum((sum_wqkv, sum_bqkv, sum_wproj, sum_bproj, sum_gain, sum_shift,...]
    gather x4 -> x0, local copies, waits for them, and re-layouts: 102 us -> none  [on_device(): pos_terms = jnp.take(pos_rows, rel_index, axis=2)]
    pallas_call x0 -> x4, Pallas kernels: none -> 85 us  [the longest x1 47.2 us: reduce_all(): pl.pallas_call(reduce_kernel, out_shape=(jax.ShapeDtypeStruct((2, PLANE,...]
    psum x1 -> x0, blocking collectives: 76.4 us -> none  [on_device(): lax.psum((sum_wqkv, sum_bqkv, sum_wproj, sum_bproj, sum_gain, sum_shift,...]
    dot_general x28 -> x0, matrix products: 44.7 us -> none  [the longest x2 7.14 us: window_core(): jnp.einsum('bhqk,bkhd->bqhd', probs_low, value_vecs, preferred_element_ty...]
    ppermute x8 -> x0, starting transfers between devices: 23 us -> none  [passed_along(): return lax.ppermute(block, axis, route)]
    transpose x2 -> x1, local copies, waits for them, and re-layouts: 12.5 us -> 0.8 us  [on_device(): side = surf_bias.transpose(1, 0, 2).reshape(4, 48)]
  transfers between devices with their start and end apart: 9 -> 0, of which waited for: 3 -> 0; matrix products, arithmetic and copies ran while one was open for 52% -> 0% of each run, Pallas kernels for 0% -> 0%
where the time goes in v1:
time: 107 us; the launch traced here: 106 us
  Pallas kernels  85 us (79%)
  local copies, waits for them, and re-layouts  13.9 us (13%)
  other arithmetic  6.78 us (6%)
    pallas_call x1, Pallas kernels, reduce_all(): pl.pallas_call(reduce_kernel, out_shape=(jax.ShapeDtypeStruct((2, PLANE,...  47.2 us
    pallas_call x1, Pallas kernels, windows(): pl.pallas_call(window_kernel, out_shape=(jax.ShapeDtypeStruct((2, PLANE,...  22.8 us
    pallas_call x1, Pallas kernels, halo_forward(): pl.pallas_call(halo_kernel, out_shape=(jax.ShapeDtypeStruct(buf.shape, bu...  13.1 us
    unnamed x14, local copies, waits for them, and re-layouts  6.95 us
    pallas_call x4, other arithmetic, finish(): pl.pallas_call(functools.partial(finish_kernel, grad_scale), out_shape=(j...  2.4 us

profile of v1, /device:TPU:1, one launch (start us, length us, event | category | flops | bytes accessed | tf_op | source)
XLA Modules:
  0.0 106.3 jit_solution(12885769428284098827)
XLA Ops:
  0.6 1.2 %reshape.69.gain = f32[1,384]{1,0:T(1,128)} reshape(f32[384]{0:T(512)} %param.22) | data formatting | bytes 3072 | tf_op jit(solution)/shard_map/reshape | solution.py:621
  1.9 1.2 %reshape.70.shift = f32[1,384]{1,0:T(1,128)} reshape(f32[384]{0:T(512)} %param.23) | data formatting | bytes 3072 | tf_op jit(solution)/shard_map/reshape | solution.py:622
  3.1 0.7 convert_element_type.21
  3.8 0.1 convert_element_type.22
  3.9 0.1 convert_element_type.24
  4.0 1.3 %reshape.71.b_qkv = f32[1,1152]{1,0:T(1,128)} reshape(f32[1152]{0:T(1024)} %param.25) | data formatting | bytes 9216 | tf_op jit(solution)/shard_map/reshape | solution.py:624
  5.3 0.1 broadcast_in_dim.2
  5.4 0.6 pad.8.cls
  6.0 0.8 copy.37
  6.8 0.1 reshape.72
  6.9 0.7 select_maximum_fusion.surf
  7.6 1.5 %slice_maximum_fusion = bf16[2,3,6,12,384]{4,1,3,2,0:T(4,128)(2,1)S(1)} fusion(bf16[1,4,6,12,384]{4,1,3,2,0:T(4,128)(2,1)} %bitcast.14, bf16[1,4,6,12,384]{4,1,3,2,0:T(4,128)(2,1)} %bitcast.16), kind=kLoop, calls=%fused_computation.2 | loop fusion | flops 165888 | bytes 774144 | tf_op jit(solution)/shard_map/stack | solution.py:609
  9.1 1.5 %fusion = bf16[2,4,6,12,384]{4,1,3,2,0:T(4,128)(2,1)S(1)} fusion(bf16[1,4,6,12,384]{4,1,3,2,0:T(4,128)(2,1)} %bitcast.15, bf16[1,4,6,12,384]{4,1,3,2,0:T(4,128)(2,1)} %bitcast.17, bf16[2,3,6,12,384]{4,1,3,2,0:T(4,128)(2,1)S(1)} %slice_maximum_fusion), kind=kLoop, calls=%fused_computation.1 | loop fusion | flops 1327104 | bytes 1216512 | tf_op jit(solution)/shard_map/jit(_roll_static)/concatenate | solution.py:610
  10.6 0.0 copy-start.4
  10.6 0.3 copy.43
  11.0 0.2 reshape.66
  11.2 0.8 copy.36.buf
  12.0 13.1 %halo.1 = (bf16[4,144,384]{2,1,0:T(8,128)(2,1)}, bf16[4,32,128]{2,1,0:T(8,128)(2,1)}) custom-call(bf16[4,144,384]{2,1,0:T(8,128)(2,1)} %copy.36.buf, bf16[4,32,128]{2,1,0:T(8,128)(2,1)} %pad.8.cls), custom_call_target="tpu_custom_call" | custom-call | tf_op jit(solution)/shard_map/halo/pallas_call | solution.py:108
  25.1 1.2 %copy.38.pos = f32[16,12,759]{2,1,0:T(8,128)} copy(f32[16,12,759]{2,0,1:T(8,128)S(1)} %copy-done.4) | data formatting | bytes 1165824 | tf_op args[9]
  26.4 22.8 %windows.1 = (bf16[2,16,160,128]{3,2,1,0:T(8,128)(2,1)}, bf16[2,2,48,128]{3,2,1,0:T(8,128)(2,1)}, bf16[4,80,384]{2,1,0:T(8,128)(2,1)}) custom-call(bf16[576,384]{1,0:T(8,128)(2,1)} %bitcast.18, bf16[128,128]{1,0:T(8,128)(2,1)} %bitcast.19, s32[144,144]{1,0:T(8,128)} %rel.1, f32[1,384]{1,0:T(1,128)} %reshape.69.gain, f32[1,384]{1,0:T(1,128)} %reshape.70.shift, ...), custom_call_target="tpu_custom_call" | custom-call | tf_op jit(solution)/shard_map/windows/pallas_call | solution.py:354
  49.1 1.3 %copy-done = bf16[2,16,160,128]{3,2,1,0:T(8,128)(2,1)S(1)} copy-done((bf16[2,16,160,128]{3,2,1,0:T(8,128)(2,1)S(1)}, bf16[2,16,160,128]{3,2,1,0:T(8,128)(2,1)}, u32[]{:S(2)}) %copy-start) | copy-done | bytes 1310744
  50.5 0.9 copy-done.2
  51.4 0.8 copy-done.3
  52.2 47.2 %reduce.5 = (bf16[2,16,192,128]{3,2,1,0:T(8,128)(2,1)S(1)}, bf16[4,80,384]{2,1,0:T(8,128)(2,1)S(1)}) custom-call(bf16[2,16,160,128]{3,2,1,0:T(8,128)(2,1)S(1)} %copy-done, bf16[2,2,48,128]{3,2,1,0:T(8,128)(2,1)S(1)} %copy-done.3, bf16[4,80,384]{2,1,0:T(8,128)(2,1)S(1)} %copy-done.2), custom_call_target="tpu_custom_call" | custom-call | tf_op jit(solution)/shard_map/reduce/pallas_call | solution.py:509
  99.5 1.8 %finish.1 = (bf16[4,6,12,384]{3,2,1,0:T(8,128)(2,1)S(1)}, f32[384,1152]{1,0:T(8,128)}, f32[1,1152]{1,0:T(1,128)S(1)}, f32[384,384]{1,0:T(8,128)}, f32[1,384]{1,0...) custom-call(bf16[2,16,192,128]{3,2,1,0:T(8,128)(2,1)S(1)} %get-tuple, ...), custom_call_target="tpu_custom_call" | custom-call | tf_op jit(solution)/shard_map/finish/pallas_call | solution.py:583
  101.3 0.8 copy.39
  102.1 0.6 reduce.2
  102.7 0.6 reduce.3
  103.2 0.6 reduce.4
  103.8 0.6 reduce.1
  104.5 0.7 copy.41
  105.2 1.2 %copy.40 = f32[16,12,759]{2,0,1:T(8,128)} copy(f32[16,12,759]{2,1,0:T(8,128)S(1)} %get-tuple-element.57) | data formatting | bytes 1165824
  (7 shorter events, 0.0 us)
Async XLA Ops:
  10.6 14.5 %copy-start.4 = (f32[16,12,759]{2,0,1:T(8,128)S(1)}, f32[16,12,759]{2,0,1:T(8,128)}, u32[]{:S(2)}) copy-start(f32[16,12,759]{2,0,1:T(8,128)} %param.27) | copy-start | bytes 1748740
  26.4 73.1 %copy-start.1 = (bf16[384,320]{1,0:T(8,128)(2,1)S(1)}, bf16[384,320]{1,0:T(8,128)(2,1)}, u32[]{:S(2)}) copy-start(bf16[384,320]{1,0:T(8,128)(2,1)} %constant.25.clone.place) | copy-start | bytes 737284
  49.1 1.3 %copy-start = (bf16[2,16,160,128]{3,2,1,0:T(8,128)(2,1)S(1)}, bf16[2,16,160,128]{3,2,1,0:T(8,128)(2,1)}, u32[]{:S(2)}) copy-start(bf16[2,16,160,128]{3,2,1,0:T(8,128)(2,1)} %get-tuple-element.27.wp) | copy-start | bytes 3932164
  50.4 0.9 copy-start.2
  51.4 0.8 copy-start.3

commit v2 on v1

v2 whole, which is shorter than its diff:
```python
import functools

import jax
import jax.numpy as jnp
import ml_dtypes
import numpy as np
from jax import lax
from jax.experimental import pallas as pl
from jax.experimental.pallas import tpu as pltpu
from jax.sharding import PartitionSpec as P

F32 = jnp.float32
BF16 = jnp.bfloat16
MESH = pl.DeviceIdType.MESH
EPS = 1e-05
LOG2E = 1.4426950408889634
BIG = 2.0**33
HEADS = 12
SLOTS = 759
WIDTH = 384
WT = 144
PITCH = 23
KEYS = 256
SCALE = 32.0**-0.5
NT = (((1,), (1,)), ((), ()))
TN = (((0,), (0,)), ((), ()))
NN = (((1,), (0,)), ((), ()))
PX, PY, PZ = 4, 4, 8
PLANE = PX * PY
VMEM = pl.BlockSpec(memory_space=pltpu.VMEM)


def dot(a, b, dims=NN):
    return lax.dot_general(a, b, dims, preferred_element_type=F32)


def constants():
    spread = np.zeros((KEYS, WT), np.float32)
    of_row = np.zeros((WT, 32), np.float32)
    of_col = np.zeros((WT, 128), np.float32)
    for k in range(WT):
        li, ri, ci = k // 72, k // 12 % 6, k % 12
        spread[li * 128 + PITCH * ri + ci, k] = 1
        of_row[k, 8 * (2 * (ri // 3) + ci // 6) + ri % 3] = 1
        of_col[k, ci % 6] = 1
    return tuple(a.astype(ml_dtypes.bfloat16) for a in (spread, of_row, of_col))


class Place:
    def __init__(self):
        lat, lon = lax.axis_index("lat"), lax.axis_index("lon")
        n_lat, n_lon = lax.axis_size("lat"), lax.axis_size("lon")
        self.lat, self.n_lat = lat, n_lat
        self.core = lax.rem(lon, 2)
        self.z = lax.rem(lon // 2, PZ)
        self.x = lax.rem(lat, 2) * 2 + lon // (2 * PZ)
        self.y = lat // 2
        self.here = self.y * PX + self.x
        up, down = lax.rem(lat + 1, n_lat), lax.rem(lat + n_lat - 1, n_lat)
        right, left = lax.rem(lon + 1, n_lon), lax.rem(lon + n_lon - 1, n_lon)
        self.north, self.south = (up, lon), (down, lon)
        self.east, self.west = (lat, right), (lat, left)
        self.north_east, self.south_west = (up, right), (down, left)
        self.sibling = (lat, lon + 1 - 2 * self.core)
        self.x_pair = self.device(self.x + 1 - 2 * lax.rem(self.x, 2), self.y, self.z, self.core)

    def device(self, x, y, z, core):
        return (y * 2 + x // 2, (lax.rem(x, 2) * PZ + z) * 2 + core)

    def in_plane(self, step, sign):
        x = lax.rem(self.x + PX + sign * (step % PX), PX)
        y = lax.rem(self.y + PY + sign * (step // PX), PY)
        return x, y, y * PX + x

    def greet(self):
        others = [self.north, self.south, self.east, self.west, self.north_east, self.south_west, self.sibling]
        for step in range(1, PLANE):
            x, y, _ = self.in_plane(step, -1)
            others.append(self.device(x, y, self.z, self.core))
        for step in range(1, PZ):
            others.append(self.device(self.x, self.y, lax.rem(self.z + PZ - step, PZ), self.core))
        for other in others:
            pl.semaphore_signal(pltpu.get_barrier_semaphore(), inc=1, device_id=other, device_id_type=MESH)
        self.greeted = len(others)

    def meet(self):
        pl.semaphore_wait(pltpu.get_barrier_semaphore(), self.greeted)


def send(src, dst, sems, k, to):
    copy = pltpu.make_async_remote_copy(
        src_ref=src,
        dst_ref=dst,
        send_sem=sems.at[0, k],
        recv_sem=sems.at[1, k],
        device_id=to,
        device_id_type=MESH,
    )
    copy.start()
    return copy


def plain_rows():
    rows = lax.broadcasted_iota(jnp.int32, (72, 128), 0)
    return rows + (PITCH - 12) * (rows // 12)


def skew_parts(rows):
    lane = lax.broadcasted_iota(jnp.int32, (72, 128), 1)
    first = lane + rows >= PITCH * 5 + 11
    there = jnp.bitwise_and(lane - rows - 2, 127)
    back = jnp.bitwise_and(lane + rows + 2, 127)
    return first, there, back


def skew(table, first, there):
    mixed = jnp.where(first, table[:, :128], table[:, 128:])
    return jnp.take_along_axis(mixed, there, axis=1)


def split(values, count):
    pieces = []
    for _ in range(count):
        piece = values.astype(BF16)
        pieces.append(piece)
        values = values - piece.astype(F32)
    return pieces


def step_kernel(
    x_in, dy_in, land, rel, gain, shift, w_qkv, b_qkv, w_proj, pos, surf, c_spread, c_row, c_col,
    full, gx_out,
    tok_x, tok_dy, cls_out, cls_in, side_in, wp, tp, gx,
    mixed, white, inv_std, normed, dy_low, qkv, dctx, turned, kv_pad, q_feat, k_feat,
    onehot, tables, d_tables, ctx_acc, dq_acc, f_acc, dkv_t, low, table_in,
    c_recv, tc_recv, t_send, t_recv, p_send, p_recv, z_own, z_send, z_recv, z_full,
    f_sems, h_sems, c_sems, t_sems, p_sems, z_sems, a_sems, g_sems, k_sems, local,
):
    place = Place()
    place.greet()

    cls_out[...] = jnp.zeros_like(cls_out)
    for q in range(4):
        cls_out[q, :3, :6] = land[3 * (q // 2) : 3 * (q // 2) + 3, 6 * (q % 2) : 6 * (q % 2) + 6].astype(F32)

    def quadrant(ref, q):
        return ref.at[pl.ds(3 * (q // 2), 3), pl.ds(6 * (q % 2), 6)]

    place.meet()
    halo = []
    for k, (q, to) in enumerate(((2, place.west), (1, place.south), (0, place.south_west))):
        for m, (a, b) in enumerate(((x_in, tok_x), (dy_in, tok_dy))):
            halo.append(send(quadrant(a, q), quadrant(b, 3 - q), f_sems, 3 * k + m, to))
        halo.append(send(cls_out.at[q], cls_in.at[3 - q], f_sems, 3 * k + 2, to))
    own = [
        pltpu.make_async_copy(quadrant(x_in, 3), quadrant(tok_x, 0), local.at[0]),
        pltpu.make_async_copy(quadrant(dy_in, 3), quadrant(tok_dy, 0), local.at[1]),
        pltpu.make_async_copy(cls_out.at[3], cls_in.at[0], local.at[2]),
    ]
    for copy in own:
        copy.start()

    lat = place.lat
    last_band = lat == place.n_lat - 1
    rel_now = rel[...]
    rel_low = jnp.bitwise_and(rel_now, 15)
    rel_wide = dot((rel_now - rel_low).astype(F32).astype(BF16), c_spread[...], NT) + dot(
        rel_low.astype(F32).astype(BF16), c_spread[...], NT
    )
    rel_lane = jnp.bitwise_and(lax.broadcasted_iota(jnp.int32, (WT, KEYS), 1), 127)
    rel_wide = jnp.where(lax.rem(rel_lane, PITCH) < 12, rel_wide, -1.0)
    first, _, back = skew_parts(plain_rows())
    slot = lax.broadcasted_iota(jnp.int32, (768, 128), 0).astype(F32)
    for b, block in enumerate((rel_wide[:72, :128], rel_wide[:72, 128:], rel_wide[72:, :128])):
        turned_back = jnp.take_along_axis(block, back, axis=1)
        for half in range(2):
            kept = jnp.where(first, turned_back, -1.0) if half == 0 else jnp.where(first, -1.0, turned_back)
            slots = jnp.max(kept, 0, keepdims=True)
            lanes = slice(b * 256 + half * 128, b * 256 + half * 128 + 128)
            onehot[:, lanes] = jnp.where(slot == slots, 1.0, 0.0).astype(BF16)
    table_in[...] = jnp.zeros_like(table_in)
    for w in range(2):
        for h in range(HEADS):
            table_in[w, h : h + 1, :SLOTS] = pos[pl.ds(16 * h + 2 * lat + w, 1), :] * LOG2E
        tables[w] = functools.reduce(jnp.add, [dot(part, onehot[...]) for part in split(table_in[w], 3)])


    for copy in halo + own:
        copy.wait()
    for j in range(3):
        cols = slice(128 * j, 128 * j + 128)
        mixed[j, :, 0:4, :] = tok_x[:, :, :, cols].reshape(72, 4, 128).astype(F32)
        mixed[j, :, 4:8, :] = tok_dy[:, :, :, cols].reshape(72, 4, 128).astype(F32)
    strided = mixed.reshape(3 * 576, 128)
    for k in range(4):
        level = (1, 2, 3, 0)[k]
        rows = slice(72 * k, 72 * k + 72)
        for j in range(3):
            cols = slice(128 * j, 128 * j + 128)
            white[rows, cols] = strided[pl.ds(576 * j + level, 72, stride=8), :]
            dq_acc[rows, cols] = strided[pl.ds(576 * j + 4 + level, 72, stride=8), :]
    x = white[...]
    dy_low[...] = dq_acc[...].astype(BF16)
    centred = x - jnp.mean(x, -1, keepdims=True)
    inv = lax.rsqrt(jnp.mean(centred * centred, -1, keepdims=True) + EPS)
    inv_std[...] = inv
    whitened = centred * inv
    white[...] = whitened
    gain_row = gain[...].reshape(1, WIDTH)
    normed[...] = (whitened * gain_row + shift[...].reshape(1, WIDTH)).astype(BF16)
    qkv[...] = (dot(normed[...], w_qkv[...]) + b_qkv[...].reshape(1, 3 * WIDTH)).astype(BF16)
    dctx[...] = dot(dy_low[...], w_proj[...], NT).astype(BF16)
    eye = (
        lax.broadcasted_iota(jnp.int32, (WIDTH, WIDTH), 0) == lax.broadcasted_iota(jnp.int32, (WIDTH, WIDTH), 1)
    ).astype(F32).astype(BF16)
    for w in range(2):
        rows = slice(w * WT, (w + 1) * WT)
        turned[w, 0] = dot(eye, qkv[rows, :WIDTH], NT).astype(BF16)
        turned[w, 1] = dot(eye, dctx[rows, :], NT).astype(BF16)
        kv_pad[w] = dot(c_spread[...], qkv[rows, WIDTH:]).astype(BF16)

    lane = lax.broadcasted_iota(jnp.int32, (WT, 128), 1)
    token = lax.broadcasted_iota(jnp.int32, (WT, 128), 0)
    cells = dot(c_row[...], cls_in[...].reshape(32, 128).astype(BF16)) * c_col[...].astype(F32)
    kind = dot(cells.astype(BF16), jnp.ones((128, 128), BF16)).astype(jnp.int32)
    turned_over = jnp.logical_and(lax.rem(token, 72) >= 36, last_band).astype(F32)
    of_key = jnp.where(kind == lax.rem(lane, 48) // 12, 1.0, 0.0)
    of_query = jnp.where(kind == lane, 1.0, 0.0).astype(BF16)
    side_in[...] = jnp.zeros_like(side_in)
    for a in range(4):
        for b in range(4):
            side_in[a : a + 1, 12 * b : 12 * b + 12] = surf[a, b : b + 1, :]
            side_in[a : a + 1, 48 + 12 * b : 60 + 12 * b] = surf[a, b : b + 1, :]
    surf_lane = lax.broadcasted_iota(jnp.int32, (128, 128), 1)
    surf_hi, surf_lo = split(side_in[...] * (1.0 / SCALE), 2)
    side = dot(of_query, jnp.where(surf_lane < 48, surf_hi.astype(F32), surf_lo.astype(F32)).astype(BF16))
    q_feat[...] = jnp.where(
        lane < 96, side, jnp.where(lane == 96, turned_over, jnp.where(lane == 97, 1.0 - turned_over, 0.0))
    ).astype(BF16)
    key_side = jnp.where(
        lane < 96,
        of_key,
        jnp.where(lane == 96, -BIG * (1.0 - turned_over), jnp.where(lane == 97, -BIG * turned_over, 0.0)),
    ).astype(BF16)
    key_lane = lax.broadcasted_iota(jnp.int32, (KEYS, 128), 1)
    key_row = jnp.bitwise_and(lax.broadcasted_iota(jnp.int32, (KEYS, 128), 0), 127)
    hidden = jnp.logical_and(lax.rem(key_row, PITCH) >= 12, jnp.logical_and(key_lane >= 96, key_lane < 98))
    k_feat[...] = jnp.where(hidden, -BIG, dot(c_spread[...], key_side)).astype(BF16)

    d_tables[...] = jnp.zeros_like(d_tables)
    f_acc[...] = jnp.zeros_like(f_acc)
    zero = jnp.zeros((72, 128), F32)

    def group_step(g, carry):
        first, there, back = skew_parts(plain_rows())
        lanes = pl.ds(pl.multiple_of(g * 128, 128), 128)
        v_lanes = pl.ds(pl.multiple_of(WIDTH + g * 128, 128), 128)
        cat_lane = lax.broadcasted_iota(jnp.int32, (1, 256), 1)
        feat_lane = cat_lane - 128
        for w in range(2):
            rows = slice(w * WT, (w + 1) * WT)
            q_cat = jnp.concatenate([qkv[rows, lanes], q_feat[...]], 1)
            k_cat = jnp.concatenate([kv_pad[w, :, lanes], k_feat[...]], 1)
            v_now = kv_pad[w, :, v_lanes]
            dctx_now = dctx[rows, lanes]
            ctx_sum = jnp.zeros((WT, 128), F32)
            dq_sum = jnp.zeros((WT, 128), F32)
            feat_sum = jnp.zeros((WT, 128), F32)
            for hh in range(4):
                head = g * 4 + hh
                mine = cat_lane // 32 == hh
                feat_mine = jnp.logical_and(
                    cat_lane >= 128,
                    jnp.logical_or(feat_lane >= 96, lax.rem(feat_lane + 132, 12) == head),
                )
                keep = jnp.logical_or(mine, feat_mine).astype(F32).astype(BF16)
                k_head = k_cat * keep
                v_head = v_now * keep[:, :128]
                raw = dot(q_cat, k_head, NT)
                d_raw = dot(dctx_now, v_head, NT)
                table = tables[w, pl.ds(head, 1), :]
                same = skew(table[:, :256], first, there)
                if w == 0:
                    upper = jnp.concatenate([same, skew(table[:, 256:512], first, there)], 1)
                    lower = jnp.concatenate([skew(table[:, 512:], first, there), same], 1)
                    bias = jnp.concatenate([upper, lower], 0)
                else:
                    raw = jnp.concatenate([raw[:72, :128], raw[72:, 128:]], 0)
                    d_raw = jnp.concatenate([d_raw[:72, :128], d_raw[72:, 128:]], 0)
                    bias = jnp.concatenate([same, same], 0)
                score = raw * (SCALE * LOG2E) + bias
                power = jnp.exp2(score - jnp.max(score, -1, keepdims=True))
                probs = power * (1.0 / jnp.sum(power, -1, keepdims=True))
                dot_sum = jnp.sum(d_raw * probs, -1, keepdims=True)
                d_score = probs * (d_raw - dot_sum)
                if w == 0:
                    probs_low = probs.astype(BF16)
                    score_low = d_score.astype(BF16)
                    blocks = (d_score[:72, :128] + d_score[72:, 128:], d_score[:72, 128:], d_score[72:, :128])
                else:
                    def wide(a):
                        top = jnp.concatenate([a[:72], zero], 1)
                        return jnp.concatenate([top, jnp.concatenate([zero, a[72:]], 1)], 0).astype(BF16)

                    probs_low = wide(probs)
                    score_low = wide(d_score)
                    blocks = (d_score[:72] + d_score[72:],)
                for b, block in enumerate(blocks):
                    turned_back = jnp.take_along_axis(block, back, axis=1)
                    early = jnp.where(first, turned_back, 0.0)
                    late = turned_back - early
                    d_tables[w, head, :, b * 256 : b * 256 + 128] = jnp.sum(early.reshape(9, 8, 128), 0)
                    d_tables[w, head, :, b * 256 + 128 : b * 256 + 256] = jnp.sum(late.reshape(9, 8, 128), 0)
                ctx_sum += dot(probs_low, v_head)
                both = dot(score_low, k_head)
                dq_sum += both[:, :128]
                feat_sum += both[:, 128:]
                head_rows = pl.ds(pl.multiple_of(g * 128 + hh * 32, 32), 32)
                dkv_t[w, 0, head_rows, :] = dot(turned[w, 0, head_rows, :], score_low) * SCALE
                dkv_t[w, 1, head_rows, :] = dot(turned[w, 1, head_rows, :], probs_low)
            ctx_acc[rows, lanes] = ctx_sum.astype(BF16)
            dq_acc[rows, lanes] = dq_sum * SCALE
            f_acc[w] += feat_sum
        return carry

    lax.fori_loop(0, 3, group_step, 0)

    for w in range(2):
        table = functools.reduce(jnp.add, [dot(part, onehot[...], NT) for part in split(jnp.sum(d_tables[w], 1), 2)])
        for half in range(2):
            for k in range(3):
                at = 128 * (3 * half + k)
                tp[w, half, 16 * k : 16 * k + 16, :] = table[:, at : at + 128].astype(BF16)

    low[:, :WIDTH] = dq_acc[...].astype(BF16)
    sums = [jnp.sum(dq_acc[...], 0, keepdims=True)]
    for part in range(2):
        total = jnp.zeros((1, WIDTH), F32)
        for w in range(2):
            token_rows = dot(c_spread[...], dkv_t[w, part].astype(BF16), (((0,), (1,)), ((), ())))
            total += jnp.sum(token_rows, 0, keepdims=True)
            low[w * WT : (w + 1) * WT, WIDTH * (part + 1) : WIDTH * (part + 2)] = token_rows.astype(BF16)
        sums.append(total)
    d_normed = dot(low[...], w_qkv[...], NT).astype(BF16).astype(F32)
    scaled = d_normed * gain_row
    first_mean = jnp.mean(scaled, -1, keepdims=True)
    second_mean = jnp.mean(scaled * white[...], -1, keepdims=True)
    d_inputs = dy_low[...].astype(F32) + inv_std[...] * (scaled - first_mean - white[...] * second_mean)
    dq_acc[...] = d_inputs
    for j in range(3):
        cols = slice(128 * j, 128 * j + 128)
        for k in range(4):
            level = (1, 2, 3, 0)[k]
            strided[pl.ds(576 * j + level, 72, stride=8), :] = dq_acc[72 * k : 72 * k + 72, cols]
        gx[:, :, :, cols] = mixed[j, :, 0:4, :].astype(BF16).reshape(6, 12, 4, 128)
    sums.append(jnp.sum(dy_low[...].astype(F32), 0, keepdims=True))
    sums.append(jnp.sum(d_normed * white[...], 0, keepdims=True))
    sums.append(jnp.sum(d_normed, 0, keepdims=True))
    d_surf = functools.reduce(jnp.add, [dot(of_query, part, TN) for part in split(f_acc[0] + f_acc[1], 2)])

    for j in range(4):
        if j < 3:
            grad = dot(normed[...], low[:, j * WIDTH : (j + 1) * WIDTH], TN)
        else:
            grad = dot(ctx_acc[...], dy_low[...], TN)
        for i in range(8):
            n = i * 4 + j
            for m in range(3):
                wp[n // PLANE, n % PLANE, 48 * m : 48 * m + 48, :] = grad[
                    48 * i : 48 * i + 48, 128 * m : 128 * m + 128
                ].astype(BF16)
    extra_row = lax.broadcasted_iota(jnp.int32, (16, 128), 0) == 12
    for n in range(2 * PLANE):
        if n < 18:
            row = sums[n // 3][:, 128 * (n % 3) : 128 * (n % 3) + 128]
        elif n < 22:
            row = d_surf[n - 18 : n - 17, :]
        else:
            row = jnp.zeros((1, 128), F32)
        wp[n // PLANE, n % PLANE, 144:160, :] = jnp.where(extra_row, row, 0.0).astype(BF16)

    core, x, y, z, here = place.core, place.x, place.y, place.z, place.here

    order = list(range(1, PLANE)) + [0]
    core_copies = {}
    t_copy = send(tp.at[1 - core], tc_recv, t_sems, 0, place.sibling)
    for step in order:
        at = place.in_plane(step, 1)[2]
        core_copies[step] = send(wp.at[1 - core, at], c_recv.at[step], c_sems, step, place.sibling)

    halo = [
        send(quadrant(gx, q), quadrant(gx_out, 3 - q), h_sems, q - 1, to)
        for q, to in ((1, place.east), (2, place.north), (3, place.north_east))
    ]
    own = pltpu.make_async_copy(quadrant(gx, 0), quadrant(gx_out, 3), local.at[3])
    own.start()

    t_copy.wait()
    t_mine = lax.rem(x, 2)
    t_send[...] = (tp[core, 1 - t_mine].astype(F32) + tc_recv[1 - t_mine].astype(F32)).astype(BF16)
    tx_copy = send(t_send, t_recv, t_sems, 1, place.x_pair)
    plane_copies = []
    for step in range(1, PLANE):
        x_at, y_at, at = place.in_plane(step, 1)
        core_copies[step].wait()
        p_send[step] = (wp[core, at].astype(F32) + c_recv[step].astype(F32)).astype(BF16)
        plane_copies.append(send(p_send.at[step], p_recv.at[step], p_sems, step, place.device(x_at, y_at, z, core)))
    core_copies[0].wait()
    total = wp[core, here].astype(F32) + c_recv[0].astype(F32)
    tx_copy.wait()
    t_total = tp[core, t_mine].astype(F32) + tc_recv[t_mine].astype(F32) + t_recv[...].astype(F32)
    for step in range(1, PLANE):
        plane_copies[step - 1].wait()
        total = total + p_recv[step].astype(F32)
    z_own[0:144, :] = total[:144]
    z_own[144:160, :] = total[144:] + t_total[:16]
    z_own[160:192, :] = t_total[16:]

    for k in range(PZ):
        z_send[k] = z_own[24 * k : 24 * k + 24, :].astype(BF16)
    z_copies = []
    for step in range(1, PZ):
        z_at = lax.rem(z + step, PZ)
        z_copies.append(send(z_send.at[z_at], z_recv.at[step], z_sems, step, place.device(x, y, z_at, core)))
    summed = z_own[pl.ds(pl.multiple_of(24 * z, 8), 24), :]
    for step in range(1, PZ):
        z_copies[step - 1].wait()
        summed = summed + z_recv[step].astype(F32)
    z_full[z] = summed.astype(BF16)
    a_copies = []
    for step in range(1, PZ):
        z_at = lax.rem(z + step, PZ)
        a_copies.append(send(z_full.at[z], z_full.at[z], a_sems, step, place.device(x, y, z_at, core)))
    for copy in a_copies:
        copy.wait()
    full[core, here] = jnp.concatenate([z_full[k].astype(F32) for k in range(PZ)], 0).astype(BF16)

    g_copies = []
    for step in range(1, PLANE):
        x_at, y_at, _ = place.in_plane(step, 1)
        g_copies.append(send(full.at[core, here], full.at[core, here], g_sems, step, place.device(x_at, y_at, z, core)))
    k_copies = [send(full.at[core, here], full.at[core, here], k_sems, 0, place.sibling)]
    for step in range(1, PLANE):
        at = place.in_plane(step, -1)[2]
        g_copies[step - 1].wait()
        k_copies.append(send(full.at[core, at], full.at[core, at], k_sems, step, place.sibling))
    for copy in k_copies + halo:
        copy.wait()
    own.wait()


def step(*operands):
    sems = pltpu.SemaphoreType.DMA
    return pl.pallas_call(
        step_kernel,
        out_shape=(
            jax.ShapeDtypeStruct((2, PLANE, 192, 128), BF16),
            jax.ShapeDtypeStruct((6, 12, 4, WIDTH), BF16),
        ),
        in_specs=[VMEM] * len(operands),
        out_specs=(VMEM, VMEM),
        scratch_shapes=[
            pltpu.VMEM((6, 12, 4, WIDTH), BF16),
            pltpu.VMEM((6, 12, 4, WIDTH), BF16),
            pltpu.VMEM((4, 8, 128), F32),
            pltpu.VMEM((4, 8, 128), F32),
            pltpu.VMEM((128, 128), F32),
            pltpu.VMEM((2, PLANE, 160, 128), BF16),
            pltpu.VMEM((2, 2, 48, 128), BF16),
            pltpu.VMEM((6, 12, 4, WIDTH), BF16),
            pltpu.VMEM((3, 72, 8, 128), F32),
            pltpu.VMEM((288, WIDTH), F32),
            pltpu.VMEM((288, 1), F32),
            pltpu.VMEM((288, WIDTH), BF16),
            pltpu.VMEM((288, WIDTH), BF16),
            pltpu.VMEM((288, 3 * WIDTH), BF16),
            pltpu.VMEM((288, WIDTH), BF16),
            pltpu.VMEM((2, 2, WIDTH, WT), BF16),
            pltpu.VMEM((2, KEYS, 2 * WIDTH), BF16),
            pltpu.VMEM((WT, 128), BF16),
            pltpu.VMEM((KEYS, 128), BF16),
            pltpu.VMEM((768, 768), BF16),
            pltpu.VMEM((2, 16, 768), F32),
            pltpu.VMEM((2, 16, 8, 768), F32),
            pltpu.VMEM((288, WIDTH), BF16),
            pltpu.VMEM((288, WIDTH), F32),
            pltpu.VMEM((2, WT, 128), F32),
            pltpu.VMEM((2, 2, WIDTH, KEYS), F32),
            pltpu.VMEM((288, 3 * WIDTH), BF16),
            pltpu.VMEM((2, 16, 768), F32),
            pltpu.VMEM((PLANE, 160, 128), BF16),
            pltpu.VMEM((2, 48, 128), BF16),
            pltpu.VMEM((48, 128), BF16),
            pltpu.VMEM((48, 128), BF16),
            pltpu.VMEM((PLANE, 160, 128), BF16),
            pltpu.VMEM((PLANE, 160, 128), BF16),
            pltpu.VMEM((192, 128), F32),
            pltpu.VMEM((PZ, 24, 128), BF16),
            pltpu.VMEM((PZ, 24, 128), BF16),
            pltpu.VMEM((PZ, 24, 128), BF16),
            sems((2, 9)),
            sems((2, 3)),
            sems((2, PLANE)),
            sems((2, 2)),
            sems((2, PLANE)),
            sems((2, PZ)),
            sems((2, PZ)),
            sems((2, PLANE)),
            sems((2, PLANE)),
            sems((4,)),
        ],
        compiler_params=pltpu.CompilerParams(
            collective_id=0, has_side_effects=True, vmem_limit_bytes=56 * 1024 * 1024
        ),
        name="step",
    )(*operands)


def finish_kernel(grad_scale, full, gx, o_gx, o_wqkv, o_bqkv, o_wproj, o_bproj, o_gain, o_shift, o_pos, o_surf):
    o_gx[...] = gx[...]
    for j in range(4):
        for i in range(8):
            n = i * 4 + j
            for m in range(3):
                part = full[n // PLANE, n % PLANE, 48 * m : 48 * m + 48, :].astype(F32) * grad_scale
                if j < 3:
                    o_wqkv[48 * i : 48 * i + 48, WIDTH * j + 128 * m : WIDTH * j + 128 * m + 128] = part
                else:
                    o_wproj[48 * i : 48 * i + 48, 128 * m : 128 * m + 128] = part
    for core in range(2):
        for at in range(PLANE):
            x, y = at % PX, at // PX
            kind = (y * 2 + x // 2) * 2 + core
            for k in range(3):
                part = full[core, at, 144 + 16 * k : 160 + 16 * k, :].astype(F32) * grad_scale
                lo = 128 * (3 * (x % 2) + k)
                width = min(128, SLOTS - lo)
                for h in range(HEADS):
                    o_pos[16 * h + kind : 16 * h + kind + 1, lo : lo + width] = part[h : h + 1, :width]

    def extra(n):
        tile = full[n // PLANE, n % PLANE, 144:160, :].astype(F32) * grad_scale
        return tile[12:13, :]

    o_bqkv[...] = jnp.concatenate([extra(n) for n in range(9)], 1).reshape(3 * WIDTH)
    for v, out in enumerate((o_bproj, o_gain, o_shift)):
        out[...] = jnp.concatenate([extra(9 + 3 * v + m) for m in range(3)], 1).reshape(WIDTH)
    for a in range(4):
        side = extra(18 + a)
        for b in range(4):
            o_surf[a, b : b + 1, :] = side[:, 12 * b : 12 * b + 12]


def finish(full, gx, grad_scale):
    one = lambda *shape: jax.ShapeDtypeStruct(shape, F32)
    return pl.pallas_call(
        functools.partial(finish_kernel, grad_scale),
        out_shape=(
            jax.ShapeDtypeStruct((6, 12, 4, WIDTH), BF16),
            one(WIDTH, 3 * WIDTH),
            one(3 * WIDTH),
            one(WIDTH, WIDTH),
            one(WIDTH),
            one(WIDTH),
            one(WIDTH),
            one(HEADS * 16, SLOTS),
            one(4, 4, HEADS),
        ),
        in_specs=[VMEM] * 2,
        out_specs=(VMEM,) * 9,
        compiler_params=pltpu.CompilerParams(vmem_limit_bytes=32 * 1024 * 1024),
        name="finish",
    )(full, gx)


def on_device(
    inputs, cotangent, land_sea, rel_index, norm_gain, norm_shift, w_qkv, b_qkv, w_proj, pos_bias, surf_bias
):
    levels, lat_rows, lon_cols, width = inputs.shape
    count = levels * lat_rows * lon_cols * lax.axis_size("lat") * lax.axis_size("lon")
    full, gx = step(
        inputs.transpose(1, 2, 0, 3),
        cotangent.transpose(1, 2, 0, 3),
        land_sea,
        rel_index,
        norm_gain,
        norm_shift,
        w_qkv,
        b_qkv,
        w_proj,
        pos_bias.transpose(1, 0, 2).reshape(-1, SLOTS),
        surf_bias.transpose(1, 2, 0),
        *(jnp.asarray(a) for a in constants()),
    )
    outs = finish(full, gx, float(count) ** -0.5)
    g_x, g_wqkv, g_bqkv, g_wproj, g_bproj, g_gain, g_shift, g_pos, g_surf = outs
    return (
        g_x.transpose(2, 0, 1, 3),
        g_wqkv,
        g_bqkv,
        g_wproj,
        g_bproj,
        g_gain,
        g_shift,
        g_pos.reshape(HEADS, 16, SLOTS).transpose(1, 0, 2),
        g_surf.transpose(2, 0, 1),
    )


def solution(mesh):
    in_specs = (P(None, "lat", "lon", None), P(None, "lat", "lon", None), P("lat", "lon")) + (P(),) * 8
    out_specs = (P(None, "lat", "lon", None),) + (P(),) * 8
    return jax.shard_map(on_device, mesh=mesh, in_specs=in_specs, out_specs=out_specs, check_vma=False)
```

time: 107 us -> 79.8 us (0.75)
  local copies, waits for them, and re-layouts: 13.9 us -> 2.34 us
  Pallas kernels: 85 us -> 76.7 us
  other arithmetic: 6.78 us -> 0 us
    pallas_call x3 -> x1, Pallas kernels: 83.1 us -> 74.9 us  [step(): pl.pallas_call(step_kernel, out_shape=(jax.ShapeDtypeStruct((2, PLANE, 19...]
    reshape x7 -> x0, local copies, waits for them, and re-layouts: 5.23 us -> none  [the longest x1 1.29 us: on_device(): b_qkv.reshape(1, 3 * width)]
    unnamed x14 -> x4, local copies, waits for them, and re-layouts: 6.95 us -> 2.34 us
    pallas_call x4 -> x0, other arithmetic: 2.4 us -> none  [finish(): pl.pallas_call(functools.partial(finish_kernel, grad_scale), out_shape=(j...]
    concatenate x2 -> x0, other arithmetic: 2.21 us -> none  [the longest x1 1.51 us: on_device(): both = jnp.roll(both, -1, 1).reshape(2, 4, 2, 3, 2, 6, width)]
    another operation x1 -> x0, other arithmetic: 1.48 us -> none  [on_device(): both = jnp.stack([inputs, cotangent])]
where the time goes in v2:
time: 79.8 us; the launch traced here: 79.7 us
  Pallas kernels  76.7 us (96%)
  local copies, waits for them, and re-layouts  2.34 us (3%)
    pallas_call x1, Pallas kernels, step(): pl.pallas_call(step_kernel, out_shape=(jax.ShapeDtypeStruct((2, PLANE, 19...  74.9 us
    unnamed x4, local copies, waits for them, and re-layouts  2.34 us
    pallas_call x1, Pallas kernels, finish(): pl.pallas_call(functools.partial(finish_kernel, grad_scale), out_shape=(j...  1.81 us

profile of v2, /device:TPU:1, one launch (start us, length us, event | category | flops | bytes accessed | tf_op | source)
XLA Modules:
  0.0 79.7 jit_solution(13745914977804633735)
XLA Ops:
  0.6 74.9 %step.1 = (bf16[2,16,192,128]{3,2,1,0:T(8,128)(2,1)}, bf16[6,12,4,384]{3,2,1,0:T(4,128)(2,1)}) custom-call(bf16[6,12,4,384]{3,2,1,0:T(4,128)(2,1)} %bitcast.12, bf16[6,12,4,384]{3,2,1,0:T(4,128)(2,1)} %bitcast.13, s32[6,12]{1,0:T(8,128)} %land.1, s32[144,144]{1,0:T(8,128)} %rel.1, f32[384]{0:T(512)} %gain.1, f32[384]{0:T(512)} %shift.1, ...), custom_call_target="tpu_custom_call" | custom-call | tf_op jit(solution)/shard_map/step/pallas_call | solution.py:454
  75.5 0.0 copy-start
  75.5 1.4 %copy-done = bf16[2,16,192,128]{3,2,1,0:T(8,128)(2,1)S(1)} copy-done((bf16[2,16,192,128]{3,2,1,0:T(8,128)(2,1)S(1)}, bf16[2,16,192,128]{3,2,1,0:T(8,128)(2,1)}, u32[]{:S(2)}) %copy-start) | copy-done | bytes 1572888
  76.9 0.0 copy-start.1
  76.9 0.9 %copy-done.1 = bf16[6,12,4,384]{3,2,1,0:T(4,128)(2,1)S(1)} copy-done((bf16[6,12,4,384]{3,2,1,0:T(4,128)(2,1)S(1)}, bf16[6,12,4,384]{3,2,1,0:T(4,128)(2,1)}, u32[]{:S(2)}) %copy-start.1) | copy-done | bytes 221208
  77.9 1.8 %finish.1 = (bf16[6,12,4,384]{3,2,1,0:T(4,128)(2,1)}, f32[384,1152]{1,0:T(8,128)}, f32[1152]{0:T(1024)}, f32[384,384]{1,0:T(8,128)}, f32[384]{0:T(512)}, /*index...) custom-call(bf16[2,16,192,128]{3,2,1,0:T(8,128)(2,1)S(1)} %copy-done, ...), custom_call_target="tpu_custom_call" | custom-call | tf_op jit(solution)/shard_map/finish/pallas_call | solution.py:556
Async XLA Ops:
  75.5 1.4 %copy-start = (bf16[2,16,192,128]{3,2,1,0:T(8,128)(2,1)S(1)}, bf16[2,16,192,128]{3,2,1,0:T(8,128)(2,1)}, u32[]{:S(2)}) copy-start(bf16[2,16,192,128]{3,2,1,0:T(8,128)(2,1)} %get-tuple-element.20.full) | copy-start | bytes 4718596
  76.9 0.9 %copy-start.1 = (bf16[6,12,4,384]{3,2,1,0:T(4,128)(2,1)S(1)}, bf16[6,12,4,384]{3,2,1,0:T(4,128)(2,1)}, u32[]{:S(2)}) copy-start(bf16[6,12,4,384]{3,2,1,0:T(4,128)(2,1)} %get-tuple-element.21.gx) | copy-start | bytes 663556

commit v3 on v2

--- a/solution.py
+++ b/solution.py
@@ -128,16 +128,24 @@
 
 
 def step_kernel(
-    x_in, dy_in, land, rel, gain, shift, w_qkv, b_qkv, w_proj, pos, surf, c_spread, c_row, c_col,
-    full, gx_out,
-    tok_x, tok_dy, cls_out, cls_in, side_in, wp, tp, gx,
-    mixed, white, inv_std, normed, dy_low, qkv, dctx, turned, kv_pad, q_feat, k_feat,
+    x_in, dy_in, land, rel, gain, shift, w_qkv_in, b_qkv, w_proj_in, pos_in, surf, c_spread, c_row, c_col,
+    full_b, full_c, gx_out,
+    w_qkv, w_proj, pos,
+    tok_x, tok_dy, cls_out, cls_in, side_in, tp, tp_low, gx,
+    mixed, white, inv_std, normed, normed_t, dy_low, qkv, dctx, turned, kv_pad, q_feat, k_feat,
     onehot, tables, d_tables, ctx_acc, dq_acc, f_acc, dkv_t, low, table_in,
-    c_recv, tc_recv, t_send, t_recv, p_send, p_recv, z_own, z_send, z_recv, z_full,
-    f_sems, h_sems, c_sems, t_sems, p_sems, z_sems, a_sems, g_sems, k_sems, local,
+    wp, c_recv, p_send, p_recv, tc_recv, t_send, t_recv, z_own, z_send, z_recv, z_full,
+    f_sems, h_sems, c_sems, t_sems, p_sems, z_sems, a_sems, bx_sems, by_sems, cx_sems, cy_sems, k_sems, local,
 ):
     place = Place()
+    core, x, y, z, here = place.core, place.x, place.y, place.z, place.here
     place.greet()
+    fetches = [
+        pltpu.make_async_copy(a, b, local.at[4 + k])
+        for k, (a, b) in enumerate(((pos_in, pos), (w_qkv_in, w_qkv), (w_proj_in, w_proj)))
+    ]
+    for copy in fetches:
+        copy.start()
 
     cls_out[...] = jnp.zeros_like(cls_out)
     for q in range(4):
@@ -147,21 +155,20 @@
         return ref.at[pl.ds(3 * (q // 2), 3), pl.ds(6 * (q % 2), 6)]
 
     place.meet()
-    halo = []
-    for k, (q, to) in enumerate(((2, place.west), (1, place.south), (0, place.south_west))):
-        for m, (a, b) in enumerate(((x_in, tok_x), (dy_in, tok_dy))):
-            halo.append(send(quadrant(a, q), quadrant(b, 3 - q), f_sems, 3 * k + m, to))
-        halo.append(send(cls_out.at[q], cls_in.at[3 - q], f_sems, 3 * k + 2, to))
-    own = [
-        pltpu.make_async_copy(quadrant(x_in, 3), quadrant(tok_x, 0), local.at[0]),
-        pltpu.make_async_copy(quadrant(dy_in, 3), quadrant(tok_dy, 0), local.at[1]),
-        pltpu.make_async_copy(cls_out.at[3], cls_in.at[0], local.at[2]),
-    ]
-    for copy in own:
+    routes = ((0, place.south_west), (1, place.south), (2, place.west))
+    halo_x = [send(quadrant(x_in, q), quadrant(tok_x, 3 - q), f_sems, q, to) for q, to in routes]
+    halo_x += [send(cls_out.at[q], cls_in.at[3 - q], f_sems, 3 + q, to) for q, to in routes]
+    halo_dy = [send(quadrant(dy_in, q), quadrant(tok_dy, 3 - q), f_sems, 6 + q, to) for q, to in routes]
+    own_x = pltpu.make_async_copy(quadrant(x_in, 3), quadrant(tok_x, 0), local.at[0])
+    own_dy = pltpu.make_async_copy(quadrant(dy_in, 3), quadrant(tok_dy, 0), local.at[1])
+    own_cls = pltpu.make_async_copy(cls_out.at[3], cls_in.at[0], local.at[2])
+    for copy in (own_x, own_dy, own_cls):
         copy.start()
 
     lat = place.lat
     last_band = lat == place.n_lat - 1
+    for copy in fetches:
+        copy.wait()
     rel_now = rel[...]
     rel_low = jnp.bitwise_and(rel_now, 15)
     rel_wide = dot((rel_now - rel_low).astype(F32).astype(BF16), c_spread[...], NT) + dot(
@@ -184,24 +191,27 @@
             table_in[w, h : h + 1, :SLOTS] = pos[pl.ds(16 * h + 2 * lat + w, 1), :] * LOG2E
         tables[w] = functools.reduce(jnp.add, [dot(part, onehot[...]) for part in split(table_in[w], 3)])
 
-
-    for copy in halo + own:
-        copy.wait()
-    for j in range(3):
-        cols = slice(128 * j, 128 * j + 128)
-        mixed[j, :, 0:4, :] = tok_x[:, :, :, cols].reshape(72, 4, 128).astype(F32)
-        mixed[j, :, 4:8, :] = tok_dy[:, :, :, cols].reshape(72, 4, 128).astype(F32)
+    eye = (
+        lax.broadcasted_iota(jnp.int32, (WIDTH, WIDTH), 0) == lax.broadcasted_iota(jnp.int32, (WIDTH, WIDTH), 1)
+    ).astype(F32).astype(BF16)
     strided = mixed.reshape(3 * 576, 128)
-    for k in range(4):
-        level = (1, 2, 3, 0)[k]
-        rows = slice(72 * k, 72 * k + 72)
+
+    def in_order(tok, first_row, out):
         for j in range(3):
             cols = slice(128 * j, 128 * j + 128)
-            white[rows, cols] = strided[pl.ds(576 * j + level, 72, stride=8), :]
-            dq_acc[rows, cols] = strided[pl.ds(576 * j + 4 + level, 72, stride=8), :]
-    x = white[...]
-    dy_low[...] = dq_acc[...].astype(BF16)
-    centred = x - jnp.mean(x, -1, keepdims=True)
+            mixed[j, :, first_row : first_row + 4, :] = tok[:, :, :, cols].reshape(72, 4, 128).astype(F32)
+        for k in range(4):
+            level = (1, 2, 3, 0)[k]
+            for j in range(3):
+                out[72 * k : 72 * k + 72, 128 * j : 128 * j + 128] = strided[
+                    pl.ds(576 * j + first_row + level, 72, stride=8), :
+                ]
+
+    for copy in halo_x + [own_x, own_cls]:
+        copy.wait()
+    in_order(tok_x, 0, white)
+    tokens = white[...]
+    centred = tokens - jnp.mean(tokens, -1, keepdims=True)
     inv = lax.rsqrt(jnp.mean(centred * centred, -1, keepdims=True) + EPS)
     inv_std[...] = inv
     whitened = centred * inv
@@ -209,14 +219,10 @@
     gain_row = gain[...].reshape(1, WIDTH)
     normed[...] = (whitened * gain_row + shift[...].reshape(1, WIDTH)).astype(BF16)
     qkv[...] = (dot(normed[...], w_qkv[...]) + b_qkv[...].reshape(1, 3 * WIDTH)).astype(BF16)
-    dctx[...] = dot(dy_low[...], w_proj[...], NT).astype(BF16)
-    eye = (
-        lax.broadcasted_iota(jnp.int32, (WIDTH, WIDTH), 0) == lax.broadcasted_iota(jnp.int32, (WIDTH, WIDTH), 1)
-    ).astype(F32).astype(BF16)
+    normed_t[...] = dot(eye, normed[...], NT).astype(BF16)
     for w in range(2):
         rows = slice(w * WT, (w + 1) * WT)
         turned[w, 0] = dot(eye, qkv[rows, :WIDTH], NT).astype(BF16)
-        turned[w, 1] = dot(eye, dctx[rows, :], NT).astype(BF16)
         kv_pad[w] = dot(c_spread[...], qkv[rows, WIDTH:]).astype(BF16)
 
     lane = lax.broadcasted_iota(jnp.int32, (WT, 128), 1)
@@ -247,14 +253,20 @@
     hidden = jnp.logical_and(lax.rem(key_row, PITCH) >= 12, jnp.logical_and(key_lane >= 96, key_lane < 98))
     k_feat[...] = jnp.where(hidden, -BIG, dot(c_spread[...], key_side)).astype(BF16)
 
-    d_tables[...] = jnp.zeros_like(d_tables)
-    f_acc[...] = jnp.zeros_like(f_acc)
+    for copy in halo_dy + [own_dy]:
+        copy.wait()
+    in_order(tok_dy, 4, dq_acc)
+    dy_low[...] = dq_acc[...].astype(BF16)
+    dctx[...] = dot(dy_low[...], w_proj[...], NT).astype(BF16)
+    for w in range(2):
+        turned[w, 1] = dot(eye, dctx[w * WT : (w + 1) * WT, :], NT).astype(BF16)
+
     zero = jnp.zeros((72, 128), F32)
 
-    def group_step(g, carry):
+    def group_step(g):
         first, there, back = skew_parts(plain_rows())
-        lanes = pl.ds(pl.multiple_of(g * 128, 128), 128)
-        v_lanes = pl.ds(pl.multiple_of(WIDTH + g * 128, 128), 128)
+        lanes = slice(g * 128, g * 128 + 128)
+        v_lanes = slice(WIDTH + g * 128, WIDTH + g * 128 + 128)
         cat_lane = lax.broadcasted_iota(jnp.int32, (1, 256), 1)
         feat_lane = cat_lane - 128
         for w in range(2):
@@ -278,7 +290,7 @@
                 v_head = v_now * keep[:, :128]
                 raw = dot(q_cat, k_head, NT)
                 d_raw = dot(dctx_now, v_head, NT)
-                table = tables[w, pl.ds(head, 1), :]
+                table = tables[w, head : head + 1, :]
                 same = skew(table[:, :256], first, there)
                 if w == 0:
                     upper = jnp.concatenate([same, skew(table[:, 256:512], first, there)], 1)
@@ -315,163 +327,210 @@
                 both = dot(score_low, k_head)
                 dq_sum += both[:, :128]
                 feat_sum += both[:, 128:]
-                head_rows = pl.ds(pl.multiple_of(g * 128 + hh * 32, 32), 32)
+                head_rows = slice(head * 32, head * 32 + 32)
                 dkv_t[w, 0, head_rows, :] = dot(turned[w, 0, head_rows, :], score_low) * SCALE
                 dkv_t[w, 1, head_rows, :] = dot(turned[w, 1, head_rows, :], probs_low)
             ctx_acc[rows, lanes] = ctx_sum.astype(BF16)
             dq_acc[rows, lanes] = dq_sum * SCALE
             f_acc[w] += feat_sum
-        return carry
-
-    lax.fori_loop(0, 3, group_step, 0)
-
-    for w in range(2):
-        table = functools.reduce(jnp.add, [dot(part, onehot[...], NT) for part in split(jnp.sum(d_tables[w], 1), 2)])
-        for half in range(2):
-            for k in range(3):
-                at = 128 * (3 * half + k)
-                tp[w, half, 16 * k : 16 * k + 16, :] = table[:, at : at + 128].astype(BF16)
-
-    low[:, :WIDTH] = dq_acc[...].astype(BF16)
-    sums = [jnp.sum(dq_acc[...], 0, keepdims=True)]
-    for part in range(2):
-        total = jnp.zeros((1, WIDTH), F32)
-        for w in range(2):
-            token_rows = dot(c_spread[...], dkv_t[w, part].astype(BF16), (((0,), (1,)), ((), ())))
-            total += jnp.sum(token_rows, 0, keepdims=True)
-            low[w * WT : (w + 1) * WT, WIDTH * (part + 1) : WIDTH * (part + 2)] = token_rows.astype(BF16)
-        sums.append(total)
+
+    sums = {}
+
+    def weight_grads(g):
+        lanes = slice(128 * g, 128 * g + 128)
+        dq = dq_acc[:, lanes]
+        low[:, lanes] = dq.astype(BF16)
+        sums[0, g] = jnp.sum(dq, 0, keepdims=True)
+        for part in range(2):
+            total = jnp.zeros((1, 128), F32)
+            for w in range(2):
+                rows_now = dot(c_spread[...], dkv_t[w, part, lanes, :].astype(BF16), (((0,), (1,)), ((), ())))
+                total += jnp.sum(rows_now, 0, keepdims=True)
+                at = WIDTH * (part + 1) + 128 * g
+                low[w * WT : (w + 1) * WT, at : at + 128] = rows_now.astype(BF16)
+            sums[part + 1, g] = total
+        for part in range(3):
+            at = WIDTH * part + 128 * g
+            grad = dot(normed_t[...], low[:, at : at + 128])
+            for i in range(8):
+                n = 3 * i + part
+                wp[g, n // PLANE, n % PLANE] = grad[48 * i : 48 * i + 48, :].astype(BF16)
+        grad = dot(ctx_acc[:, lanes], dy_low[...], TN)
+        for u in range(8):
+            n = 24 + u
+            for m in range(3):
+                wp[g, n // PLANE, n % PLANE, 16 * m : 16 * m + 16, :] = grad[
+                    16 * u : 16 * u + 16, 128 * m : 128 * m + 128
+                ].astype(BF16)
+        return send(wp.at[g, 1 - core], c_recv.at[g], c_sems, g, place.sibling)
+
+    def plane_sends(g, core_copy):
+        core_copy.wait()
+        copies = []
+        for step in range(1, PLANE):
+            x_at, y_at, at = place.in_plane(step, 1)
+            p_send[g, step] = (wp[g, core, at].astype(F32) + c_recv[g, at].astype(F32)).astype(BF16)
+            copies.append(
+                send(
+                    p_send.at[g, step], p_recv.at[g, step], p_sems, g * PLANE + step, place.device(x_at, y_at, z, core)
+                )
+            )
+        return copies
+
+    d_tables[...] = jnp.zeros_like(d_tables)
+    f_acc[...] = jnp.zeros_like(f_acc)
+    group_step(0)
+    core_copies = [weight_grads(0)]
+    group_step(1)
+    plane_copies = [plane_sends(0, core_copies[0])]
+    core_copies.append(weight_grads(1))
+    group_step(2)
+    plane_copies.append(plane_sends(1, core_copies[1]))
+    core_copies.append(weight_grads(2))
+
     d_normed = dot(low[...], w_qkv[...], NT).astype(BF16).astype(F32)
     scaled = d_normed * gain_row
     first_mean = jnp.mean(scaled, -1, keepdims=True)
     second_mean = jnp.mean(scaled * white[...], -1, keepdims=True)
-    d_inputs = dy_low[...].astype(F32) + inv_std[...] * (scaled - first_mean - white[...] * second_mean)
-    dq_acc[...] = d_inputs
+    dq_acc[...] = dy_low[...].astype(F32) + inv_std[...] * (scaled - first_mean - white[...] * second_mean)
+    plane_copies.append(plane_sends(2, core_copies[2]))
     for j in range(3):
         cols = slice(128 * j, 128 * j + 128)
         for k in range(4):
             level = (1, 2, 3, 0)[k]
             strided[pl.ds(576 * j + level, 72, stride=8), :] = dq_acc[72 * k : 72 * k + 72, cols]
         gx[:, :, :, cols] = mixed[j, :, 0:4, :].astype(BF16).reshape(6, 12, 4, 128)
-    sums.append(jnp.sum(dy_low[...].astype(F32), 0, keepdims=True))
-    sums.append(jnp.sum(d_normed * white[...], 0, keepdims=True))
-    sums.append(jnp.sum(d_normed, 0, keepdims=True))
-    d_surf = functools.reduce(jnp.add, [dot(of_query, part, TN) for part in split(f_acc[0] + f_acc[1], 2)])
-
-    for j in range(4):
-        if j < 3:
-            grad = dot(normed[...], low[:, j * WIDTH : (j + 1) * WIDTH], TN)
-        else:
-            grad = dot(ctx_acc[...], dy_low[...], TN)
-        for i in range(8):
-            n = i * 4 + j
-            for m in range(3):
-                wp[n // PLANE, n % PLANE, 48 * m : 48 * m + 48, :] = grad[
-                    48 * i : 48 * i + 48, 128 * m : 128 * m + 128
-                ].astype(BF16)
-    extra_row = lax.broadcasted_iota(jnp.int32, (16, 128), 0) == 12
-    for n in range(2 * PLANE):
-        if n < 18:
-            row = sums[n // 3][:, 128 * (n % 3) : 128 * (n % 3) + 128]
-        elif n < 22:
-            row = d_surf[n - 18 : n - 17, :]
-        else:
-            row = jnp.zeros((1, 128), F32)
-        wp[n // PLANE, n % PLANE, 144:160, :] = jnp.where(extra_row, row, 0.0).astype(BF16)
-
-    core, x, y, z, here = place.core, place.x, place.y, place.z, place.here
-
-    order = list(range(1, PLANE)) + [0]
-    core_copies = {}
-    t_copy = send(tp.at[1 - core], tc_recv, t_sems, 0, place.sibling)
-    for step in order:
-        at = place.in_plane(step, 1)[2]
-        core_copies[step] = send(wp.at[1 - core, at], c_recv.at[step], c_sems, step, place.sibling)
-
-    halo = [
+    home = [
         send(quadrant(gx, q), quadrant(gx_out, 3 - q), h_sems, q - 1, to)
         for q, to in ((1, place.east), (2, place.north), (3, place.north_east))
     ]
-    own = pltpu.make_async_copy(quadrant(gx, 0), quadrant(gx_out, 3), local.at[3])
-    own.start()
-
+    own_gx = pltpu.make_async_copy(quadrant(gx, 0), quadrant(gx_out, 3), local.at[3])
+    own_gx.start()
+
+    for w in range(2):
+        table = functools.reduce(jnp.add, [dot(part, onehot[...], NT) for part in split(jnp.sum(d_tables[w], 1), 2)])
+        for half in range(2):
+            for k in range(3):
+                at = 128 * (3 * half + k)
+                tp[w, half, 16 * k : 16 * k + 16, :] = table[:, at : at + 128]
+    small = [sums[part, g] for part in range(3) for g in range(3)]
+    for total in (
+        jnp.sum(dy_low[...].astype(F32), 0, keepdims=True),
+        jnp.sum(d_normed * white[...], 0, keepdims=True),
+        jnp.sum(d_normed, 0, keepdims=True),
+    ):
+        small += [total[:, 128 * m : 128 * m + 128] for m in range(3)]
+    d_surf = functools.reduce(jnp.add, [dot(of_query, part, TN) for part in split(f_acc[0] + f_acc[1], 2)])
+    small += [d_surf[a : a + 1, :] for a in range(4)]
+    for e, row in enumerate(small):
+        w, half, at = small_row(e)
+        tp[w, half, at : at + 1, :] = row
+    tp_low[...] = tp[...].astype(BF16)
+    t_copy = send(tp_low.at[1 - core], tc_recv, t_sems, 0, place.sibling)
+
+    t_mine = lax.rem(x, 2)
+    total = [wp[g, core, here].astype(F32) + c_recv[g, here].astype(F32) for g in range(3)]
     t_copy.wait()
-    t_mine = lax.rem(x, 2)
-    t_send[...] = (tp[core, 1 - t_mine].astype(F32) + tc_recv[1 - t_mine].astype(F32)).astype(BF16)
+    t_send[...] = (tp[core, 1 - t_mine] + tc_recv[1 - t_mine].astype(F32)).astype(BF16)
     tx_copy = send(t_send, t_recv, t_sems, 1, place.x_pair)
-    plane_copies = []
-    for step in range(1, PLANE):
-        x_at, y_at, at = place.in_plane(step, 1)
-        core_copies[step].wait()
-        p_send[step] = (wp[core, at].astype(F32) + c_recv[step].astype(F32)).astype(BF16)
-        plane_copies.append(send(p_send.at[step], p_recv.at[step], p_sems, step, place.device(x_at, y_at, z, core)))
-    core_copies[0].wait()
-    total = wp[core, here].astype(F32) + c_recv[0].astype(F32)
+    t_total = tp[core, t_mine] + tc_recv[t_mine].astype(F32)
+    for g in range(3):
+        for step in range(1, PLANE):
+            plane_copies[g][step - 1].wait()
+            total[g] = total[g] + p_recv[g, step].astype(F32)
+        z_own[48 * g : 48 * g + 48, :] = total[g]
     tx_copy.wait()
-    t_total = tp[core, t_mine].astype(F32) + tc_recv[t_mine].astype(F32) + t_recv[...].astype(F32)
-    for step in range(1, PLANE):
-        plane_copies[step - 1].wait()
-        total = total + p_recv[step].astype(F32)
-    z_own[0:144, :] = total[:144]
-    z_own[144:160, :] = total[144:] + t_total[:16]
-    z_own[160:192, :] = t_total[16:]
+    z_own[144:192, :] = t_total + t_recv[...].astype(F32)
 
     for k in range(PZ):
         z_send[k] = z_own[24 * k : 24 * k + 24, :].astype(BF16)
     z_copies = []
-    for step in range(1, PZ):
+    for step in (4, 3, 5, 2, 6, 1, 7):
         z_at = lax.rem(z + step, PZ)
         z_copies.append(send(z_send.at[z_at], z_recv.at[step], z_sems, step, place.device(x, y, z_at, core)))
     summed = z_own[pl.ds(pl.multiple_of(24 * z, 8), 24), :]
+    for copy in z_copies:
+        copy.wait()
     for step in range(1, PZ):
-        z_copies[step - 1].wait()
         summed = summed + z_recv[step].astype(F32)
     z_full[z] = summed.astype(BF16)
     a_copies = []
-    for step in range(1, PZ):
+    for step in (4, 3, 5, 2, 6, 1, 7):
         z_at = lax.rem(z + step, PZ)
         a_copies.append(send(z_full.at[z], z_full.at[z], a_sems, step, place.device(x, y, z_at, core)))
     for copy in a_copies:
         copy.wait()
-    full[core, here] = jnp.concatenate([z_full[k].astype(F32) for k in range(PZ)], 0).astype(BF16)
-
-    g_copies = []
-    for step in range(1, PLANE):
-        x_at, y_at, _ = place.in_plane(step, 1)
-        g_copies.append(send(full.at[core, here], full.at[core, here], g_sems, step, place.device(x_at, y_at, z, core)))
-    k_copies = [send(full.at[core, here], full.at[core, here], k_sems, 0, place.sibling)]
-    for step in range(1, PLANE):
-        at = place.in_plane(step, -1)[2]
-        g_copies[step - 1].wait()
-        k_copies.append(send(full.at[core, at], full.at[core, at], k_sems, step, place.sibling))
-    for copy in k_copies + halo:
+    full_b[core, y, x] = jnp.concatenate([z_full[k].astype(F32) for k in range(4)], 0).astype(BF16)
+    full_c[core, x, y] = jnp.concatenate([z_full[k].astype(F32) for k in range(4, 8)], 0).astype(BF16)
+
+    def x_away(step):
+        return place.device(lax.rem(x + step, PX), y, z, core)
+
+    def y_away(step):
+        return place.device(x, lax.rem(y + step, PY), z, core)
+
+    b_first, c_first, b_then, c_then, last = {}, {}, {}, {}, []
+    for d in (2, 1, 3):
+        b_first[d] = send(full_b.at[core, y, x], full_b.at[core, y, x], bx_sems, d, x_away(d))
+        c_first[d] = send(full_c.at[core, x, y], full_c.at[core, x, y], cy_sems, d, y_away(d))
+    for d in (2, 1, 3):
+        b_then[0, d] = send(full_b.at[core, y, x], full_b.at[core, y, x], by_sems, d, y_away(d))
+        c_then[0, d] = send(full_c.at[core, x, y], full_c.at[core, x, y], cx_sems, d, x_away(d))
+    for e in (1, 3, 2):
+        x_from, y_from = lax.rem(x + PX - e, PX), lax.rem(y + PY - e, PY)
+        b_first[e].wait()
+        for d in (2, 1, 3):
+            b_then[e, d] = send(full_b.at[core, y, x_from], full_b.at[core, y, x_from], by_sems, 4 * e + d, y_away(d))
+        c_first[e].wait()
+        for d in (2, 1, 3):
+            c_then[e, d] = send(full_c.at[core, x, y_from], full_c.at[core, x, y_from], cx_sems, 4 * e + d, x_away(d))
+    last.append(send(full_b.at[core, y], full_b.at[core, y], k_sems, 0, place.sibling))
+    last.append(send(full_c.at[core, x], full_c.at[core, x], k_sems, 4, place.sibling))
+    for d in (1, 3, 2):
+        x_from, y_from = lax.rem(x + PX - d, PX), lax.rem(y + PY - d, PY)
+        for e in range(4):
+            b_then[e, d].wait()
+        last.append(send(full_b.at[core, y_from], full_b.at[core, y_from], k_sems, d, place.sibling))
+        for e in range(4):
+            c_then[e, d].wait()
+        last.append(send(full_c.at[core, x_from], full_c.at[core, x_from], k_sems, 4 + d, place.sibling))
+    for copy in last + home:
         copy.wait()
-    own.wait()
+    own_gx.wait()
 
 
 def step(*operands):
     sems = pltpu.SemaphoreType.DMA
+    anywhere = pl.BlockSpec(memory_space=pl.ANY)
+    in_specs = [VMEM] * len(operands)
+    for k in (0, 1, 6, 8, 9):
+        in_specs[k] = anywhere
     return pl.pallas_call(
         step_kernel,
         out_shape=(
-            jax.ShapeDtypeStruct((2, PLANE, 192, 128), BF16),
+            jax.ShapeDtypeStruct((2, PY, PX, 96, 128), BF16),
+            jax.ShapeDtypeStruct((2, PX, PY, 96, 128), BF16),
             jax.ShapeDtypeStruct((6, 12, 4, WIDTH), BF16),
         ),
-        in_specs=[VMEM] * len(operands),
-        out_specs=(VMEM, VMEM),
+        in_specs=in_specs,
+        out_specs=(VMEM, VMEM, VMEM),
         scratch_shapes=[
+            pltpu.VMEM((WIDTH, 3 * WIDTH), BF16),
+            pltpu.VMEM((WIDTH, WIDTH), BF16),
+            pltpu.VMEM((HEADS * 16, SLOTS), F32),
             pltpu.VMEM((6, 12, 4, WIDTH), BF16),
             pltpu.VMEM((6, 12, 4, WIDTH), BF16),
             pltpu.VMEM((4, 8, 128), F32),
             pltpu.VMEM((4, 8, 128), F32),
             pltpu.VMEM((128, 128), F32),
-            pltpu.VMEM((2, PLANE, 160, 128), BF16),
+            pltpu.VMEM((2, 2, 48, 128), F32),
             pltpu.VMEM((2, 2, 48, 128), BF16),
             pltpu.VMEM((6, 12, 4, WIDTH), BF16),
             pltpu.VMEM((3, 72, 8, 128), F32),
             pltpu.VMEM((288, WIDTH), F32),
             pltpu.VMEM((288, 1), F32),
             pltpu.VMEM((288, WIDTH), BF16),
+            pltpu.VMEM((WIDTH, 288), BF16),
             pltpu.VMEM((288, WIDTH), BF16),
             pltpu.VMEM((288, 3 * WIDTH), BF16),
             pltpu.VMEM((288, WIDTH), BF16),
@@ -488,70 +547,96 @@
             pltpu.VMEM((2, 2, WIDTH, KEYS), F32),
             pltpu.VMEM((288, 3 * WIDTH), BF16),
             pltpu.VMEM((2, 16, 768), F32),
-            pltpu.VMEM((PLANE, 160, 128), BF16),
+            pltpu.VMEM((3, 2, PLANE, 48, 128), BF16),
+            pltpu.VMEM((3, PLANE, 48, 128), BF16),
+            pltpu.VMEM((3, PLANE, 48, 128), BF16),
+            pltpu.VMEM((3, PLANE, 48, 128), BF16),
             pltpu.VMEM((2, 48, 128), BF16),
             pltpu.VMEM((48, 128), BF16),
             pltpu.VMEM((48, 128), BF16),
-            pltpu.VMEM((PLANE, 160, 128), BF16),
-            pltpu.VMEM((PLANE, 160, 128), BF16),
             pltpu.VMEM((192, 128), F32),
             pltpu.VMEM((PZ, 24, 128), BF16),
             pltpu.VMEM((PZ, 24, 128), BF16),
             pltpu.VMEM((PZ, 24, 128), BF16),
             sems((2, 9)),
             sems((2, 3)),
-            sems((2, PLANE)),
+            sems((2, 3)),
             sems((2, 2)),
-            sems((2, PLANE)),
+            sems((2, 3 * PLANE)),
             sems((2, PZ)),
             sems((2, PZ)),
-            sems((2, PLANE)),
-            sems((2, PLANE)),
-            sems((4,)),
+            sems((2, 4)),
+            sems((2, 16)),
+            sems((2, 16)),
+            sems((2, 4)),
+            sems((2, 8)),
+            sems((7,)),
         ],
         compiler_params=pltpu.CompilerParams(
-            collective_id=0, has_side_effects=True, vmem_limit_bytes=56 * 1024 * 1024
+            collective_id=0, has_side_effects=True, vmem_limit_bytes=60 * 1024 * 1024
         ),
         name="step",
     )(*operands)
 
 
-def finish_kernel(grad_scale, full, gx, o_gx, o_wqkv, o_bqkv, o_wproj, o_bproj, o_gain, o_shift, o_pos, o_surf):
+def small_row(e):
+    quarter, k = e // 6, e % 6
+    return quarter // 2, quarter % 2, 16 * (k // 4) + 12 + k % 4
+
+
+def finish_kernel(
+    grad_scale, full_b, full_c, gx, o_gx, o_wqkv, o_bqkv, o_wproj, o_bproj, o_gain, o_shift, o_pos, o_surf
+):
     o_gx[...] = gx[...]
-    for j in range(4):
-        for i in range(8):
-            n = i * 4 + j
-            for m in range(3):
-                part = full[n // PLANE, n % PLANE, 48 * m : 48 * m + 48, :].astype(F32) * grad_scale
-                if j < 3:
-                    o_wqkv[48 * i : 48 * i + 48, WIDTH * j + 128 * m : WIDTH * j + 128 * m + 128] = part
-                else:
-                    o_wproj[48 * i : 48 * i + 48, 128 * m : 128 * m + 128] = part
+
+    def chunk(core, at):
+        x, y = at % PX, at // PX
+        return full_b.at[core, y, x], full_c.at[core, x, y]
+
+    for n in range(2 * PLANE):
+        b, c = chunk(n // PLANE, n % PLANE)
+        for g in range(3):
+            source = (b, b, c)[g]
+            rows = (0, 48, 0)[g]
+            part = source[rows : rows + 48, :].astype(F32) * grad_scale
+            if n < 24:
+                i, at = n // 3, WIDTH * (n % 3) + 128 * g
+                o_wqkv[48 * i : 48 * i + 48, at : at + 128] = part
+            else:
+                at = 128 * g + 16 * (n - 24)
+                for m in range(3):
+                    o_wproj[at : at + 16, 128 * m : 128 * m + 128] = part[16 * m : 16 * m + 16, :]
+
+    quarters = {}
     for core in range(2):
         for at in range(PLANE):
             x, y = at % PX, at // PX
             kind = (y * 2 + x // 2) * 2 + core
+            rows = chunk(core, at)[1][48:96, :].astype(F32) * grad_scale
+            key = core, x % 2
+            quarters[key] = rows if key not in quarters else quarters[key] + rows
             for k in range(3):
-                part = full[core, at, 144 + 16 * k : 160 + 16 * k, :].astype(F32) * grad_scale
                 lo = 128 * (3 * (x % 2) + k)
                 width = min(128, SLOTS - lo)
                 for h in range(HEADS):
-                    o_pos[16 * h + kind : 16 * h + kind + 1, lo : lo + width] = part[h : h + 1, :width]
-
-    def extra(n):
-        tile = full[n // PLANE, n % PLANE, 144:160, :].astype(F32) * grad_scale
-        return tile[12:13, :]
-
-    o_bqkv[...] = jnp.concatenate([extra(n) for n in range(9)], 1).reshape(3 * WIDTH)
+                    o_pos[16 * h + kind : 16 * h + kind + 1, lo : lo + width] = rows[
+                        16 * k + h : 16 * k + h + 1, :width
+                    ]
+
+    def small(e):
+        w, half, at = small_row(e)
+        return quarters[w, half][at : at + 1, :]
+
+    o_bqkv[...] = jnp.concatenate([small(n) for n in range(9)], 1).reshape(3 * WIDTH)
     for v, out in enumerate((o_bproj, o_gain, o_shift)):
-        out[...] = jnp.concatenate([extra(9 + 3 * v + m) for m in range(3)], 1).reshape(WIDTH)
+        out[...] = jnp.concatenate([small(9 + 3 * v + m) for m in range(3)], 1).reshape(WIDTH)
     for a in range(4):
-        side = extra(18 + a)
+        side = small(18 + a)
         for b in range(4):
             o_surf[a, b : b + 1, :] = side[:, 12 * b : 12 * b + 12]
 
 
-def finish(full, gx, grad_scale):
+def finish(full_b, full_c, gx, grad_scale):
     one = lambda *shape: jax.ShapeDtypeStruct(shape, F32)
     return pl.pallas_call(
         functools.partial(finish_kernel, grad_scale),
@@ -566,11 +651,11 @@
             one(HEADS * 16, SLOTS),
             one(4, 4, HEADS),
         ),
-        in_specs=[VMEM] * 2,
+        in_specs=[VMEM] * 3,
         out_specs=(VMEM,) * 9,
-        compiler_params=pltpu.CompilerParams(vmem_limit_bytes=32 * 1024 * 1024),
+        compiler_params=pltpu.CompilerParams(vmem_limit_bytes=60 * 1024 * 1024),
         name="finish",
-    )(full, gx)
+    )(full_b, full_c, gx)
 
 
 def on_device(
@@ -578,7 +663,7 @@
 ):
     levels, lat_rows, lon_cols, width = inputs.shape
     count = levels * lat_rows * lon_cols * lax.axis_size("lat") * lax.axis_size("lon")
-    full, gx = step(
+    full_b, full_c, gx = step(
         inputs.transpose(1, 2, 0, 3),
         cotangent.transpose(1, 2, 0, 3),
         land_sea,
@@ -592,7 +677,7 @@
         surf_bias.transpose(1, 2, 0),
         *(jnp.asarray(a) for a in constants()),
     )
-    outs = finish(full, gx, float(count) ** -0.5)
+    outs = finish(full_b, full_c, gx, float(count) ** -0.5)
     g_x, g_wqkv, g_bqkv, g_wproj, g_bproj, g_gain, g_shift, g_pos, g_surf = outs
     return (
         g_x.transpose(2, 0, 1, 3),

time: 79.8 us -> 70.8 us (0.89)
  Pallas kernels: 76.7 us -> 70 us
  local copies, waits for them, and re-layouts: 2.34 us -> 0 us
    pallas_call x1, Pallas kernels: 74.9 us -> 66.8 us  [step(): pl.pallas_call(step_kernel, out_shape=(jax.ShapeDtypeStruct((2, PY, PX, 9...]
    unnamed x4 -> x0, local copies, waits for them, and re-layouts: 2.34 us -> none
    pallas_call x1, Pallas kernels: 1.81 us -> 3.22 us  [finish(): pl.pallas_call(functools.partial(finish_kernel, grad_scale), out_shape=(j...]
where the time goes in v3:
time: 70.8 us; the launch traced here: 70.7 us
  Pallas kernels  70 us (99%)
    pallas_call x1, Pallas kernels, step(): pl.pallas_call(step_kernel, out_shape=(jax.ShapeDtypeStruct((2, PY, PX, 9...  66.8 us
    pallas_call x1, Pallas kernels, finish(): pl.pallas_call(functools.partial(finish_kernel, grad_scale), out_shape=(j...  3.22 us

profile of v3, /device:TPU:1, one launch (start us, length us, event | category | flops | bytes accessed | tf_op | source)
XLA Modules:
  0.0 70.7 jit_solution(16142787083140315827)
XLA Ops:
  0.6 66.8 %step.1 = (bf16[2,4,4,96,128]{4,3,2,1,0:T(8,128)(2,1)}, bf16[2,4,4,96,128]{4,3,2,1,0:T(8,128)(2,1)}, bf16[6,12,4,384]{3,2,1,0:T(4,128)(2,1)}) custom-call(bf16[6,12,4,384]{3,2,1,0:T(4,128)(2,1)} %bitcast.12, bf16[6,12,4,384]{3,2,1,0:T(4,128)(2,1)} %bitcast.13, s32[6,12]{1,0:T(8,128)} %land.1, s32[144,144]{1,0:T(8,128)} %rel.1, f32[384]{0:T(512)} %gain.1, ...), custom_call_target="tpu_custom_call" | custom-call | tf_op jit(solution)/shard_map/step/pallas_call | solution.py:508
  67.4 3.2 %finish.1 = (bf16[6,12,4,384]{3,2,1,0:T(4,128)(2,1)}, f32[384,1152]{1,0:T(8,128)}, f32[1152]{0:T(1024)}, f32[384,384]{1,0:T(8,128)}, f32[384]{0:T(512)}, /*index...) custom-call(bf16[2,4,4,96,128]{4,3,2,1,0:T(8,128)(2,1)} %get-tuple-element.21.full_b, ...), custom_call_target="tpu_custom_call" | custom-call | tf_op jit(solution)/shard_map/finish/pallas_call | solution.py:641

commit v4 on v3

--- a/solution.py
+++ b/solution.py
@@ -43,7 +43,7 @@
         spread[li * 128 + PITCH * ri + ci, k] = 1
         of_row[k, 8 * (2 * (ri // 3) + ci // 6) + ri % 3] = 1
         of_col[k, ci % 6] = 1
-    return tuple(a.astype(ml_dtypes.bfloat16) for a in (spread, of_row, of_col))
+    return tuple(a.astype(ml_dtypes.bfloat16) for a in (spread, spread.T, of_row, of_col))
 
 
 class Place:
@@ -128,11 +128,11 @@
 
 
 def step_kernel(
-    x_in, dy_in, land, rel, gain, shift, w_qkv_in, b_qkv, w_proj_in, pos_in, surf, c_spread, c_row, c_col,
+    x_in, dy_in, land, rel, gain, shift, w_qkv_in, b_qkv, w_proj_in, pos_in, surf, c_spread, c_back, c_row, c_col,
     full_b, full_c, gx_out,
     w_qkv, w_proj, pos,
     tok_x, tok_dy, cls_out, cls_in, side_in, tp, tp_low, gx,
-    mixed, white, inv_std, normed, normed_t, dy_low, qkv, dctx, turned, kv_pad, q_feat, k_feat,
+    mixed, white, inv_std, normed, normed_t, dy_low, qkv, dctx, turned, k_cat, k_cat_t, v_cat, v_turned, q_feat,
     onehot, tables, d_tables, ctx_acc, dq_acc, f_acc, dkv_t, low, table_in,
     wp, c_recv, p_send, p_recv, tc_recv, t_send, t_recv, z_own, z_send, z_recv, z_full,
     f_sems, h_sems, c_sems, t_sems, p_sems, z_sems, a_sems, bx_sems, by_sems, cx_sems, cy_sems, k_sems, local,
@@ -223,7 +223,15 @@
     for w in range(2):
         rows = slice(w * WT, (w + 1) * WT)
         turned[w, 0] = dot(eye, qkv[rows, :WIDTH], NT).astype(BF16)
-        kv_pad[w] = dot(c_spread[...], qkv[rows, WIDTH:]).astype(BF16)
+        padded = dot(c_spread[...], qkv[rows, WIDTH:]).astype(BF16)
+        k_turned = dot(eye, padded[:, :WIDTH], NT).astype(BF16)
+        v_turned[w] = dot(eye, padded[:, WIDTH:], NT).astype(BF16)
+        for g in range(3):
+            lanes = slice(128 * g, 128 * g + 128)
+            k_cat[w, g, :, :128] = padded[:, lanes]
+            k_cat_t[w, g, :128, :] = k_turned[lanes, :]
+            v_cat[w, g, :, :128] = padded[:, WIDTH + 128 * g : WIDTH + 128 * g + 128]
+            v_cat[w, g, :, 128:] = jnp.ones((KEYS, 128), BF16)
 
     lane = lax.broadcasted_iota(jnp.int32, (WT, 128), 1)
     token = lax.broadcasted_iota(jnp.int32, (WT, 128), 0)
@@ -251,7 +259,12 @@
     key_lane = lax.broadcasted_iota(jnp.int32, (KEYS, 128), 1)
     key_row = jnp.bitwise_and(lax.broadcasted_iota(jnp.int32, (KEYS, 128), 0), 127)
     hidden = jnp.logical_and(lax.rem(key_row, PITCH) >= 12, jnp.logical_and(key_lane >= 96, key_lane < 98))
-    k_feat[...] = jnp.where(hidden, -BIG, dot(c_spread[...], key_side)).astype(BF16)
+    k_feat = jnp.where(hidden, -BIG, dot(c_spread[...], key_side)).astype(BF16)
+    k_feat_t = dot(eye[:128, :128], k_feat, NT).astype(BF16)
+    for w in range(2):
+        for g in range(3):
+            k_cat[w, g, :, 128:] = k_feat
+            k_cat_t[w, g, 128:, :] = k_feat_t
 
     for copy in halo_dy + [own_dy]:
         copy.wait()
@@ -262,34 +275,42 @@
         turned[w, 1] = dot(eye, dctx[w * WT : (w + 1) * WT, :], NT).astype(BF16)
 
     zero = jnp.zeros((72, 128), F32)
+    cat_lane = lax.broadcasted_iota(jnp.int32, (1, 256), 1)
+    half_lane = lax.broadcasted_iota(jnp.int32, (1, 128), 1)
+    block_row = jnp.bitwise_and(lax.broadcasted_iota(jnp.int32, (256, 512), 0), 127)
+    block_lane = lax.broadcasted_iota(jnp.int32, (256, 512), 1)
+    blocks_of_ones = jnp.where(block_row // 32 == block_lane // 128, 1.0, 0.0).astype(BF16)
+    first, there, back = skew_parts(plain_rows())
+
+    def own_level(a):
+        return jnp.concatenate([a[:72, :128], a[72:, 128:]], 0)
+
+    def both_levels(a):
+        top = jnp.concatenate([a[:72], zero], 1)
+        return jnp.concatenate([top, jnp.concatenate([zero, a[72:]], 1)], 0)
 
     def group_step(g):
-        first, there, back = skew_parts(plain_rows())
         lanes = slice(g * 128, g * 128 + 128)
-        v_lanes = slice(WIDTH + g * 128, WIDTH + g * 128 + 128)
-        cat_lane = lax.broadcasted_iota(jnp.int32, (1, 256), 1)
-        feat_lane = cat_lane - 128
         for w in range(2):
             rows = slice(w * WT, (w + 1) * WT)
+            part = [slice(WT * hh, WT * hh + WT) for hh in range(4)]
             q_cat = jnp.concatenate([qkv[rows, lanes], q_feat[...]], 1)
-            k_cat = jnp.concatenate([kv_pad[w, :, lanes], k_feat[...]], 1)
-            v_now = kv_pad[w, :, v_lanes]
             dctx_now = dctx[rows, lanes]
-            ctx_sum = jnp.zeros((WT, 128), F32)
-            dq_sum = jnp.zeros((WT, 128), F32)
-            feat_sum = jnp.zeros((WT, 128), F32)
+            q_all, dctx_all = [], []
+            for hh in range(4):
+                mine = cat_lane // 32 == hh
+                feat_mine = jnp.logical_and(
+                    cat_lane >= 128, jnp.logical_or(cat_lane >= 224, lax.rem(cat_lane + 4, 12) == g * 4 + hh)
+                )
+                keep = jnp.logical_or(mine, feat_mine).astype(F32).astype(BF16)
+                q_all.append(q_cat * keep)
+                dctx_all.append(dctx_now * keep[:, :128])
+            raw_all = dot(jnp.concatenate(q_all, 0), k_cat_t[w, g])
+            d_raw_all = dot(jnp.concatenate(dctx_all, 0), v_turned[w, lanes, :])
+            powers = []
             for hh in range(4):
                 head = g * 4 + hh
-                mine = cat_lane // 32 == hh
-                feat_mine = jnp.logical_and(
-                    cat_lane >= 128,
-                    jnp.logical_or(feat_lane >= 96, lax.rem(feat_lane + 132, 12) == head),
-                )
-                keep = jnp.logical_or(mine, feat_mine).astype(F32).astype(BF16)
-                k_head = k_cat * keep
-                v_head = v_now * keep[:, :128]
-                raw = dot(q_cat, k_head, NT)
-                d_raw = dot(dctx_now, v_head, NT)
+                raw = raw_all[part[hh]]
                 table = tables[w, head : head + 1, :]
                 same = skew(table[:, :256], first, there)
                 if w == 0:
@@ -297,42 +318,51 @@
                     lower = jnp.concatenate([skew(table[:, 512:], first, there), same], 1)
                     bias = jnp.concatenate([upper, lower], 0)
                 else:
-                    raw = jnp.concatenate([raw[:72, :128], raw[72:, 128:]], 0)
-                    d_raw = jnp.concatenate([d_raw[:72, :128], d_raw[72:, 128:]], 0)
+                    raw = own_level(raw)
                     bias = jnp.concatenate([same, same], 0)
                 score = raw * (SCALE * LOG2E) + bias
-                power = jnp.exp2(score - jnp.max(score, -1, keepdims=True))
-                probs = power * (1.0 / jnp.sum(power, -1, keepdims=True))
-                dot_sum = jnp.sum(d_raw * probs, -1, keepdims=True)
-                d_score = probs * (d_raw - dot_sum)
+                powers.append(jnp.exp2(score - jnp.max(score, -1, keepdims=True)))
+            wide = [a if w == 0 else both_levels(a) for a in powers]
+            mixed_all = dot(jnp.concatenate([a.astype(BF16) for a in wide], 0), v_cat[w, g])
+            inverse, context = [], jnp.zeros((WT, 128), F32)
+            for hh in range(4):
+                inverse.append(1.0 / mixed_all[part[hh], 128:])
+                context = jnp.where(half_lane // 32 == hh, mixed_all[part[hh], :128] * inverse[hh], context)
+            ctx_acc[rows, lanes] = context.astype(BF16)
+            shares = jnp.concatenate(split(dctx_now.astype(F32) * context, 2), 1)
+            deltas = dot(shares, blocks_of_ones)
+            score_lows = []
+            for hh in range(4):
+                head = g * 4 + hh
+                d_raw, delta = d_raw_all[part[hh]], deltas[:, 128 * hh : 128 * hh + 128]
                 if w == 0:
-                    probs_low = probs.astype(BF16)
-                    score_low = d_score.astype(BF16)
+                    double = lambda a: jnp.concatenate([a, a], 1)
+                    probs = powers[hh] * double(inverse[hh])
+                    d_score = probs * (d_raw - double(delta))
                     blocks = (d_score[:72, :128] + d_score[72:, 128:], d_score[:72, 128:], d_score[72:, :128])
+                    probs_low, score_low = probs.astype(BF16), d_score.astype(BF16)
                 else:
-                    def wide(a):
-                        top = jnp.concatenate([a[:72], zero], 1)
-                        return jnp.concatenate([top, jnp.concatenate([zero, a[72:]], 1)], 0).astype(BF16)
-
-                    probs_low = wide(probs)
-                    score_low = wide(d_score)
+                    probs = powers[hh] * inverse[hh]
+                    d_score = probs * (own_level(d_raw) - delta)
                     blocks = (d_score[:72] + d_score[72:],)
+                    probs_low, score_low = both_levels(probs).astype(BF16), both_levels(d_score).astype(BF16)
+                score_lows.append(score_low)
+                head_rows = slice(head * 32, head * 32 + 32)
+                dkv_t[w, 0, head_rows, :] = dot(turned[w, 0, head_rows, :], score_low) * SCALE
+                dkv_t[w, 1, head_rows, :] = dot(turned[w, 1, head_rows, :], probs_low)
                 for b, block in enumerate(blocks):
                     turned_back = jnp.take_along_axis(block, back, axis=1)
                     early = jnp.where(first, turned_back, 0.0)
                     late = turned_back - early
                     d_tables[w, head, :, b * 256 : b * 256 + 128] = jnp.sum(early.reshape(9, 8, 128), 0)
                     d_tables[w, head, :, b * 256 + 128 : b * 256 + 256] = jnp.sum(late.reshape(9, 8, 128), 0)
-                ctx_sum += dot(probs_low, v_head)
-                both = dot(score_low, k_head)
-                dq_sum += both[:, :128]
-                feat_sum += both[:, 128:]
-                head_rows = slice(head * 32, head * 32 + 32)
-                dkv_t[w, 0, head_rows, :] = dot(turned[w, 0, head_rows, :], score_low) * SCALE
-                dkv_t[w, 1, head_rows, :] = dot(turned[w, 1, head_rows, :], probs_low)
-            ctx_acc[rows, lanes] = ctx_sum.astype(BF16)
-            dq_acc[rows, lanes] = dq_sum * SCALE
-            f_acc[w] += feat_sum
+            both_all = dot(jnp.concatenate(score_lows, 0), k_cat[w, g])
+            dq, feats = jnp.zeros((WT, 128), F32), f_acc[w]
+            for hh in range(4):
+                dq = jnp.where(half_lane // 32 == hh, both_all[part[hh], :128], dq)
+                feats = jnp.where(lax.rem(half_lane, 12) == g * 4 + hh, both_all[part[hh], 128:], feats)
+            dq_acc[rows, lanes] = dq * SCALE
+            f_acc[w] = feats
 
     sums = {}
 
@@ -344,7 +374,7 @@
         for part in range(2):
             total = jnp.zeros((1, 128), F32)
             for w in range(2):
-                rows_now = dot(c_spread[...], dkv_t[w, part, lanes, :].astype(BF16), (((0,), (1,)), ((), ())))
+                rows_now = dot(c_back[...], dkv_t[w, part, lanes, :].astype(BF16), NT)
                 total += jnp.sum(rows_now, 0, keepdims=True)
                 at = WIDTH * (part + 1) + 128 * g
                 low[w * WT : (w + 1) * WT, at : at + 128] = rows_now.astype(BF16)
@@ -535,9 +565,11 @@
             pltpu.VMEM((288, 3 * WIDTH), BF16),
             pltpu.VMEM((288, WIDTH), BF16),
             pltpu.VMEM((2, 2, WIDTH, WT), BF16),
-            pltpu.VMEM((2, KEYS, 2 * WIDTH), BF16),
+            pltpu.VMEM((2, 3, KEYS, 256), BF16),
+            pltpu.VMEM((2, 3, 256, KEYS), BF16),
+            pltpu.VMEM((2, 3, KEYS, 256), BF16),
+            pltpu.VMEM((2, WIDTH, KEYS), BF16),
             pltpu.VMEM((WT, 128), BF16),
-            pltpu.VMEM((KEYS, 128), BF16),
             pltpu.VMEM((768, 768), BF16),
             pltpu.VMEM((2, 16, 768), F32),
             pltpu.VMEM((2, 16, 8, 768), F32),

time: 70.8 us -> 65.4 us (0.924)
  Pallas kernels: 70 us -> 64.7 us
    pallas_call x1, Pallas kernels: 66.8 us -> 61.4 us  [step(): pl.pallas_call(step_kernel, out_shape=(jax.ShapeDtypeStruct((2, PY, PX, 9...]
where the time goes in v4:
time: 65.4 us; the launch traced here: 65.3 us
  Pallas kernels  64.7 us (99%)
    pallas_call x1, Pallas kernels, step(): pl.pallas_call(step_kernel, out_shape=(jax.ShapeDtypeStruct((2, PY, PX, 9...  61.4 us
    pallas_call x1, Pallas kernels, finish(): pl.pallas_call(functools.partial(finish_kernel, grad_scale), out_shape=(j...  3.22 us

profile of v4, /device:TPU:1, one launch (start us, length us, event | category | flops | bytes accessed | tf_op | source)
XLA Modules:
  0.0 65.3 jit_solution(15678415334248035015)
XLA Ops:
  0.6 61.4 %step.1 = (bf16[2,4,4,96,128]{4,3,2,1,0:T(8,128)(2,1)}, bf16[2,4,4,96,128]{4,3,2,1,0:T(8,128)(2,1)}, bf16[6,12,4,384]{3,2,1,0:T(4,128)(2,1)}) custom-call(bf16[6,12,4,384]{3,2,1,0:T(4,128)(2,1)} %bitcast.12, bf16[6,12,4,384]{3,2,1,0:T(4,128)(2,1)} %bitcast.13, s32[6,12]{1,0:T(8,128)} %land.1, s32[144,144]{1,0:T(8,128)} %rel.1, f32[384]{0:T(512)} %gain.1, ...), custom_call_target="tpu_custom_call" | custom-call | tf_op jit(solution)/shard_map/step/pallas_call | solution.py:538
  62.1 3.2 %finish.1 = (bf16[6,12,4,384]{3,2,1,0:T(4,128)(2,1)}, f32[384,1152]{1,0:T(8,128)}, f32[1152]{0:T(1024)}, f32[384,384]{1,0:T(8,128)}, f32[384]{0:T(512)}, /*index...) custom-call(bf16[2,4,4,96,128]{4,3,2,1,0:T(8,128)(2,1)} %get-tuple-element.21.full_b, ...), custom_call_target="tpu_custom_call" | custom-call | tf_op jit(solution)/shard_map/finish/pallas_call | solution.py:673

commit v5 on v4

--- a/solution.py
+++ b/solution.py
@@ -2,8 +2,6 @@
 
 import jax
 import jax.numpy as jnp
-import ml_dtypes
-import numpy as np
 from jax import lax
 from jax.experimental import pallas as pl
 from jax.experimental.pallas import tpu as pltpu
@@ -34,18 +32,6 @@
     return lax.dot_general(a, b, dims, preferred_element_type=F32)
 
 
-def constants():
-    spread = np.zeros((KEYS, WT), np.float32)
-    of_row = np.zeros((WT, 32), np.float32)
-    of_col = np.zeros((WT, 128), np.float32)
-    for k in range(WT):
-        li, ri, ci = k // 72, k // 12 % 6, k % 12
-        spread[li * 128 + PITCH * ri + ci, k] = 1
-        of_row[k, 8 * (2 * (ri // 3) + ci // 6) + ri % 3] = 1
-        of_col[k, ci % 6] = 1
-    return tuple(a.astype(ml_dtypes.bfloat16) for a in (spread, spread.T, of_row, of_col))
-
-
 class Place:
     def __init__(self):
         lat, lon = lax.axis_index("lat"), lax.axis_index("lon")
@@ -100,6 +86,11 @@
     return copy
 
 
+def key_of(token):
+    level, cell = token // 72, lax.rem(token, 72)
+    return 128 * level + cell + (PITCH - 12) * (cell // 12)
+
+
 def plain_rows():
     rows = lax.broadcasted_iota(jnp.int32, (72, 128), 0)
     return rows + (PITCH - 12) * (rows // 12)
@@ -128,9 +119,9 @@
 
 
 def step_kernel(
-    x_in, dy_in, land, rel, gain, shift, w_qkv_in, b_qkv, w_proj_in, pos_in, surf, c_spread, c_back, c_row, c_col,
+    x_in, dy_in, land_in, rel_in, gain_in, shift_in, w_qkv_in, b_qkv_in, w_proj_in, pos_in, surf_in,
     full_b, full_c, gx_out,
-    w_qkv, w_proj, pos,
+    land, rel, gain, shift, w_qkv, b_qkv, w_proj, pos, surf, c_spread, c_back, w_qkv_t, w_proj_t, onehot_t,
     tok_x, tok_dy, cls_out, cls_in, side_in, tp, tp_low, gx,
     mixed, white, inv_std, normed, normed_t, dy_low, qkv, dctx, turned, k_cat, k_cat_t, v_cat, v_turned, q_feat,
     onehot, tables, d_tables, ctx_acc, dq_acc, f_acc, dkv_t, low, table_in,
@@ -142,12 +133,18 @@
     place.greet()
     fetches = [
         pltpu.make_async_copy(a, b, local.at[4 + k])
-        for k, (a, b) in enumerate(((pos_in, pos), (w_qkv_in, w_qkv), (w_proj_in, w_proj)))
+        for k, (a, b) in enumerate(
+            (
+                (land_in, land), (pos_in, pos), (rel_in, rel), (w_qkv_in, w_qkv), (w_proj_in, w_proj),
+                (gain_in, gain), (shift_in, shift), (b_qkv_in, b_qkv), (surf_in, surf),
+            )
+        )
     ]
     for copy in fetches:
         copy.start()
 
     cls_out[...] = jnp.zeros_like(cls_out)
+    fetches[0].wait()
     for q in range(4):
         cls_out[q, :3, :6] = land[3 * (q // 2) : 3 * (q // 2) + 3, 6 * (q % 2) : 6 * (q % 2) + 6].astype(F32)
 
@@ -167,8 +164,12 @@
 
     lat = place.lat
     last_band = lat == place.n_lat - 1
-    for copy in fetches:
+    for copy in fetches[1:]:
         copy.wait()
+    key_at = lax.broadcasted_iota(jnp.int32, (KEYS, WT), 0)
+    c_spread[...] = jnp.where(key_at == key_of(lax.broadcasted_iota(jnp.int32, (KEYS, WT), 1)), 1.0, 0.0).astype(BF16)
+    key_at = lax.broadcasted_iota(jnp.int32, (WT, KEYS), 1)
+    c_back[...] = jnp.where(key_at == key_of(lax.broadcasted_iota(jnp.int32, (WT, KEYS), 0)), 1.0, 0.0).astype(BF16)
     rel_now = rel[...]
     rel_low = jnp.bitwise_and(rel_now, 15)
     rel_wide = dot((rel_now - rel_low).astype(F32).astype(BF16), c_spread[...], NT) + dot(
@@ -190,6 +191,10 @@
         for h in range(HEADS):
             table_in[w, h : h + 1, :SLOTS] = pos[pl.ds(16 * h + 2 * lat + w, 1), :] * LOG2E
         tables[w] = functools.reduce(jnp.add, [dot(part, onehot[...]) for part in split(table_in[w], 3)])
+
+    onehot_t[...] = onehot[...].T
+    w_qkv_t[...] = w_qkv[...].T
+    w_proj_t[...] = w_proj[...].T
 
     eye = (
         lax.broadcasted_iota(jnp.int32, (WIDTH, WIDTH), 0) == lax.broadcasted_iota(jnp.int32, (WIDTH, WIDTH), 1)
@@ -235,7 +240,12 @@
 
     lane = lax.broadcasted_iota(jnp.int32, (WT, 128), 1)
     token = lax.broadcasted_iota(jnp.int32, (WT, 128), 0)
-    cells = dot(c_row[...], cls_in[...].reshape(32, 128).astype(BF16)) * c_col[...].astype(F32)
+    cell = lax.rem(token, 72)
+    cell_row, cell_col = cell // 12, lax.rem(cell, 12)
+    in_quad = 8 * (2 * (cell_row // 3) + cell_col // 6) + lax.rem(cell_row, 3)
+    pick_row = jnp.where(lane == in_quad, 1.0, 0.0).astype(BF16)[:, :32]
+    pick_col = jnp.where(lane == lax.rem(cell_col, 6), 1.0, 0.0)
+    cells = dot(pick_row, cls_in[...].reshape(32, 128).astype(BF16)) * pick_col
     kind = dot(cells.astype(BF16), jnp.ones((128, 128), BF16)).astype(jnp.int32)
     turned_over = jnp.logical_and(lax.rem(token, 72) >= 36, last_band).astype(F32)
     of_key = jnp.where(kind == lax.rem(lane, 48) // 12, 1.0, 0.0)
@@ -270,7 +280,7 @@
         copy.wait()
     in_order(tok_dy, 4, dq_acc)
     dy_low[...] = dq_acc[...].astype(BF16)
-    dctx[...] = dot(dy_low[...], w_proj[...], NT).astype(BF16)
+    dctx[...] = dot(dy_low[...], w_proj_t[...]).astype(BF16)
     for w in range(2):
         turned[w, 1] = dot(eye, dctx[w * WT : (w + 1) * WT, :], NT).astype(BF16)
 
@@ -418,7 +428,7 @@
     plane_copies.append(plane_sends(1, core_copies[1]))
     core_copies.append(weight_grads(2))
 
-    d_normed = dot(low[...], w_qkv[...], NT).astype(BF16).astype(F32)
+    d_normed = dot(low[...], w_qkv_t[...]).astype(BF16).astype(F32)
     scaled = d_normed * gain_row
     first_mean = jnp.mean(scaled, -1, keepdims=True)
     second_mean = jnp.mean(scaled * white[...], -1, keepdims=True)
@@ -438,7 +448,7 @@
     own_gx.start()
 
     for w in range(2):
-        table = functools.reduce(jnp.add, [dot(part, onehot[...], NT) for part in split(jnp.sum(d_tables[w], 1), 2)])
+        table = functools.reduce(jnp.add, [dot(part, onehot_t[...]) for part in split(jnp.sum(d_tables[w], 1), 2)])
         for half in range(2):
             for k in range(3):
                 at = 128 * (3 * half + k)
@@ -532,22 +542,31 @@
 def step(*operands):
     sems = pltpu.SemaphoreType.DMA
     anywhere = pl.BlockSpec(memory_space=pl.ANY)
-    in_specs = [VMEM] * len(operands)
-    for k in (0, 1, 6, 8, 9):
-        in_specs[k] = anywhere
+    in_specs = [anywhere] * len(operands)
     return pl.pallas_call(
         step_kernel,
         out_shape=(
-            jax.ShapeDtypeStruct((2, PY, PX, 96, 128), BF16),
-            jax.ShapeDtypeStruct((2, PX, PY, 96, 128), BF16),
-            jax.ShapeDtypeStruct((6, 12, 4, WIDTH), BF16),
+            pltpu.VMEM((2, PY, PX, 96, 128), BF16),
+            pltpu.VMEM((2, PX, PY, 96, 128), BF16),
+            pltpu.VMEM((6, 12, 4, WIDTH), BF16),
         ),
         in_specs=in_specs,
         out_specs=(VMEM, VMEM, VMEM),
         scratch_shapes=[
+            pltpu.VMEM((6, 12), jnp.int32),
+            pltpu.VMEM((WT, WT), jnp.int32),
+            pltpu.VMEM((WIDTH,), F32),
+            pltpu.VMEM((WIDTH,), F32),
             pltpu.VMEM((WIDTH, 3 * WIDTH), BF16),
+            pltpu.VMEM((3 * WIDTH,), F32),
             pltpu.VMEM((WIDTH, WIDTH), BF16),
             pltpu.VMEM((HEADS * 16, SLOTS), F32),
+            pltpu.VMEM((4, 4, HEADS), F32),
+            pltpu.VMEM((KEYS, WT), BF16),
+            pltpu.VMEM((WT, KEYS), BF16),
+            pltpu.VMEM((3 * WIDTH, WIDTH), BF16),
+            pltpu.VMEM((WIDTH, WIDTH), BF16),
+            pltpu.VMEM((768, 768), BF16),
             pltpu.VMEM((6, 12, 4, WIDTH), BF16),
             pltpu.VMEM((6, 12, 4, WIDTH), BF16),
             pltpu.VMEM((4, 8, 128), F32),
@@ -602,7 +621,7 @@
             sems((2, 16)),
             sems((2, 4)),
             sems((2, 8)),
-            sems((7,)),
+            sems((13,)),
         ],
         compiler_params=pltpu.CompilerParams(
             collective_id=0, has_side_effects=True, vmem_limit_bytes=60 * 1024 * 1024
@@ -685,7 +704,7 @@
         ),
         in_specs=[VMEM] * 3,
         out_specs=(VMEM,) * 9,
-        compiler_params=pltpu.CompilerParams(vmem_limit_bytes=60 * 1024 * 1024),
+        compiler_params=pltpu.CompilerParams(vmem_limit_bytes=32 * 1024 * 1024),
         name="finish",
     )(full_b, full_c, gx)
 
@@ -707,7 +726,6 @@
         w_proj,
         pos_bias.transpose(1, 0, 2).reshape(-1, SLOTS),
         surf_bias.transpose(1, 2, 0),
-        *(jnp.asarray(a) for a in constants()),
     )
     outs = finish(full_b, full_c, gx, float(count) ** -0.5)
     g_x, g_wqkv, g_bqkv, g_wproj, g_bproj, g_gain, g_shift, g_pos, g_surf = outs

time: 65.4 us -> 62.3 us (0.953)
  Pallas kernels: 64.7 us -> 61.5 us
    pallas_call x1, Pallas kernels: 61.4 us -> 59.7 us  [step(): pl.pallas_call(step_kernel, out_shape=(pltpu.VMEM((2, PY, PX, 96, 128), B...]
    pallas_call x1, Pallas kernels: 3.22 us -> 1.81 us  [finish(): pl.pallas_call(functools.partial(finish_kernel, grad_scale), out_shape=(j...]
where the time goes in v5:
time: 62.3 us; the launch traced here: 62.2 us
  Pallas kernels  61.5 us (99%)
  between operations  0.65 us (1%)
    pallas_call x1, Pallas kernels, step(): pl.pallas_call(step_kernel, out_shape=(pltpu.VMEM((2, PY, PX, 96, 128), B...  59.7 us
    pallas_call x1, Pallas kernels, finish(): pl.pallas_call(functools.partial(finish_kernel, grad_scale), out_shape=(j...  1.81 us

profile of v5, /device:TPU:1, one launch (start us, length us, event | category | flops | bytes accessed | tf_op | source)
XLA Modules:
  0.0 62.2 jit_solution(7924341178024736795)
XLA Ops:
  0.6 59.7 %step.1 = (bf16[2,4,4,96,128]{4,3,2,1,0:T(8,128)(2,1)S(1)}, bf16[2,4,4,96,128]{4,3,2,1,0:T(8,128)(2,1)S(1)}, bf16[6,12,4,384]{3,2,1,0:T(4,128)(2,1)S(1)}) custom-call(bf16[6,12,4,384]{3,2,1,0:T(4,128)(2,1)} %bitcast.12, bf16[6,12,4,384]{3,2,1,0:T(4,128)(2,1)} %bitcast.13, s32[6,12]{1,0:T(8,128)} %land_in.1, s32[144,144]{1,0:T(8,128)} %rel_in.1, f32[384]{0:T(512)} %gain_in.1, ...), custom_call_target="tpu_custom_call" | custom-call | tf_op jit(solution)/shard_map/step/pallas_call | solution.py:546
  60.3 1.8 %finish.1 = (bf16[6,12,4,384]{3,2,1,0:T(4,128)(2,1)}, f32[384,1152]{1,0:T(8,128)}, f32[1152]{0:T(1024)}, f32[384,384]{1,0:T(8,128)}, f32[384]{0:T(512)}, /*index...) custom-call(bf16[2,4,4,96,128]{4,3,2,1,0:T(8,128)(2,1)S(1)} %get-tuple-element.21.full_b, ...), custom_call_target="tpu_custom_call" | custom-call | tf_op jit(solution)/shard_map/finish/pallas_call | solution.py:692

commit v6 on v5

--- a/solution.py
+++ b/solution.py
@@ -125,7 +125,7 @@
     tok_x, tok_dy, cls_out, cls_in, side_in, tp, tp_low, gx,
     mixed, white, inv_std, normed, normed_t, dy_low, qkv, dctx, turned, k_cat, k_cat_t, v_cat, v_turned, q_feat,
     onehot, tables, d_tables, ctx_acc, dq_acc, f_acc, dkv_t, low, table_in,
-    wp, c_recv, p_send, p_recv, tc_recv, t_send, t_recv, z_own, z_send, z_recv, z_full,
+    wp, c_recv, p_send, p_recv, tc_recv, t_send, t_recv, z_own, z_send, z_recv, z_full, z_cat,
     f_sems, h_sems, c_sems, t_sems, p_sems, z_sems, a_sems, bx_sems, by_sems, cx_sems, cy_sems, k_sems, local,
 ):
     place = Place()
@@ -299,7 +299,7 @@
         top = jnp.concatenate([a[:72], zero], 1)
         return jnp.concatenate([top, jnp.concatenate([zero, a[72:]], 1)], 0)
 
-    def group_step(g):
+    def group_step(g, between=lambda: None):
         lanes = slice(g * 128, g * 128 + 128)
         for w in range(2):
             rows = slice(w * WT, (w + 1) * WT)
@@ -373,6 +373,8 @@
                 feats = jnp.where(lax.rem(half_lane, 12) == g * 4 + hh, both_all[part[hh], 128:], feats)
             dq_acc[rows, lanes] = dq * SCALE
             f_acc[w] = feats
+            if w == 0:
+                between()
 
     sums = {}
 
@@ -419,33 +421,17 @@
 
     d_tables[...] = jnp.zeros_like(d_tables)
     f_acc[...] = jnp.zeros_like(f_acc)
+    plane_copies = []
     group_step(0)
     core_copies = [weight_grads(0)]
     group_step(1)
-    plane_copies = [plane_sends(0, core_copies[0])]
+    plane_copies.append(plane_sends(0, core_copies[0]))
     core_copies.append(weight_grads(1))
     group_step(2)
     plane_copies.append(plane_sends(1, core_copies[1]))
     core_copies.append(weight_grads(2))
 
     d_normed = dot(low[...], w_qkv_t[...]).astype(BF16).astype(F32)
-    scaled = d_normed * gain_row
-    first_mean = jnp.mean(scaled, -1, keepdims=True)
-    second_mean = jnp.mean(scaled * white[...], -1, keepdims=True)
-    dq_acc[...] = dy_low[...].astype(F32) + inv_std[...] * (scaled - first_mean - white[...] * second_mean)
-    plane_copies.append(plane_sends(2, core_copies[2]))
-    for j in range(3):
-        cols = slice(128 * j, 128 * j + 128)
-        for k in range(4):
-            level = (1, 2, 3, 0)[k]
-            strided[pl.ds(576 * j + level, 72, stride=8), :] = dq_acc[72 * k : 72 * k + 72, cols]
-        gx[:, :, :, cols] = mixed[j, :, 0:4, :].astype(BF16).reshape(6, 12, 4, 128)
-    home = [
-        send(quadrant(gx, q), quadrant(gx_out, 3 - q), h_sems, q - 1, to)
-        for q, to in ((1, place.east), (2, place.north), (3, place.north_east))
-    ]
-    own_gx = pltpu.make_async_copy(quadrant(gx, 0), quadrant(gx_out, 3), local.at[3])
-    own_gx.start()
 
     for w in range(2):
         table = functools.reduce(jnp.add, [dot(part, onehot_t[...]) for part in split(jnp.sum(d_tables[w], 1), 2)])
@@ -467,41 +453,73 @@
         tp[w, half, at : at + 1, :] = row
     tp_low[...] = tp[...].astype(BF16)
     t_copy = send(tp_low.at[1 - core], tc_recv, t_sems, 0, place.sibling)
+    plane_copies.append(plane_sends(2, core_copies[2]))
+
+    scaled = d_normed * gain_row
+    first_mean = jnp.mean(scaled, -1, keepdims=True)
+    second_mean = jnp.mean(scaled * white[...], -1, keepdims=True)
+    dq_acc[...] = dy_low[...].astype(F32) + inv_std[...] * (scaled - first_mean - white[...] * second_mean)
+    for j in range(3):
+        cols = slice(128 * j, 128 * j + 128)
+        for k in range(4):
+            level = (1, 2, 3, 0)[k]
+            strided[pl.ds(576 * j + level, 72, stride=8), :] = dq_acc[72 * k : 72 * k + 72, cols]
+        gx[:, :, :, cols] = mixed[j, :, 0:4, :].astype(BF16).reshape(6, 12, 4, 128)
+
+    def plane_total(g):
+        total = wp[g, core, here].astype(F32) + c_recv[g, here].astype(F32)
+        for step in range(1, PLANE):
+            plane_copies[g][step - 1].wait()
+            total = total + p_recv[g, step].astype(F32)
+        return total
+
+    def along_z(src, dst, sems, s):
+        return [
+            send(src(step), dst(step), sems, PZ * s + step, place.device(x, y, lax.rem(z + step, PZ), core))
+            for step in (4, 3, 5, 2, 6, 1, 7)
+        ]
+
+    def z_sum(s, upper, lower):
+        for k in range(PZ):
+            piece = (upper, lower)[k // 4][12 * (k % 4) : 12 * (k % 4) + 12, :]
+            z_own[s, k] = piece
+            z_send[s, k] = piece.astype(BF16)
+        return along_z(lambda step: z_send.at[s, lax.rem(z + step, PZ)], lambda step: z_recv.at[s, step], z_sems, s)
+
+    def z_share(s, copies):
+        for copy in copies:
+            copy.wait()
+        summed = z_own[s, z]
+        for step in range(1, PZ):
+            summed = summed + z_recv[s, step].astype(F32)
+        z_full[s, z] = summed.astype(BF16)
+        return along_z(lambda step: z_full.at[s, z], lambda step: z_full.at[s, z], a_sems, s)
+
+    def z_join(s, copies):
+        for copy in copies:
+            copy.wait()
+        for k in range(PZ):
+            z_cat[12 * k : 12 * k + 12, :] = z_full[s, k].astype(F32)
+        return z_cat[...].astype(BF16)
 
     t_mine = lax.rem(x, 2)
-    total = [wp[g, core, here].astype(F32) + c_recv[g, here].astype(F32) for g in range(3)]
+    total_0 = plane_total(0)
     t_copy.wait()
     t_send[...] = (tp[core, 1 - t_mine] + tc_recv[1 - t_mine].astype(F32)).astype(BF16)
     tx_copy = send(t_send, t_recv, t_sems, 1, place.x_pair)
     t_total = tp[core, t_mine] + tc_recv[t_mine].astype(F32)
-    for g in range(3):
-        for step in range(1, PLANE):
-            plane_copies[g][step - 1].wait()
-            total[g] = total[g] + p_recv[g, step].astype(F32)
-        z_own[48 * g : 48 * g + 48, :] = total[g]
+    early = z_sum(0, total_0, plane_total(1))
+    total_2 = plane_total(2)
     tx_copy.wait()
-    z_own[144:192, :] = t_total + t_recv[...].astype(F32)
-
-    for k in range(PZ):
-        z_send[k] = z_own[24 * k : 24 * k + 24, :].astype(BF16)
-    z_copies = []
-    for step in (4, 3, 5, 2, 6, 1, 7):
-        z_at = lax.rem(z + step, PZ)
-        z_copies.append(send(z_send.at[z_at], z_recv.at[step], z_sems, step, place.device(x, y, z_at, core)))
-    summed = z_own[pl.ds(pl.multiple_of(24 * z, 8), 24), :]
-    for copy in z_copies:
-        copy.wait()
-    for step in range(1, PZ):
-        summed = summed + z_recv[step].astype(F32)
-    z_full[z] = summed.astype(BF16)
-    a_copies = []
-    for step in (4, 3, 5, 2, 6, 1, 7):
-        z_at = lax.rem(z + step, PZ)
-        a_copies.append(send(z_full.at[z], z_full.at[z], a_sems, step, place.device(x, y, z_at, core)))
-    for copy in a_copies:
-        copy.wait()
-    full_b[core, y, x] = jnp.concatenate([z_full[k].astype(F32) for k in range(4)], 0).astype(BF16)
-    full_c[core, x, y] = jnp.concatenate([z_full[k].astype(F32) for k in range(4, 8)], 0).astype(BF16)
+    late = z_sum(1, total_2, t_total + t_recv[...].astype(F32))
+    early = z_share(0, early)
+    home = [
+        send(quadrant(gx, q), quadrant(gx_out, 3 - q), h_sems, q - 1, to)
+        for q, to in ((1, place.east), (2, place.north), (3, place.north_east))
+    ]
+    own_gx = pltpu.make_async_copy(quadrant(gx, 0), quadrant(gx_out, 3), local.at[3])
+    own_gx.start()
+    late = z_share(1, late)
 
     def x_away(step):
         return place.device(lax.rem(x + step, PX), y, z, core)
@@ -510,27 +528,35 @@
         return place.device(x, lax.rem(y + step, PY), z, core)
 
     b_first, c_first, b_then, c_then, last = {}, {}, {}, {}, []
+    full_b[core, y, x] = z_join(0, early)
     for d in (2, 1, 3):
         b_first[d] = send(full_b.at[core, y, x], full_b.at[core, y, x], bx_sems, d, x_away(d))
+    for d in (2, 1, 3):
+        b_then[0, d] = send(full_b.at[core, y, x], full_b.at[core, y, x], by_sems, d, y_away(d))
+    full_c[core, x, y] = z_join(1, late)
+    for d in (2, 1, 3):
         c_first[d] = send(full_c.at[core, x, y], full_c.at[core, x, y], cy_sems, d, y_away(d))
     for d in (2, 1, 3):
-        b_then[0, d] = send(full_b.at[core, y, x], full_b.at[core, y, x], by_sems, d, y_away(d))
         c_then[0, d] = send(full_c.at[core, x, y], full_c.at[core, x, y], cx_sems, d, x_away(d))
     for e in (1, 3, 2):
-        x_from, y_from = lax.rem(x + PX - e, PX), lax.rem(y + PY - e, PY)
+        x_from = lax.rem(x + PX - e, PX)
         b_first[e].wait()
         for d in (2, 1, 3):
             b_then[e, d] = send(full_b.at[core, y, x_from], full_b.at[core, y, x_from], by_sems, 4 * e + d, y_away(d))
+    last.append(send(full_b.at[core, y], full_b.at[core, y], k_sems, 0, place.sibling))
+    for e in (1, 3, 2):
+        y_from = lax.rem(y + PY - e, PY)
         c_first[e].wait()
         for d in (2, 1, 3):
             c_then[e, d] = send(full_c.at[core, x, y_from], full_c.at[core, x, y_from], cx_sems, 4 * e + d, x_away(d))
-    last.append(send(full_b.at[core, y], full_b.at[core, y], k_sems, 0, place.sibling))
     last.append(send(full_c.at[core, x], full_c.at[core, x], k_sems, 4, place.sibling))
     for d in (1, 3, 2):
-        x_from, y_from = lax.rem(x + PX - d, PX), lax.rem(y + PY - d, PY)
+        y_from = lax.rem(y + PY - d, PY)
         for e in range(4):
             b_then[e, d].wait()
         last.append(send(full_b.at[core, y_from], full_b.at[core, y_from], k_sems, d, place.sibling))
+    for d in (1, 3, 2):
+        x_from = lax.rem(x + PX - d, PX)
         for e in range(4):
             c_then[e, d].wait()
         last.append(send(full_c.at[core, x_from], full_c.at[core, x_from], k_sems, 4 + d, place.sibling))
@@ -605,17 +631,18 @@
             pltpu.VMEM((2, 48, 128), BF16),
             pltpu.VMEM((48, 128), BF16),
             pltpu.VMEM((48, 128), BF16),
-            pltpu.VMEM((192, 128), F32),
-            pltpu.VMEM((PZ, 24, 128), BF16),
-            pltpu.VMEM((PZ, 24, 128), BF16),
-            pltpu.VMEM((PZ, 24, 128), BF16),
+            pltpu.VMEM((2, PZ, 12, 128), F32),
+            pltpu.VMEM((2, PZ, 12, 128), BF16),
+            pltpu.VMEM((2, PZ, 12, 128), BF16),
+            pltpu.VMEM((2, PZ, 12, 128), BF16),
+            pltpu.VMEM((96, 128), F32),
             sems((2, 9)),
             sems((2, 3)),
             sems((2, 3)),
             sems((2, 2)),
             sems((2, 3 * PLANE)),
-            sems((2, PZ)),
-            sems((2, PZ)),
+            sems((2, 2 * PZ)),
+            sems((2, 2 * PZ)),
             sems((2, 4)),
             sems((2, 16)),
             sems((2, 16)),

time: 62.3 us -> 59.4 us (0.953)
  Pallas kernels: 61.5 us -> 58.7 us
    pallas_call x1, Pallas kernels: 59.7 us -> 56.9 us  [step(): pl.pallas_call(step_kernel, out_shape=(pltpu.VMEM((2, PY, PX, 96, 128), B...]
where the time goes in v6:
time: 59.4 us; the launch traced here: 59.3 us
  Pallas kernels  58.7 us (99%)
  between operations  0.65 us (1%)
    pallas_call x1, Pallas kernels, step(): pl.pallas_call(step_kernel, out_shape=(pltpu.VMEM((2, PY, PX, 96, 128), B...  56.9 us
    pallas_call x1, Pallas kernels, finish(): pl.pallas_call(functools.partial(finish_kernel, grad_scale), out_shape=(j...  1.81 us

profile of v6, /device:TPU:1, one launch (start us, length us, event | category | flops | bytes accessed | tf_op | source)
XLA Modules:
  0.0 59.3 jit_solution(6024953678669789785)
XLA Ops:
  0.6 56.9 %step.1 = (bf16[2,4,4,96,128]{4,3,2,1,0:T(8,128)(2,1)S(1)}, bf16[2,4,4,96,128]{4,3,2,1,0:T(8,128)(2,1)S(1)}, bf16[6,12,4,384]{3,2,1,0:T(4,128)(2,1)S(1)}) custom-call(bf16[6,12,4,384]{3,2,1,0:T(4,128)(2,1)} %bitcast.12, bf16[6,12,4,384]{3,2,1,0:T(4,128)(2,1)} %bitcast.13, s32[6,12]{1,0:T(8,128)} %land_in.1, s32[144,144]{1,0:T(8,128)} %rel_in.1, f32[384]{0:T(512)} %gain_in.1, ...), custom_call_target="tpu_custom_call" | custom-call | tf_op jit(solution)/shard_map/step/pallas_call | solution.py:572
  57.5 1.8 %finish.1 = (bf16[6,12,4,384]{3,2,1,0:T(4,128)(2,1)}, f32[384,1152]{1,0:T(8,128)}, f32[1152]{0:T(1024)}, f32[384,384]{1,0:T(8,128)}, f32[384]{0:T(512)}, /*index...) custom-call(bf16[2,4,4,96,128]{4,3,2,1,0:T(8,128)(2,1)S(1)} %get-tuple-element.21.full_b, ...), custom_call_target="tpu_custom_call" | custom-call | tf_op jit(solution)/shard_map/finish/pallas_call | solution.py:719

commit v7 on v6

--- a/solution.py
+++ b/solution.py
@@ -121,7 +121,7 @@
 def step_kernel(
     x_in, dy_in, land_in, rel_in, gain_in, shift_in, w_qkv_in, b_qkv_in, w_proj_in, pos_in, surf_in,
     full_b, full_c, gx_out,
-    land, rel, gain, shift, w_qkv, b_qkv, w_proj, pos, surf, c_spread, c_back, w_qkv_t, w_proj_t, onehot_t,
+    land, rel, gain, shift, w_qkv, b_qkv, w_proj, pos, surf, c_spread, c_back, w_qkv_t, w_proj_t, onehot_t, bias_0, bias_1,
     tok_x, tok_dy, cls_out, cls_in, side_in, tp, tp_low, gx,
     mixed, white, inv_std, normed, normed_t, dy_low, qkv, dctx, turned, k_cat, k_cat_t, v_cat, v_turned, q_feat,
     onehot, tables, d_tables, ctx_acc, dq_acc, f_acc, dkv_t, low, table_in,
@@ -192,6 +192,32 @@
             table_in[w, h : h + 1, :SLOTS] = pos[pl.ds(16 * h + 2 * lat + w, 1), :] * LOG2E
         tables[w] = functools.reduce(jnp.add, [dot(part, onehot[...]) for part in split(table_in[w], 3)])
 
+    first, there, back = skew_parts(plain_rows())
+    for h in range(HEADS):
+        table = tables[0, h : h + 1, :]
+        for b in range(3):
+            block = skew(table[:, 256 * b : 256 * b + 256], first, there)
+            if b == 0:
+                bias_0[h, :72, :128] = block
+                bias_0[h, 72:, 128:] = block
+            elif b == 1:
+                bias_0[h, :72, 128:] = block
+            else:
+                bias_0[h, 72:, :128] = block
+        bias_1[h] = skew(tables[1, h : h + 1, :256], first, there)
+    for w in range(2):
+        for g in range(3):
+            v_cat[w, g, :, 128:] = jnp.ones((KEYS, 128), BF16)
+    d_tables[...] = jnp.zeros_like(d_tables)
+    f_acc[...] = jnp.zeros_like(f_acc)
+    side_in[...] = jnp.zeros_like(side_in)
+    for a in range(4):
+        for b in range(4):
+            side_in[a : a + 1, 12 * b : 12 * b + 12] = surf[a, b : b + 1, :]
+            side_in[a : a + 1, 48 + 12 * b : 60 + 12 * b] = surf[a, b : b + 1, :]
+    block_row = jnp.bitwise_and(lax.broadcasted_iota(jnp.int32, (256, 512), 0), 127)
+    block_lane = lax.broadcasted_iota(jnp.int32, (256, 512), 1)
+    blocks_of_ones = jnp.where(block_row // 32 == block_lane // 128, 1.0, 0.0).astype(BF16)
     onehot_t[...] = onehot[...].T
     w_qkv_t[...] = w_qkv[...].T
     w_proj_t[...] = w_proj[...].T
@@ -236,7 +262,6 @@
             k_cat[w, g, :, :128] = padded[:, lanes]
             k_cat_t[w, g, :128, :] = k_turned[lanes, :]
             v_cat[w, g, :, :128] = padded[:, WIDTH + 128 * g : WIDTH + 128 * g + 128]
-            v_cat[w, g, :, 128:] = jnp.ones((KEYS, 128), BF16)
 
     lane = lax.broadcasted_iota(jnp.int32, (WT, 128), 1)
     token = lax.broadcasted_iota(jnp.int32, (WT, 128), 0)
@@ -250,11 +275,6 @@
     turned_over = jnp.logical_and(lax.rem(token, 72) >= 36, last_band).astype(F32)
     of_key = jnp.where(kind == lax.rem(lane, 48) // 12, 1.0, 0.0)
     of_query = jnp.where(kind == lane, 1.0, 0.0).astype(BF16)
-    side_in[...] = jnp.zeros_like(side_in)
-    for a in range(4):
-        for b in range(4):
-            side_in[a : a + 1, 12 * b : 12 * b + 12] = surf[a, b : b + 1, :]
-            side_in[a : a + 1, 48 + 12 * b : 60 + 12 * b] = surf[a, b : b + 1, :]
     surf_lane = lax.broadcasted_iota(jnp.int32, (128, 128), 1)
     surf_hi, surf_lo = split(side_in[...] * (1.0 / SCALE), 2)
     side = dot(of_query, jnp.where(surf_lane < 48, surf_hi.astype(F32), surf_lo.astype(F32)).astype(BF16))
@@ -287,11 +307,6 @@
     zero = jnp.zeros((72, 128), F32)
     cat_lane = lax.broadcasted_iota(jnp.int32, (1, 256), 1)
     half_lane = lax.broadcasted_iota(jnp.int32, (1, 128), 1)
-    block_row = jnp.bitwise_and(lax.broadcasted_iota(jnp.int32, (256, 512), 0), 127)
-    block_lane = lax.broadcasted_iota(jnp.int32, (256, 512), 1)
-    blocks_of_ones = jnp.where(block_row // 32 == block_lane // 128, 1.0, 0.0).astype(BF16)
-    first, there, back = skew_parts(plain_rows())
-
     def own_level(a):
         return jnp.concatenate([a[:72, :128], a[72:, 128:]], 0)
 
@@ -321,15 +336,11 @@
             for hh in range(4):
                 head = g * 4 + hh
                 raw = raw_all[part[hh]]
-                table = tables[w, head : head + 1, :]
-                same = skew(table[:, :256], first, there)
                 if w == 0:
-                    upper = jnp.concatenate([same, skew(table[:, 256:512], first, there)], 1)
-                    lower = jnp.concatenate([skew(table[:, 512:], first, there), same], 1)
-                    bias = jnp.concatenate([upper, lower], 0)
+                    bias = bias_0[head]
                 else:
                     raw = own_level(raw)
-                    bias = jnp.concatenate([same, same], 0)
+                    bias = jnp.concatenate([bias_1[head], bias_1[head]], 0)
                 score = raw * (SCALE * LOG2E) + bias
                 powers.append(jnp.exp2(score - jnp.max(score, -1, keepdims=True)))
             wide = [a if w == 0 else both_levels(a) for a in powers]
@@ -419,8 +430,6 @@
             )
         return copies
 
-    d_tables[...] = jnp.zeros_like(d_tables)
-    f_acc[...] = jnp.zeros_like(f_acc)
     plane_copies = []
     group_step(0)
     core_copies = [weight_grads(0)]
@@ -433,8 +442,12 @@
 
     d_normed = dot(low[...], w_qkv_t[...]).astype(BF16).astype(F32)
 
+    plane_copies.append(plane_sends(2, core_copies[2]))
+
+    stacked = [part for w in range(2) for part in split(jnp.sum(d_tables[w], 1), 2)]
+    by_slot = dot(jnp.concatenate(stacked, 0), onehot_t[...])
     for w in range(2):
-        table = functools.reduce(jnp.add, [dot(part, onehot_t[...]) for part in split(jnp.sum(d_tables[w], 1), 2)])
+        table = by_slot[32 * w : 32 * w + 16] + by_slot[32 * w + 16 : 32 * w + 32]
         for half in range(2):
             for k in range(3):
                 at = 128 * (3 * half + k)
@@ -453,7 +466,6 @@
         tp[w, half, at : at + 1, :] = row
     tp_low[...] = tp[...].astype(BF16)
     t_copy = send(tp_low.at[1 - core], tc_recv, t_sems, 0, place.sibling)
-    plane_copies.append(plane_sends(2, core_copies[2]))
 
     scaled = d_normed * gain_row
     first_mean = jnp.mean(scaled, -1, keepdims=True)
@@ -593,6 +605,8 @@
             pltpu.VMEM((3 * WIDTH, WIDTH), BF16),
             pltpu.VMEM((WIDTH, WIDTH), BF16),
             pltpu.VMEM((768, 768), BF16),
+            pltpu.VMEM((HEADS, WT, KEYS), F32),
+            pltpu.VMEM((HEADS, 72, 128), F32),
             pltpu.VMEM((6, 12, 4, WIDTH), BF16),
             pltpu.VMEM((6, 12, 4, WIDTH), BF16),
             pltpu.VMEM((4, 8, 128), F32),

time: 59.4 us -> 58.6 us (0.987)
  Pallas kernels: 58.7 us -> 57.9 us
    pallas_call x1, Pallas kernels: 56.9 us -> 56.1 us  [step(): pl.pallas_call(step_kernel, out_shape=(pltpu.VMEM((2, PY, PX, 96, 128), B...]
where the time goes in v7:
time: 58.6 us; the launch traced here: 58.5 us
  Pallas kernels  57.9 us (99%)
  between operations  0.65 us (1%)
    pallas_call x1, Pallas kernels, step(): pl.pallas_call(step_kernel, out_shape=(pltpu.VMEM((2, PY, PX, 96, 128), B...  56.1 us
    pallas_call x1, Pallas kernels, finish(): pl.pallas_call(functools.partial(finish_kernel, grad_scale), out_shape=(j...  1.81 us

profile of v7, /device:TPU:1, one launch (start us, length us, event | category | flops | bytes accessed | tf_op | source)
XLA Modules:
  0.0 58.5 jit_solution(9222332039791482479)
XLA Ops:
  0.6 56.1 %step.1 = (bf16[2,4,4,96,128]{4,3,2,1,0:T(8,128)(2,1)S(1)}, bf16[2,4,4,96,128]{4,3,2,1,0:T(8,128)(2,1)S(1)}, bf16[6,12,4,384]{3,2,1,0:T(4,128)(2,1)S(1)}) custom-call(bf16[6,12,4,384]{3,2,1,0:T(4,128)(2,1)} %bitcast.12, bf16[6,12,4,384]{3,2,1,0:T(4,128)(2,1)} %bitcast.13, s32[6,12]{1,0:T(8,128)} %land_in.1, s32[144,144]{1,0:T(8,128)} %rel_in.1, f32[384]{0:T(512)} %gain_in.1, ...), custom_call_target="tpu_custom_call" | custom-call | tf_op jit(solution)/shard_map/step/pallas_call | solution.py:584
  56.7 1.8 %finish.1 = (bf16[6,12,4,384]{3,2,1,0:T(4,128)(2,1)}, f32[384,1152]{1,0:T(8,128)}, f32[1152]{0:T(1024)}, f32[384,384]{1,0:T(8,128)}, f32[384]{0:T(512)}, /*index...) custom-call(bf16[2,4,4,96,128]{4,3,2,1,0:T(8,128)(2,1)S(1)} %get-tuple-element.21.full_b, ...), custom_call_target="tpu_custom_call" | custom-call | tf_op jit(solution)/shard_map/finish/pallas_call | solution.py:733
